TPU v7x, 32 devices: a whole 2x2x4 slice. The times are simulated.
32 devices in a mesh: doc: 4 (over y, x), ctx: 8 (over z, core).
Axes of the slice: x: 2, y: 2, z: 4, core: 2. Of those that a mesh axis runs over, the one named last changes fastest.
Arguments:
- queries: bfloat16 [4, 1024, 4096], P('doc', 'ctx'), may hold values from -6 to 6, as said below
- key_heads: bfloat16 [4, 1024, 512], P('doc', 'ctx'), may hold values from -6 to 6, as said below
- value_heads: bfloat16 [4, 1024, 512], P('doc', 'ctx'), may hold values from -6 to 6
- out_grad: bfloat16 [4, 1024, 4096], P('doc', 'ctx'), may hold values from -6 to 6
- log_sums: float32 [4, 32, 1024], P('doc', 'ctx'), as said below
- row_delta: float32 [4, 32, 1024], P('doc', 'ctx'), may hold values from -6 to 6
- doc_start: int32 [4], P('doc'), may hold values from 0 to 512, as said below
- layer_input: bfloat16 [4, 1024, 8192], P('doc', 'ctx'), may hold values from -6 to 6
- hash_in: int32 [8192], replicated, may hold values from 0 to 255
- hash_out: int32 [4096], P('ctx'), may hold values from 0 to 127
- query_sketch: bfloat16 [4096, 8192], P('doc', 'ctx'), may hold values from -6 to 6
Outputs:
- doc_sketch: float32 [4, 8192], P('doc', 'ctx')
- scores: float32 [4, 4096], P(None, ('doc', 'ctx'))
Inputs may be any that keep to these rules, and one draw needn't show every extreme that they name: `queries`: drawn together with key_heads; float values. `key_heads`: drawn together with queries; float values. log_sums[e, h, i] is the log of the sum of exp(logits[i, j]) over the positions j visible to i, for the given queries and key_heads; 0 for rows before doc_start[e]. `doc_start`: some document starts at 0 and some at 512.
All inputs are finite; a program needn't handle non-finite values.
Results may differ from a plain program's by a relative error of at most 0.024.
Values may be sent and summed in bfloat16 or wider, within the bound.
No kernel may reach another device: no remote copies, remote signals or barrier semaphores. Data moves between devices by JAX's collectives and lax.ppermute only.
A program may use at most 128 MiB of HBM per device.

v0:
```python
import jax
import jax.numpy as jnp
from jax import lax
from jax.sharding import PartitionSpec as P

HD = 128
K1 = 128
K2 = 64


def sign_table(codes, buckets):
    levels = jnp.arange(buckets, dtype=jnp.int32)
    plus_part = (codes[..., None] == levels).astype(jnp.float32)
    minus_part = (codes[..., None] == levels + buckets).astype(jnp.float32)
    return (plus_part - minus_part).astype(jnp.bfloat16)


def local(
    queries,
    key_heads,
    value_heads,
    out_grad,
    log_sums,
    row_delta,
    doc_start,
    layer_input,
    hash_in,
    hash_out,
    query_sketch,
):
    ctx_count = lax.axis_size("ctx")
    tok_rows = queries.shape[1]
    seq_len = tok_rows * ctx_count
    local_heads = log_sums.shape[1]
    all_heads = local_heads * ctx_count
    kv_count = key_heads.shape[2] // HD
    group_size = all_heads // kv_count
    query_local = queries[0].reshape(tok_rows, all_heads, HD)
    grad_local = out_grad[0].reshape(tok_rows, all_heads, HD)
    key_local = key_heads[0].reshape(tok_rows, kv_count, HD)
    value_local = value_heads[0].reshape(tok_rows, kv_count, HD)
    query_part, grad_part = (
        lax.all_to_all(query_local, "ctx", split_axis=1, concat_axis=0, tiled=True),
        lax.all_to_all(grad_local, "ctx", split_axis=1, concat_axis=0, tiled=True),
    )
    key_all, value_all = (
        lax.all_gather(key_local, "ctx", axis=0, tiled=True),
        lax.all_gather(value_local, "ctx", axis=0, tiled=True),
    )
    first_head = lax.axis_index("ctx") * local_heads
    kv_index = (first_head + jnp.arange(local_heads, dtype=jnp.int32)) // group_size
    key_part = jnp.take(key_all, kv_index, axis=1)
    value_part = jnp.take(value_all, kv_index, axis=1)
    factor = HD ** (-0.5)
    first_pos = doc_start[0]
    log_part = log_sums[0]
    delta_part = row_delta[0]
    block_rows = min(256, seq_len)
    pieces = []
    for block_index in range(seq_len // block_rows):
        low_row = block_index * block_rows
        high_row = low_row + block_rows
        query_rows = query_part[low_row:high_row]
        grad_rows = grad_part[low_row:high_row]
        key_rows = key_part[:high_row]
        value_rows = value_part[:high_row]
        logits = (
            jnp.einsum("qhd,khd->hqk", query_rows, key_rows, preferred_element_type=jnp.float32)
            * factor
        )
        row_pos = low_row + jnp.arange(block_rows, dtype=jnp.int32)
        col_pos = jnp.arange(high_row, dtype=jnp.int32)
        visible = (col_pos[None, :] <= row_pos[:, None]) & (col_pos[None, :] >= first_pos)
        weights = jnp.where(
            visible[None], jnp.exp(logits - log_part[:, low_row:high_row, None]), 0.0
        )
        grad_weights = jnp.einsum(
            "qhd,khd->hqk", grad_rows, value_rows, preferred_element_type=jnp.float32
        )
        grad_scores = (weights * (grad_weights - delta_part[:, low_row:high_row, None])).astype(
            jnp.bfloat16
        )
        grad_query = (
            jnp.einsum("hqk,khd->qhd", grad_scores, key_rows, preferred_element_type=jnp.float32)
            * factor
        )
        pieces.append(grad_query.astype(jnp.bfloat16))
    grad_full = jnp.concatenate(pieces, axis=0)
    table_out = sign_table(hash_out.reshape(local_heads, HD), K2)
    hashed_grads = jnp.einsum(
        "shd,hdb->shb", grad_full, table_out, preferred_element_type=jnp.float32
    ).astype(jnp.bfloat16)
    table_in = sign_table(hash_in, K1)
    hashed_local = jnp.dot(layer_input[0], table_in, preferred_element_type=jnp.float32).astype(
        jnp.bfloat16
    )
    hashed_all = lax.all_gather(hashed_local, "ctx", axis=0, tiled=True)
    partial_sketch = jnp.einsum(
        "sa,shb->ab", hashed_all, hashed_grads, preferred_element_type=jnp.float32
    )
    summed = lax.psum_scatter(
        partial_sketch.astype(jnp.bfloat16), "ctx", scatter_dimension=0, tiled=True
    ).astype(jnp.float32)
    local_sketch = (summed * (seq_len * layer_input.shape[2] // K1) ** (-0.5)).reshape(1, -1)
    every_sketch = lax.all_gather(local_sketch, "doc", axis=0, tiled=True)
    partial_scores = jnp.dot(
        every_sketch, query_sketch.astype(jnp.float32).T, precision=lax.Precision.HIGHEST
    )
    scores_part = lax.psum_scatter(partial_scores, "ctx", scatter_dimension=1, tiled=True) * (
        K1 * K2
    ) ** (-0.5)
    return (local_sketch, scores_part)


def solution(mesh):
    return jax.shard_map(
        local,
        mesh=mesh,
        in_specs=(
            P("doc", "ctx", None),
            P("doc", "ctx", None),
            P("doc", "ctx", None),
            P("doc", "ctx", None),
            P("doc", "ctx", None),
            P("doc", "ctx", None),
            P("doc"),
            P("doc", "ctx", None),
            P(),
            P("ctx"),
            P("doc", "ctx"),
        ),
        out_specs=(P("doc", "ctx"), P(None, ("doc", "ctx"))),
        check_vma=False,
    )
```

profile of v0, /device:TPU:0, one launch (start us, length us, event | category | flops | bytes accessed | tf_op | source)
XLA Modules:
  0.0 223.6 jit_solution(5490642674166983815)
XLA Ops:
  7.2 0.0 copy-start
  7.2 0.0 all-gather.4.cloned.1.call-start
  7.2 1.2 copy.59
  8.4 0.8 copy.60
  9.2 0.0 all-gather.4.cloned.1.call-update
  9.2 2.3 %copy.61 = bf16[1,128,4096]{1,2,0:T(8,128)(2,1)} copy(bf16[1,128,4096]{2,1,0:T(8,128)(2,1)} %param.13) | data formatting | bytes 2097152 | tf_op args[0]
  11.5 6.5 %all-to-all-start = ((bf16[128,32,128]{0,2,1:T(8,128)(2,1)}), bf16[128,32,128]{0,2,1:T(8,128)(2,1)S(1)}, u32[]{:S(2)}, u32[]{:S(2)}) async-start(bf16[128,32,128]{0,2,1:T(8,128)(2,1)} %bitcast.158), calls=%async_computation | async-start | bytes 2097152 | tf_op jit(solution)/shard_map/all_to_all | solution.py:43
  17.9 0.0 all-gather.6.cloned.1.call-start
  18.0 0.1 copy.64
  18.1 0.8 copy.65
  18.9 0.0 all-gather.6.cloned.1.call-update
  18.9 2.3 %copy.66 = bf16[1,128,4096]{1,2,0:T(8,128)(2,1)} copy(bf16[1,128,4096]{2,1,0:T(8,128)(2,1)} %param.16) | data formatting | bytes 2097152 | tf_op args[3]
  21.9 0.5 compare_and_fusion
  22.4 0.6 iota_add_fusion.3
  23.0 29.9 %all-to-all-done = bf16[128,32,128]{0,2,1:T(8,128)(2,1)S(1)} async-done(((bf16[128,32,128]{0,2,1:T(8,128)(2,1)}), bf16[128,32,128]{0,2,1:T(8,128)(2,1)S(1)}, u32[]{:S(2)}, u32[]{:S(2)}) %all-to-all-start) | async-done | bytes 1048608 | tf_op jit(solution)/shard_map/all_to_all | solution.py:43
  53.0 4.2 %all-to-all-start.1 = ((bf16[128,32,128]{0,2,1:T(8,128)(2,1)}), bf16[128,32,128]{0,2,1:T(8,128)(2,1)}, u32[]{:S(2)}, u32[]{:S(2)}) async-start(bf16[128,32,128]{0,2,1:T(8,128)(2,1)} %bitcast.157), calls=%async_computation.1 | async-start | bytes 2097152 | tf_op jit(solution)/shard_map/all_to_all | solution.py:44
  57.2 0.0 copy-start.10
  57.2 0.0 copy-start.11
  57.2 0.0 reduce-scatter.5.cloned.1.call-start
  57.3 1.9 fusion.35
  59.2 36.2 %all_gather.12 = bf16[1024,128]{0,1:T(8,128)(2,1)} all-gather(bf16[128,128]{0,1:T(8,128)(2,1)S(1)} %fusion.35), channel_id=1, replica_groups=mesh['doc'=4,'ctx'=8] {'ctx'}, dimensions={0}, use_global_device_ids=true | all-gather | bytes 294912 | tf_op jit(solution)/shard_map/all_gather | solution.py:97
  95.4 0.6 fusion.82
  96.0 0.7 fusion.66
  96.7 0.1 fusion.60
  96.9 0.8 fusion.53
  97.7 0.9 fusion.49
  98.6 1.3 copy.62
  100.0 2.1 fusion.81
  102.0 0.7 copy.71
  102.8 0.0 all-to-all-done.1
  102.8 1.6 copy.67
  104.4 0.9 fusion.80
  105.3 0.7 copy.72
  106.0 0.7 copy.63
  106.7 0.7 copy.68
  107.5 1.0 copy.75
  108.4 0.0 all-gather.4.cloned.1.call-done
  108.5 2.9 %gather_fusion = bf16[4,1024,128]{2,1,0:T(8,128)(2,1)} fusion(bf16[1024,4,128]{2,0,1:T(8,128)(2,1)} %all-gather.4.cloned.1.call-done, s32[1024]{0:T(1024)S(1)} %pad_clamp_fusion), kind=kCustom, calls=%fused_computation.clone | custom fusion | bytes 2097168 | tf_op jit(solution)/shard_map/jit(_take)/gather | solution.py:52
  111.4 2.9 %gather_fusion.1 = bf16[4,1024,128]{2,1,0:T(8,128)(2,1)} fusion(bf16[1024,4,128]{2,0,1:T(8,128)(2,1)} %all-gather.6.cloned.1.call-done, s32[1024]{0:T(1024)S(1)} %pad_clamp_fusion), kind=kCustom, calls=%fused_computation.1.clone | custom fusion | bytes 2097168 | tf_op jit(solution)/shard_map/jit(_take)/gather | solution.py:53
  114.2 2.8 %select_bitcast_fusion = (bf16[1024,4,128]{2,0,1:T(8,128)(2,1)}, bf16[1024,4,128]{2,0,1:T(8,128)(2,1)S(1)}) fusion(bf16[4,1024,128]{2,1,0:T(8,128)(2,1)} %gather_fusion.1, pred[4]{0:T(512)(128)(4,1)} %compare_and_fusion, bf16[4,1024,128]{2,1,0:T(8,128)(2,1)} %gather_fusion), kind=kLoop, calls=%fused_computation.56 | loop fusion | flops 1048576 | bytes 4194308 | tf_op jit(solution)/shard_map/jit(_take)/select_n | solution.py:53
  117.0 2.8 %fusion.62 = f32[4,512,256]{2,1,0:T(8,128)} fusion(bf16[256,4,128]{2,0,1:T(8,128)(2,1)} %bitcast.163, bf16[1024,4,128]{2,0,1:T(8,128)(2,1)S(1)} %get-tuple-element.20), kind=kOutput, calls=%fused_computation.76 | convolution fusion | flops 134217728 | bytes 2883584 | tf_op jit(solution)/shard_map/qhd,khd->hqk/dot_general | solution.py:68
  119.9 2.2 %fusion.55 = f32[4,768,256]{2,1,0:T(8,128)} fusion(bf16[256,4,128]{2,0,1:T(8,128)(2,1)S(1)} %bitcast.161, bf16[1024,4,128]{2,0,1:T(8,128)(2,1)S(1)} %get-tuple-element.20), kind=kOutput, calls=%fused_computation.69 | convolution fusion | flops 201326592 | bytes 4194304 | tf_op jit(solution)/shard_map/qhd,khd->hqk/dot_general | solution.py:68
  122.1 0.7 copy.76
  122.9 2.7 %fusion.84 = f32[4,1024,256]{2,1,0:T(8,128)} fusion(bf16[1024,4,128]{2,0,1:T(8,128)(2,1)S(1)} %get-tuple-element.20, bf16[256,4,128]{2,0,1:T(8,128)(2,1)S(1)} %bitcast.164), kind=kOutput, calls=%fused_computation.118 | convolution fusion | flops 268435456 | bytes 5505024 | tf_op jit(solution)/shard_map/qhd,khd->hqk/dot_general | solution.py:68
  125.6 0.7 copy.80
  126.3 1.4 fusion.12
  127.7 2.5 %fusion.30 = bf16[256,4,128]{0,2,1:T(8,128)(2,1)} fusion(f32[4,256,256]{1,2,0:T(8,128)} %fusion.12, bf16[256,4,128]{2,0,1:T(8,128)(2,1)S(1)} %bitcast.162, f32[4,256]{1,0:T(4,128)S(1)} %get-tuple-element.11, bf16[1024,4,128]{2,0,1:T(8,128)(2,1)} %get-tuple-element.19, bf16[1024,4,128]{2,0,1:T(8,128)(2,1)S(1)} %get-tuple-element.20), kind=kOutput, calls=%fused_computation.44 | convolution fusion | flops 135266304 | bytes 2101248 | tf_op jit(solution)/shard_map/hqk,khd->qhd/dot_general | solution.py:84
  130.2 3.5 %fusion.29 = bf16[256,4,128]{0,2,1:T(8,128)(2,1)} fusion(f32[4,512,256]{2,1,0:T(8,128)} %fusion.62, bf16[256,4,128]{2,0,1:T(8,128)(2,1)} %bitcast.167, f32[4,256]{1,0:T(4,128)} %get-tuple-element.14, f32[4,256]{1,0:T(4,128)} %get-tuple-element.21, pred[256,512]{0,1:T(8,128)(4,1)S(1)} %fusion.60, bf16[1024,4,128]{2,0,1:T(8,128)(2,1)} %get-tuple-element.19, ...), kind=kOutput, calls=%fused_computation.43 | convolution fusion | flops 271843328 | bytes 3809280 | tf_op jit(solution)/shard_map/hqk,khd->qhd/dot_general | solution.py:84
  133.7 4.3 %fusion.31 = bf16[256,4,128]{0,2,1:T(8,128)(2,1)} fusion(f32[4,768,256]{2,1,0:T(8,128)} %fusion.55, bf16[256,4,128]{2,0,1:T(8,128)(2,1)} %bitcast.170, f32[4,256]{1,0:T(4,128)S(1)} %copy-done.12, f32[4,256]{1,0:T(4,128)S(1)} %copy-done.13, pred[256,768]{0,1:T(8,128)(4,1)} %fusion.53, bf16[1024,4,128]{2,0,1:T(8,128)(2,1)} %get-tuple-element.19, ...), kind=kOutput, calls=%fused_computation.45 | convolution fusion | flops 407633920 | bytes 5447680 | tf_op jit(solution)/shard_map/hqk,khd->qhd/dot_general | solution.py:84
  138.0 5.1 %fusion.28 = bf16[256,4,128]{0,2,1:T(8,128)(2,1)} fusion(bf16[1024,4,128]{2,0,1:T(8,128)(2,1)S(1)} %get-tuple-element.20, f32[4,1024,256]{2,1,0:T(8,128)} %fusion.84, bf16[1024,4,128]{2,0,1:T(8,128)(2,1)} %get-tuple-element.19, bf16[256,4,128]{2,0,1:T(8,128)(2,1)} %bitcast.169, f32[4,256]{1,0:T(4,128)S(1)} %get-tuple-element.12, ...), kind=kOutput, calls=%fused_computation.42 | convolution fusion | flops 543424512 | bytes 7086080 | tf_op jit(solution)/shard_map/hqk,khd->qhd/dot_general | solution.py:84
  143.1 1.6 fusion.18
  144.7 0.8 fusion.85
  145.5 0.0 reduce-scatter.5.cloned.1.call-update
  145.5 0.0 reduce-scatter.7.cloned.1.call-start
  145.6 28.6 %reduce-scatter.5.cloned.1.call-done = bf16[16,64]{1,0:T(8,128)(2,1)} async-done(((bf16[128,64]{1,0:T(8,128)(2,1)}), bf16[16,64]{1,0:T(8,128)(2,1)}) %reduce-scatter.5.cloned.1.call-update) | async-done | bytes 2064 | tf_op jit(solution)/shard_map/reduce_scatter | solution.py:101
  174.2 0.7 convert_multiply_fusion
  174.8 0.1 reshape.218
  174.9 8.1 %all-gather = f32[4,1,1024]{2,1,0:T(1,128)S(1)} all-gather(f32[1,1,1024]{2,1,0:T(1,128)S(1)} %reshape.218), channel_id=1, replica_groups=mesh['doc'=4,'ctx'=8] {'doc'}, dimensions={0}, use_global_device_ids=true | all-gather | bytes 20480 | tf_op jit(solution)/shard_map/all_gather | solution.py:105
  183.0 4.2 %convolution_bitcast_fusion = f32[1024,4]{1,0:T(8,128)} fusion(bf16[1024,1024]{1,0:T(8,128)(2,1)} %param.23, f32[4,1,1024]{2,1,0:T(1,128)S(1)} %all-gather), kind=kOutput, calls=%fused_computation.32 | convolution fusion | flops 50331648 | bytes 2129920
  187.2 0.0 reduce-scatter.7.cloned.1.call-update
  187.2 0.7 reshape.199
  187.9 27.6 %reduce-scatter.7.cloned.1.call-done = f32[128,4]{1,0:T(8,128)} async-done(((f32[1024,4]{1,0:T(8,128)}), f32[128,4]{1,0:T(8,128)}) %reduce-scatter.7.cloned.1.call-update) | async-done | bytes 2064
  215.5 0.9 copy.94
  216.4 0.6 broadcast_multiply_fusion
  (45 shorter events, 0.1 us)
Async XLA Ops:
  7.2 50.1 %copy-start = (bf16[1,128,8192]{2,1,0:T(8,128)(2,1)S(1)}, bf16[1,128,8192]{2,1,0:T(8,128)(2,1)}, u32[]{:S(2)}) copy-start(bf16[1,128,8192]{2,1,0:T(8,128)(2,1)} %param.20) | copy-start | bytes 6291460
  7.2 10.8 %copy-start.8 = (bf16[1,128,512]{2,1,0:T(8,128)(2,1)S(1)}, bf16[1,128,512]{2,1,0:T(8,128)(2,1)}, u32[]{:S(2)}) copy-start(bf16[1,128,512]{2,1,0:T(8,128)(2,1)} %param.15) | copy-start | bytes 393220
  7.2 101.3 %all-gather.4.cloned.1.call-start = ((), (), s32[]{:S(2)}) async-start(), calls=%async_computation.4 | async-start | bytes 1179648 | tf_op jit(solution)/shard_map/all_gather | solution.py:47
  11.5 45.8 %copy-start.15 = (s32[8192]{0:T(1024)S(1)}, s32[8192]{0:T(1024)}, u32[]{:S(2)}) copy-start(s32[8192]{0:T(1024)} %param.21) | copy-start | bytes 98308
  11.5 41.5 %all-to-all-start = ((bf16[128,32,128]{0,2,1:T(8,128)(2,1)}), bf16[128,32,128]{0,2,1:T(8,128)(2,1)S(1)}, u32[]{:S(2)}, u32[]{:S(2)}) async-start(bf16[128,32,128]{0,2,1:T(8,128)(2,1)} %bitcast.158), calls=%async_computation | async-start | bytes 2097152 | tf_op jit(solution)/shard_map/all_to_all | solution.py:43
  17.9 93.4 %all-gather.6.cloned.1.call-start = ((), (), s32[]{:S(2)}) async-start(), calls=%async_computation.5 | async-start | bytes 1179648 | tf_op jit(solution)/shard_map/all_gather | solution.py:48
  53.0 49.8 %all-to-all-start.1 = ((bf16[128,32,128]{0,2,1:T(8,128)(2,1)}), bf16[128,32,128]{0,2,1:T(8,128)(2,1)}, u32[]{:S(2)}, u32[]{:S(2)}) async-start(bf16[128,32,128]{0,2,1:T(8,128)(2,1)} %bitcast.157), calls=%async_computation.1 | async-start | bytes 2097152 | tf_op jit(solution)/shard_map/all_to_all | solution.py:44
  57.2 38.2 %copy-start.10 = (f32[1,4,1024]{2,1,0:T(4,128)S(1)}, f32[1,4,1024]{2,1,0:T(4,128)}, u32[]{:S(2)}) copy-start(f32[1,4,1024]{2,1,0:T(4,128)} %param.18) | copy-start | bytes 49156
  57.2 38.2 %copy-start.11 = (f32[1,4,1024]{2,1,0:T(4,128)S(1)}, f32[1,4,1024]{2,1,0:T(4,128)}, u32[]{:S(2)}) copy-start(f32[1,4,1024]{2,1,0:T(4,128)} %param.17) | copy-start | bytes 49156
  57.2 116.9 %reduce-scatter.5.cloned.1.call-start = ((), (), s32[]{:S(2)}) async-start(), calls=%async_computation.6 | async-start | bytes 36864 | tf_op jit(solution)/shard_map/reduce_scatter | solution.py:101
  117.0 5.1 %copy-start.5 = (bf16[2,128,4,128]{3,1,2,0:T(8,128)(2,1)S(1)}, bf16[2,128,4,128]{3,1,2,0:T(8,128)(2,1)}, u32[]{:S(2)}) copy-start(bf16[2,128,4,128]{3,1,2,0:T(8,128)(2,1)} %get-tuple-element.5) | copy-start | bytes 786436
  117.0 5.8 %copy-start.2 = (bf16[2,128,4,128]{3,1,2,0:T(8,128)(2,1)S(1)}, bf16[2,128,4,128]{3,1,2,0:T(8,128)(2,1)}, u32[]{:S(2)}) copy-start(bf16[2,128,4,128]{3,1,2,0:T(8,128)(2,1)} %get-tuple-element.8) | copy-start | bytes 786436
  122.8 2.7 %copy-start.4 = (bf16[2,128,4,128]{3,1,2,0:T(8,128)(2,1)S(1)}, bf16[2,128,4,128]{3,1,2,0:T(8,128)(2,1)}, u32[]{:S(2)}) copy-start(bf16[2,128,4,128]{3,1,2,0:T(8,128)(2,1)} %get-tuple-element.4) | copy-start | bytes 786436
  122.9 3.5 %copy-start.7 = (bf16[2,128,4,128]{3,1,0,2:T(8,128)(2,1)S(1)}, bf16[2,128,4,128]{3,1,0,2:T(8,128)(2,1)}, u32[]{:S(2)}) copy-start(bf16[2,128,4,128]{3,1,0,2:T(8,128)(2,1)} %copy.63) | copy-start | bytes 786436
  122.9 3.4 %copy-start.9 = (pred[256,256]{0,1:T(8,128)(4,1)S(1)}, pred[256,256]{0,1:T(8,128)(4,1)}, u32[]{:S(2)}) copy-start(pred[256,256]{0,1:T(8,128)(4,1)} %fusion.66) | copy-start | bytes 196612
  122.9 3.4 %copy-start.14 = (f32[4,256]{1,0:T(4,128)S(1)}, f32[4,256]{1,0:T(4,128)}, u32[]{:S(2)}) copy-start(f32[4,256]{1,0:T(4,128)} %get-tuple-element.24) | copy-start | bytes 12292
  122.9 4.8 %copy-start.3 = (bf16[2,128,4,128]{3,1,0,2:T(8,128)(2,1)S(1)}, bf16[2,128,4,128]{3,1,0,2:T(8,128)(2,1)}, u32[]{:S(2)}) copy-start(bf16[2,128,4,128]{3,1,0,2:T(8,128)(2,1)} %copy.68) | copy-start | bytes 786436
  130.2 3.5 %copy-start.12 = (f32[4,256]{1,0:T(4,128)S(1)}, f32[4,256]{1,0:T(4,128)}, u32[]{:S(2)}) copy-start(f32[4,256]{1,0:T(4,128)} %get-tuple-element.13) | copy-start | bytes 12292
  130.2 3.5 %copy-start.13 = (f32[4,256]{1,0:T(4,128)S(1)}, f32[4,256]{1,0:T(4,128)}, u32[]{:S(2)}) copy-start(f32[4,256]{1,0:T(4,128)} %get-tuple-element.22) | copy-start | bytes 12292
  133.7 4.3 %copy-start.6 = (pred[256,1024]{0,1:T(8,128)(4,1)S(1)}, pred[256,1024]{0,1:T(8,128)(4,1)}, u32[]{:S(2)}) copy-start(pred[256,1024]{0,1:T(8,128)(4,1)} %fusion.49) | copy-start | bytes 786436
  138.0 5.1 %copy-start.16 = (s32[512]{0:T(512)S(1)}, s32[512]{0:T(512)}, u32[]{:S(2)}) copy-start(s32[512]{0:T(512)} %param.22) | copy-start | bytes 6148
  138.0 5.1 %copy-start.17 = (s32[64]{0:T(128)S(1)}, s32[64]{0:T(128)}, u32[]{:S(2)}) copy-start(s32[64]{0:T(128)} %iota_add_fusion.3) | copy-start | bytes 772
  143.1 1.6 copy-start.1
  145.5 70.0 %reduce-scatter.7.cloned.1.call-start = ((), (), s32[]{:S(2)}) async-start(), calls=%async_computation.7 | async-start | bytes 589824
Sparse Core Ops, SparseCore 0:
  9.6 31.4 all-gather.3
  42.7 27.7 all-gather.5
  145.6 28.4 reduce-scatter.4
  187.4 28.1 reduce-scatter.6
where the time goes:
time: 224 us
  waiting for transfers between devices  86.2 us (38%)
  blocking collectives  44.3 us (20%)
  matrix products  32.9 us (15%)
  local copies, waits for them, and re-layouts  26.7 us (12%)
  between operations  14.7 us (7%)
  starting transfers between devices  10.8 us (5%)
  other arithmetic  7.84 us (4%)
    all_gather x1, blocking collectives, local(): hashed_all = lax.all_gather(hashed_local, 'ctx', axis=0, tiled=True)  36.2 us
    all_to_all x1, waiting for transfers between devices, local(): lax.all_to_all(query_local, 'ctx', split_axis=1, concat_axis=0, tiled=True)  29.9 us
    reduce_scatter x1, waiting for transfers between devices, local(): lax.psum_scatter(partial_sketch.astype(jnp.bfloat16), 'ctx', scatter_dime...  28.6 us
    unnamed x5, waiting for transfers between devices  27.7 us
    dot_general x4, matrix products, local(): jnp.einsum('hqk,khd->qhd', grad_scores, key_rows, preferred_element_type=...  15.3 us
    dot_general x4, matrix products, local(): jnp.einsum('qhd,khd->hqk', query_rows, key_rows, preferred_element_type=j...  9.14 us
    all_gather x1, blocking collectives, local(): every_sketch = lax.all_gather(local_sketch, 'doc', axis=0, tiled=True)  8.11 us
    unnamed x42, local copies, waits for them, and re-layouts  6.88 us
  transfers between devices with their start and end apart: 6, of which 3 were waited for; matrix products, arithmetic and copies ran while one was open for 11% of the time, Pallas kernels for 0%

commit v1 on v0

v1 whole, which is shorter than its diff:
```python
import functools

import jax
import jax.numpy as jnp
from jax import lax
from jax.experimental import pallas as pl
from jax.experimental.pallas import tpu as pltpu
from jax.sharding import PartitionSpec as P

HD = 128
K1 = 128
K2 = 64
LANES = 128
VMEM_LIMIT = 48 * 1024 * 1024


def dot_nt(left, right):
    return lax.dot_general(
        left, right, (((1,), (1,)), ((), ())), preferred_element_type=jnp.float32
    )


def dot_tn(left, right):
    return lax.dot_general(
        left, right, (((0,), (0,)), ((), ())), preferred_element_type=jnp.float32
    )


def sign_table(codes, levels, buckets):
    plus_part = (codes[:, None] == levels[None, :]).astype(jnp.float32)
    minus_part = (codes[:, None] == levels[None, :] + buckets).astype(jnp.float32)
    return (plus_part - minus_part).astype(jnp.bfloat16)


def split_terms(value, terms):
    parts = []
    for _ in range(terms):
        part = value.astype(jnp.bfloat16)
        parts.append(part)
        value = value - part.astype(jnp.float32)
    return parts


def stage_kernel(info, *refs, heads, causal, first, last, scale):
    refs = list(refs)
    q_own, q_sib, g_own, g_sib, log_ref, delta_ref, table_ref = refs[:7]
    k_same, k_cross, v_same, v_cross = refs[7:11]
    rest = refs[11:]
    if not first:
        before = rest.pop(0)
    if last:
        hi_own, hi_sib = rest.pop(0), rest.pop(0)
    out_ref, total = rest
    group = pl.program_id(0)
    rows = q_own.shape[0]
    keys = jnp.concatenate([k_same[...], k_cross[...]], axis=0)
    values = jnp.concatenate([v_same[...], v_cross[...]], axis=0)
    key_index = lax.broadcasted_iota(jnp.int32, (2 * rows, LANES), 0)
    key_pos = jnp.where(key_index < rows, info[4] + key_index, info[5] - rows + key_index)
    seen = key_pos >= info[3]
    if causal:
        shape = (2 * rows, 2 * rows)
        row_at = lax.broadcasted_iota(jnp.int32, shape, 0)
        col_at = lax.broadcasted_iota(jnp.int32, shape, 1)
        row_at = jnp.where(row_at < rows, info[1] + row_at, info[2] - rows + row_at)
        col_at = jnp.where(col_at < rows, info[4] + col_at, info[5] - rows + col_at)
        visible = col_at <= row_at
    log_cols = log_ref[...].T
    delta_cols = delta_ref[...].T

    @pl.when(group == 0)
    def _():
        if first:
            total[...] = jnp.zeros_like(total)
        else:
            total[...] = before[...]

    sums = jnp.zeros(total.shape, jnp.float32)
    for head in range(heads):
        at = slice(head * HD, (head + 1) * HD)
        hashed_keys = jnp.dot(keys, table_ref[at, :], preferred_element_type=jnp.float32)
        hashed_keys = jnp.where(seen, hashed_keys, 0.0).astype(jnp.bfloat16)
        query = jnp.concatenate([q_own[:, at], q_sib[:, at]], axis=0)
        grad = jnp.concatenate([g_own[:, at], g_sib[:, at]], axis=0)
        logits = dot_nt(query, keys) * (HD**-0.5) - log_cols[:, head : head + 1]
        weights = jnp.exp(jnp.minimum(logits, 1.0))
        if causal:
            weights = jnp.where(visible, weights, 0.0)
        grad_weights = dot_nt(grad, values) - delta_cols[:, head : head + 1]
        scores = (weights * grad_weights).astype(jnp.bfloat16)
        sums += jnp.dot(scores, hashed_keys, preferred_element_type=jnp.float32)
    total[...] += sums

    @pl.when(group == pl.num_programs(0) - 1)
    def _():
        if not last:
            out_ref[...] = total[...]
        else:
            hashed = jnp.concatenate([hi_own[...], hi_sib[...]], axis=0)
            both = sum(dot_tn(hashed, part) for part in split_terms(total[...], 2))
            half = K1 // 2
            lane = lax.broadcasted_iota(jnp.int32, (half, LANES), 1)
            out_ref[...] = jnp.where(lane < K2, both[:half], both[half:]) * scale


def stage(info, q, q_sib, g, g_sib, logs, deltas, table, same, cross, before, hashed, causal, scale):
    rows = q.shape[0]
    half = q_sib.shape[1]
    groups = same.shape[1] // (2 * HD)
    width = half // groups
    heads = width // HD
    first, last = before is None, hashed is not None
    own_spec = pl.BlockSpec((rows, width), lambda g, info: (0, info[0] * groups + g))
    sib_spec = pl.BlockSpec((rows, width), lambda g, info: (0, g))
    stat_spec = pl.BlockSpec((heads, 2 * rows), lambda g, info: (g, 0))
    key_spec = pl.BlockSpec((rows, HD), lambda g, info: (0, g))
    value_spec = pl.BlockSpec((rows, HD), lambda g, info: (0, groups + g))
    whole = lambda shape: pl.BlockSpec(shape, lambda g, info: (0, 0))
    in_specs = [own_spec, sib_spec, own_spec, sib_spec, stat_spec, stat_spec]
    in_specs += [pl.BlockSpec((width, LANES), lambda g, info: (g, 0))]
    in_specs += [key_spec, key_spec, value_spec, value_spec]
    args = [q, q_sib, g, g_sib, logs, deltas, table, same, cross, same, cross]
    if not first:
        in_specs.append(whole(before.shape))
        args.append(before)
    if last:
        in_specs += [whole(hashed[0].shape)] * 2
        args += list(hashed)
    out_shape = (K1 // 2, LANES) if last else (2 * rows, LANES)
    cells = 2 * rows * 2 * rows * heads * groups
    return pl.pallas_call(
        functools.partial(
            stage_kernel, heads=heads, causal=causal, first=first, last=last, scale=scale
        ),
        out_shape=jax.ShapeDtypeStruct(out_shape, jnp.float32),
        grid_spec=pltpu.PrefetchScalarGridSpec(
            num_scalar_prefetch=1,
            grid=(groups,),
            in_specs=in_specs,
            out_specs=whole(out_shape),
            scratch_shapes=[pltpu.VMEM((2 * rows, LANES), jnp.float32)],
        ),
        compiler_params=pltpu.CompilerParams(vmem_limit_bytes=VMEM_LIMIT),
        cost_estimate=pl.CostEstimate(
            flops=6 * HD * cells, bytes_accessed=5 * 2**20, transcendentals=cells
        ),
    )(info, *args)


def score_kernel(info, recv_ref, stored_ref, own_ref, partial_ref, sums, flat, *, scale):
    docs, parts, chunk, _ = recv_ref.shape
    for doc in range(docs):
        sums[doc] = jnp.sum(recv_ref[doc], axis=0)
    for row in range(chunk):
        flat[:, row * LANES : (row + 1) * LANES] = sums[:, row, :]
        own_ref[:, row * LANES : (row + 1) * LANES] = sums[info[0], row : row + 1, :]
    pieces = split_terms(flat[...], 3)
    stacked = jnp.concatenate(pieces, axis=0)
    products = dot_nt(stacked, stored_ref[...])
    partial = (products[:docs] + products[docs : 2 * docs] + products[2 * docs :]) * scale
    if len(partial_ref.shape) == 3:
        for part in range(parts):
            partial_ref[part] = partial[:, part * LANES : (part + 1) * LANES]
    else:
        partial_ref[...] = partial


def local(
    queries,
    key_heads,
    value_heads,
    out_grad,
    log_sums,
    row_delta,
    doc_start,
    layer_input,
    hash_in,
    hash_out,
    query_sketch,
):
    ctx_count = lax.axis_size("ctx")
    docs = lax.axis_size("doc")
    chips = ctx_count // 2
    place = lax.axis_index("ctx")
    chip, core = place // 2, place % 2
    tok_rows = queries.shape[1]
    seq_len = tok_rows * ctx_count
    local_heads = log_sums.shape[1]
    core_heads = local_heads * chips
    half = queries.shape[2] // 2
    kv_half = key_heads.shape[2] // 2
    first_core = core == 0

    def halves(array, width):
        low, high = array[:, :width], array[:, width:]
        return jnp.where(first_core, low, high), jnp.where(first_core, high, low)

    def permute(array, target):
        pairs = [(i, target(i)) for i in range(ctx_count)]
        return lax.ppermute(array, "ctx", [pair for pair in pairs if pair[1] < ctx_count])

    key_mine, key_other = halves(key_heads[0], kv_half)
    value_mine, value_other = halves(value_heads[0], kv_half)
    mine = jnp.concatenate([key_mine, value_mine], axis=1)
    other = jnp.concatenate([key_other, value_other], axis=1)
    arrived = {}
    for step in range(chips - 1, 0, -1):
        arrived[step] = (
            permute(mine, lambda i: i + 2 * step),
            permute(other, lambda i: (i ^ 1) + 2 * step),
        )
    swap = lambda array: permute(array, lambda i: i ^ 1)
    arrived[0] = (mine, swap(other))
    q_sib = swap(halves(queries[0], half)[1])
    g_sib = swap(halves(out_grad[0], half)[1])

    stats = jnp.concatenate([log_sums[0], row_delta[0]], axis=0)
    stats = stats.reshape(2 * local_heads, chips, 2 * tok_rows).transpose(1, 0, 2)
    codes = hash_out.astype(jnp.float32).reshape(1, -1, 2 * tok_rows) if (
        hash_out.shape[0] % (2 * tok_rows) == 0
    ) else jnp.pad(hash_out.astype(jnp.float32), (0, -hash_out.shape[0] % (2 * tok_rows))).reshape(
        1, -1, 2 * tok_rows
    )
    code_rows = codes.shape[1]
    packed = jnp.concatenate(
        [stats, jnp.broadcast_to(codes, (chips, code_rows, 2 * tok_rows))], axis=1
    )
    packed = jnp.broadcast_to(packed[:, None], (chips, 2) + packed.shape[1:]).reshape(
        (ctx_count,) + packed.shape[1:]
    )
    packed = lax.all_to_all(packed, "ctx", split_axis=0, concat_axis=0, tiled=True)
    packed = jnp.where(first_core, packed[:chips], packed[chips:])
    stats = packed[:, : 2 * local_heads]
    stats = jnp.where(
        first_core,
        stats,
        jnp.concatenate([stats[:, :, tok_rows:], stats[:, :, :tok_rows]], axis=2),
    )
    logs = stats[:, :local_heads].reshape(core_heads, 2 * tok_rows)
    deltas = stats[:, local_heads:].reshape(core_heads, 2 * tok_rows)
    codes = packed[:, 2 * local_heads :].reshape(chips, -1)[:, : local_heads * HD]
    out_levels = (jnp.arange(LANES, dtype=jnp.int32) % K2).astype(jnp.float32)
    table_out = sign_table(codes.reshape(-1), out_levels, float(K2))

    in_levels = jnp.arange(K1, dtype=jnp.int32)
    in_levels = (in_levels % (K1 // 2)) * 2 + in_levels // (K1 // 2)
    table_in = sign_table(hash_in, in_levels, K1)
    hashed = jnp.dot(layer_input[0], table_in, preferred_element_type=jnp.float32).astype(
        jnp.bfloat16
    )
    hashed_pair = (hashed, swap(hashed))

    own_base = place * tok_rows
    sib_base = (place ^ 1) * tok_rows
    scale = HD**-0.5 * (seq_len * layer_input.shape[2] // K1) ** -0.5
    total = None
    for step in range(chips):
        shift = 2 * step * tok_rows
        info = jnp.stack(
            [core, own_base, sib_base, doc_start[0], own_base - shift, sib_base - shift]
        ).astype(jnp.int32)
        total = stage(
            info,
            queries[0],
            q_sib,
            out_grad[0],
            g_sib,
            logs,
            deltas,
            table_out,
            arrived[step][0],
            arrived[step][1],
            total,
            hashed_pair if step == chips - 1 else None,
            step == 0,
            scale,
        )

    chunk = K1 * K2 // LANES // ctx_count
    parts = total.reshape(1, ctx_count, chunk, LANES)
    parts = jnp.broadcast_to(parts, (docs,) + parts.shape[1:]).reshape(-1, chunk, LANES)
    parts = lax.all_to_all(parts, ("doc", "ctx"), split_axis=0, concat_axis=0, tiled=True)
    parts = parts.reshape(docs, ctx_count, chunk, LANES)
    stored = query_sketch.shape[0]
    wide = stored // ctx_count == LANES
    partial_shape = (ctx_count, docs, LANES) if wide else (docs, stored)
    local_sketch, partial = pl.pallas_call(
        functools.partial(score_kernel, scale=(K1 * K2) ** -0.5),
        out_shape=(
            jax.ShapeDtypeStruct((1, chunk * LANES), jnp.float32),
            jax.ShapeDtypeStruct(partial_shape, jnp.float32),
        ),
        in_specs=[
            pl.BlockSpec(memory_space=pltpu.SMEM),
            pl.BlockSpec(memory_space=pltpu.VMEM),
            pl.BlockSpec(memory_space=pltpu.VMEM),
        ],
        out_specs=(
            pl.BlockSpec(memory_space=pltpu.VMEM),
            pl.BlockSpec(memory_space=pltpu.VMEM),
        ),
        scratch_shapes=[
            pltpu.VMEM((docs, chunk, LANES), jnp.float32),
            pltpu.VMEM((docs, chunk * LANES), jnp.float32),
        ],
        compiler_params=pltpu.CompilerParams(vmem_limit_bytes=VMEM_LIMIT),
    )(lax.axis_index("doc").astype(jnp.int32).reshape(1), parts, query_sketch)
    if not wide:
        partial = partial.reshape(docs, ctx_count, -1).transpose(1, 0, 2)
    partial = lax.all_to_all(partial, "ctx", split_axis=0, concat_axis=0, tiled=True)
    return local_sketch, jnp.sum(partial, axis=0)


def solution(mesh):
    return jax.shard_map(
        local,
        mesh=mesh,
        in_specs=(
            P("doc", "ctx", None),
            P("doc", "ctx", None),
            P("doc", "ctx", None),
            P("doc", "ctx", None),
            P("doc", "ctx", None),
            P("doc", "ctx", None),
            P("doc"),
            P("doc", "ctx", None),
            P(),
            P("ctx"),
            P("doc", "ctx"),
        ),
        out_specs=(P("doc", "ctx"), P(None, ("doc", "ctx"))),
        check_vma=False,
    )
```

time: 224 us -> 90.9 us (0.41)
  waiting for transfers between devices: 86.2 us -> 8.2 us
  blocking collectives: 44.3 us -> 8 us
  matrix products: 32.9 us -> 2.79 us
  Pallas kernels: 0 us -> 22.6 us
  starting transfers between devices: 10.8 us -> 24.6 us
  local copies, waits for them, and re-layouts: 26.7 us -> 13.6 us
  between operations: 14.7 us -> 1.62 us
    all_gather x2 -> x0, blocking collectives: 44.3 us -> none  [the longest x1 36.2 us: local(): hashed_all = lax.all_gather(hashed_local, 'ctx', axis=0, tiled=True)]
    reduce_scatter x1 -> x0, waiting for transfers between devices: 28.6 us -> none  [local(): lax.psum_scatter(partial_sketch.astype(jnp.bfloat16), 'ctx', scatter_dime...]
    unnamed x5 -> x0, waiting for transfers between devices: 27.7 us -> none
    dot_general x10 -> x0, matrix products: 26.9 us -> none  [the longest x4 15.3 us: local(): jnp.einsum('hqk,khd->qhd', grad_scores, key_rows, preferred_element_type=...]
    pallas_call x0 -> x5, Pallas kernels: none -> 22.6 us  [the longest x4 21.4 us: stage(): pl.pallas_call(functools.partial(stage_kernel, heads=heads, causal=causal...]
    all_to_all x2, waiting for transfers between devices: 29.9 us -> 8.17 us  [the longest x1 8.17 us: local(): lax.all_to_all(parts, ('doc', 'ctx'), split_axis=0, concat_axis=0, tiled=...]
    ppermute x0 -> x10, starting transfers between devices: none -> 17.7 us  [permute(): lax.ppermute(array, 'ctx', [pair for pair in pairs if pair[1] < ctx_count])]
    slice x11 -> x2, local copies, waits for them, and re-layouts: 8.95 us -> 0.62 us  [the longest x1 0.62 us: local(): deltas = stats[:, local_heads:].reshape(core_heads, 2 * tok_rows)]
  transfers between devices with their start and end apart: 6 -> 12, of which waited for: 3 -> 1; matrix products, arithmetic and copies ran while one was open for 11% -> 17% of each run, Pallas kernels for 0% -> 18%
where the time goes in v1:
time: 90.9 us; the launch traced here: 89.7 us
  starting transfers between devices  24.6 us (27%)
  Pallas kernels  22.6 us (25%)
  local copies, waits for them, and re-layouts  13.6 us (15%)
  other arithmetic  8.42 us (9%)
  waiting for transfers between devices  8.2 us (9%)
  blocking collectives  8 us (9%)
  matrix products  2.79 us (3%)
  between operations  1.62 us (2%)
    pallas_call x4, Pallas kernels, stage(): pl.pallas_call(functools.partial(stage_kernel, heads=heads, causal=causal...  21.4 us
    ppermute x10, starting transfers between devices, permute(): lax.ppermute(array, 'ctx', [pair for pair in pairs if pair[1] < ctx_count])  17.7 us
    all_to_all x1, waiting for transfers between devices, local(): lax.all_to_all(parts, ('doc', 'ctx'), split_axis=0, concat_axis=0, tiled=...  8.17 us
    all_to_all x1, blocking collectives, local(): lax.all_to_all(partial, 'ctx', split_axis=0, concat_axis=0, tiled=True)  8 us
    unnamed x30, local copies, waits for them, and re-layouts  5.45 us
    all_to_all x1, starting transfers between devices, local(): lax.all_to_all(packed, 'ctx', split_axis=0, concat_axis=0, tiled=True)  4 us
    select_n x3, other arithmetic, halves(): return (jnp.where(first_core, low, high), jnp.where(first_core, high, low))  3.5 us
    all_to_all x1, starting transfers between devices, local(): lax.all_to_all(parts, ('doc', 'ctx'), split_axis=0, concat_axis=0, tiled=...  2.85 us
  transfers between devices with their start and end apart: 12, of which 1 were waited for; matrix products, arithmetic and copies ran while one was open for 17% of the time, Pallas kernels for 18%

profile of v1, /device:TPU:0, one launch (start us, length us, event | category | flops | bytes accessed | tf_op | source)
XLA Modules:
  0.0 89.7 jit_solution(3289573771798371650)
XLA Ops:
  0.6 0.0 copy-start
  0.6 0.0 copy-start.1
  0.7 1.8 %broadcast_select_fusion = (bf16[128,256]{1,0:T(8,128)(2,1)S(1)}, bf16[128,256]{1,0:T(8,128)(2,1)}, bf16[128,256]{1,0:T(8,128)(2,1)}, bf16[128,256]{1,0:T(8,128)(2,1)S(1)}) fusion(pred[]{:T(512)S(6)} %eq.29, bf16[128,512]{1,0:T(8,128)(2,1)} %bitcast.44, bf16[128,512]{1,0:T(8,128)(2,1)} %bitcast.45), kind=kLoop, calls=%fused_computation.14 | loop fusion | flops 131072 | bytes 524289 | tf_op jit(solution)/shard_map/jit(_where)/select_n | solution.py:196
  2.4 0.7 pad_maximum_fusion.1
  3.1 0.5 collective-permute-start.8
  3.6 4.6 %collective-permute-start.7 = (bf16[128,512]{1,0:T(8,128)(2,1)}, bf16[128,512]{1,0:T(8,128)(2,1)S(1)}, u32[]{:S(2)}, u32[]{:S(2)}) collective-permute-start(bf16[128,512]{1,0:T(8,128)(2,1)} %pad_maximum_fusion.1), channel_id=1, source_target_pairs={{0,3},{1,2},{2,5},{3,4},{4,7},{5,6},{8,11},{9,10},{10,13},{11,12},... | collective-permute-start | bytes 393224 | tf_op jit(solution)/shard_map/ppermute | solution.py:200
  8.2 0.7 concatenate.20
  8.9 0.7 concatenate.21
  9.6 0.7 convert_element_type.38
  10.4 0.7 broadcast_in_dim.12
  11.1 4.0 %all-to-all-start = ((f32[8,10,256]{2,1,0:T(8,128)}), f32[8,10,256]{2,1,0:T(8,128)}, u32[]{:S(2)}, u32[]{:S(2)}) async-start(f32[8,10,256]{2,1,0:T(8,128)} %bitcast.9), calls=%async_computation | async-start | bytes 262144 | tf_op jit(solution)/shard_map/all_to_all | solution.py:231
  15.1 0.0 copy-start.2
  15.1 0.0 copy-done.1
  15.1 0.9 slice_select_fusion.1
  16.0 0.4 collective-permute-start
  16.3 0.2 copy-done.2
  16.5 0.9 slice_select_fusion
  17.3 0.4 collective-permute-start.1
  17.7 0.9 pad_maximum_fusion.refs_7_.refs_9_
  18.6 4.2 %collective-permute-start.6 = (bf16[128,512]{1,0:T(8,128)(2,1)S(1)}, bf16[128,512]{1,0:T(8,128)(2,1)}, u32[]{:S(2)}, u32[]{:S(2)}) collective-permute-start(bf16[128,512]{1,0:T(8,128)(2,1)S(1)} %pad_maximum_fusion.refs_7_.refs_9_), channel_id=1, source_target_pairs={{0,2},{1,3},{2,4},{3,5},{4,6},{5,7},{8,10},{9,11},{10,12},{11,13},... | collective-permute-start | bytes 393224 | tf_op jit(solution)/shard_map/ppermute | solution.py:200
  22.9 2.8 %fusion.8.refs_12_ = bf16[128,128]{1,0:T(8,128)(2,1)} fusion(s32[128]{0:T(128)S(1)} %get-tuple-element.17, s32[128]{0:T(128)S(1)} %get-tuple-element.16, s32[8192]{0:T(1024)} %param.19, bf16[1,128,8192]{2,1,0:T(8,128)(2,1)S(1)} %copy-done), kind=kOutput, calls=%fused_computation.7 | convolution fusion | flops 274743296 | bytes 2163712 | tf_op jit(solution)/shard_map/dot_general | solution.py:248
  26.3 0.7 stack.62.info
  27.0 0.7 stack.61.info
  27.6 0.6 stack.58.info
  28.2 0.7 stack.55.info
  28.9 0.0 all-to-all-done
  28.9 0.9 slice_select_fusion.2
  29.8 1.2 %subtract_convert_fusion.6.refs_6_ = bf16[2048,128]{1,0:T(8,128)(2,1)} fusion(f32[128]{0:T(128)S(1)} %broadcast_add_fusion.1, f32[128]{0:T(128)S(1)} %fusion.12, f32[2048]{0:T(1024)S(1)} %bitcast.46), kind=kLoop, calls=%fused_computation.8 | loop fusion | flops 1572864 | bytes 533504 | tf_op jit(solution)/shard_map/convert_element_type | solution.py:32
  31.0 0.6 fusion.14
  31.6 0.7 reshape.73.refs_4_
  32.4 1.3 %reshape.74.refs_5_ = f32[16,256]{1,0:T(8,128)} reshape(f32[4,4,256]{2,1,0:T(4,128)} %get-tuple-element.12) | data formatting | bytes 32768 | tf_op jit(solution)/shard_map/reshape | solution.py:240
  33.7 0.0 collective-permute-done.8.refs_8_.refs_10_
  33.7 3.7 %collective-permute-start.4 = (bf16[128,512]{1,0:T(8,128)(2,1)S(1)}, bf16[128,512]{1,0:T(8,128)(2,1)S(1)}, u32[]{:S(2)}, u32[]{:S(2)}) collective-permute-start(bf16[128,512]{1,0:T(8,128)(2,1)S(1)} %pad_maximum_fusion.refs_7_.refs_9_), channel_id=1, source_target_pairs={{0,4},{1,5},{2,6},{3,7},{8,12},{9,13},{10,14},{11,15},{16,20},{17,... | collective-permute-start | bytes 393224 | tf_op jit(solution)/shard_map/ppermute | solution.py:200
  37.4 0.0 collective-permute-done.refs_1_
  37.4 1.3 %collective-permute-start.5 = (bf16[128,512]{1,0:T(8,128)(2,1)}, bf16[128,512]{1,0:T(8,128)(2,1)S(1)}, u32[]{:S(2)}, u32[]{:S(2)}) collective-permute-start(bf16[128,512]{1,0:T(8,128)(2,1)} %pad_maximum_fusion.1), channel_id=1, source_target_pairs={{0,5},{1,4},{2,7},{3,6},{8,13},{9,12},{10,15},{11,14},{16,21},{17,... | collective-permute-start | bytes 393224 | tf_op jit(solution)/shard_map/ppermute | solution.py:200
  38.7 0.0 collective-permute-done.1.refs_3_
  38.7 1.3 %collective-permute-start.2 = (bf16[128,512]{1,0:T(8,128)(2,1)S(1)}, bf16[128,512]{1,0:T(8,128)(2,1)S(1)}, u32[]{:S(2)}, u32[]{:S(2)}) collective-permute-start(bf16[128,512]{1,0:T(8,128)(2,1)S(1)} %pad_maximum_fusion.refs_7_.refs_9_), channel_id=1, source_target_pairs={{0,6},{1,7},{8,14},{9,15},{16,22},{17,23},{24,30},{25,31}} | collective-permute-start | bytes 393224 | tf_op jit(solution)/shard_map/ppermute | solution.py:200
  40.0 0.0 copy-start.3
  40.0 1.2 %copy-done.3 = bf16[1,128,4096]{2,1,0:T(8,128)(2,1)S(1)} copy-done((bf16[1,128,4096]{2,1,0:T(8,128)(2,1)S(1)}, bf16[1,128,4096]{2,1,0:T(8,128)(2,1)}, u32[]{:S(2)}) %copy-start.3) | copy-done | bytes 1048600
  41.2 1.0 %copy-done.5 = bf16[2048,128]{1,0:T(8,128)(2,1)S(1)} copy-done((bf16[2048,128]{1,0:T(8,128)(2,1)S(1)}, bf16[2048,128]{1,0:T(8,128)(2,1)}, u32[]{:S(2)}) %copy-start.5) | copy-done | bytes 524312
  42.3 0.7 copy-done.8
  43.0 0.7 copy-done.13
  43.7 5.4 %shard_map.122.refs_11_ = f32[256,128]{1,0:T(8,128)S(1)} custom-call(s32[6]{0:T(128)S(1)} %copy-done.13, bf16[128,4096]{1,0:T(8,128)(2,1)S(1)} %bitcast.33, bf16[128,2048]{1,0:T(8,128)(2,1)} %collective-permute-done.refs_1_, bf16[128,4096]{1,0:T(8,128)(2,1)S(1)} %bitcast.38, bf16[128,2048]{1,0:T(8,128)(2,1)} %collective-permute-done.1.refs_3_, ...), custom_call_target="tpu_custom_call" | custom-call | flops 805306368 | bytes 5242880 | tf_op jit(solution)/shard_map/pallas_call | solution.py:131
  49.0 0.0 copy-start.11
  49.0 0.0 collective-permute-done.6.refs_7_.refs_9_
  49.0 1.3 %collective-permute-start.3 = (bf16[128,512]{1,0:T(8,128)(2,1)}, bf16[128,512]{1,0:T(8,128)(2,1)S(1)}, u32[]{:S(2)}, u32[]{:S(2)}) collective-permute-start(bf16[128,512]{1,0:T(8,128)(2,1)} %pad_maximum_fusion.1), channel_id=1, source_target_pairs={{0,7},{1,6},{8,15},{9,14},{16,23},{17,22},{24,31},{25,30}} | collective-permute-start | bytes 393224 | tf_op jit(solution)/shard_map/ppermute | solution.py:200
  50.3 0.0 collective-permute-done.7.refs_8_.refs_10_
  50.4 0.2 collective-permute-start.9
  50.5 5.3 %shard_map.123.refs_11_ = f32[256,128]{1,0:T(8,128)S(1)} custom-call(s32[6]{0:T(128)S(1)} %copy-done.12, bf16[128,4096]{1,0:T(8,128)(2,1)S(1)} %bitcast.34, bf16[128,2048]{1,0:T(8,128)(2,1)} %collective-permute-done.refs_1_, bf16[128,4096]{1,0:T(8,128)(2,1)S(1)} %bitcast.39, bf16[128,2048]{1,0:T(8,128)(2,1)} %collective-permute-done.1.refs_3_, ...), custom_call_target="tpu_custom_call" | custom-call | flops 805306368 | bytes 5242880 | tf_op jit(solution)/shard_map/pallas_call | solution.py:131
  55.8 0.0 copy-start.10
  55.9 0.0 collective-permute-done.4.refs_7_.refs_9_
  55.9 0.0 collective-permute-done.5.refs_8_.refs_10_
  55.9 5.3 %shard_map.124.refs_11_ = f32[256,128]{1,0:T(8,128)S(1)} custom-call(s32[6]{0:T(128)S(1)} %copy-done.11, bf16[128,4096]{1,0:T(8,128)(2,1)S(1)} %bitcast.35, bf16[128,2048]{1,0:T(8,128)(2,1)} %collective-permute-done.refs_1_, bf16[128,4096]{1,0:T(8,128)(2,1)S(1)} %bitcast.40, bf16[128,2048]{1,0:T(8,128)(2,1)} %collective-permute-done.1.refs_3_, ...), custom_call_target="tpu_custom_call" | custom-call | flops 805306368 | bytes 5242880 | tf_op jit(solution)/shard_map/pallas_call | solution.py:131
  61.2 0.0 collective-permute-done.9.refs_13_
  61.2 0.0 collective-permute-done.2.refs_7_.refs_9_
  61.2 0.0 collective-permute-done.3.refs_8_.refs_10_
  61.2 5.5 %shard_map.125 = f32[64,128]{1,0:T(8,128)S(1)} custom-call(s32[6]{0:T(128)S(1)} %copy-done.10, bf16[128,4096]{1,0:T(8,128)(2,1)S(1)} %bitcast.36, bf16[128,2048]{1,0:T(8,128)(2,1)} %collective-permute-done.refs_1_, bf16[128,4096]{1,0:T(8,128)(2,1)S(1)} %bitcast.41, bf16[128,2048]{1,0:T(8,128)(2,1)} %collective-permute-done.1.refs_3_, ...), custom_call_target="tpu_custom_call" | custom-call | flops 805306368 | bytes 5242880 | tf_op jit(solution)/shard_map/pallas_call | solution.py:131
  66.7 0.7 broadcast_in_dim.14
  67.4 2.8 %all-to-all-start.1 = ((f32[32,8,128]{2,1,0:T(8,128)}), f32[32,8,128]{2,1,0:T(8,128)S(1)}, u32[]{:S(2)}, u32[]{:S(2)}) async-start(f32[32,8,128]{2,1,0:T(8,128)} %bitcast.19), calls=%async_computation.1 | async-start | bytes 262144 | tf_op jit(solution)/shard_map/all_to_all | solution.py:282
  70.2 8.2 %all-to-all-done.1 = f32[32,8,128]{2,1,0:T(8,128)S(1)} async-done(((f32[32,8,128]{2,1,0:T(8,128)}), f32[32,8,128]{2,1,0:T(8,128)S(1)}, u32[]{:S(2)}, u32[]{:S(2)}) %all-to-all-start.1) | async-done | bytes 131104 | tf_op jit(solution)/shard_map/all_to_all | solution.py:282
  78.4 1.6 %copy-done.7 = bf16[1024,1024]{1,0:T(8,128)(2,1)S(1)} copy-done((bf16[1024,1024]{1,0:T(8,128)(2,1)S(1)}, bf16[1024,1024]{1,0:T(8,128)(2,1)}, u32[]{:S(2)}) %copy-start.7) | copy-done | bytes 2097176
  80.0 1.1 %shard_map.126 = (f32[1,1024]{1,0:T(1,128)}, f32[8,4,128]{2,1,0:T(4,128)S(1)}) custom-call(s32[1]{0:T(128)} %bitcast.info, f32[4,8,8,128]{3,2,1,0:T(8,128)S(1)} %bitcast.42, bf16[1024,1024]{1,0:T(8,128)(2,1)S(1)} %copy-done.7), custom_call_target="tpu_custom_call" | custom-call | tf_op jit(solution)/shard_map/pallas_call | solution.py:287
  81.1 8.0 %all_to_all.15 = f32[8,4,128]{2,1,0:T(4,128)S(1)} all-to-all(f32[8,4,128]{2,1,0:T(4,128)S(1)} %get-tuple-element.5), channel_id=1, replica_groups=mesh['doc'=4,'ctx'=8] {'ctx'}, dimensions={0} | all-to-all | bytes 32768 | tf_op jit(solution)/shard_map/all_to_all | solution.py:310
  89.2 0.6 reduce_sum.9
  (27 shorter events, 0.1 us)
Async XLA Ops:
  0.6 22.2 %copy-start = (bf16[1,128,8192]{2,1,0:T(8,128)(2,1)S(1)}, bf16[1,128,8192]{2,1,0:T(8,128)(2,1)}, u32[]{:S(2)}) copy-start(bf16[1,128,8192]{2,1,0:T(8,128)(2,1)} %param.18) | copy-start | bytes 6291460
  0.6 14.4 %copy-start.1 = (bf16[1,128,4096]{2,1,0:T(8,128)(2,1)S(1)}, bf16[1,128,4096]{2,1,0:T(8,128)(2,1)}, u32[]{:S(2)}) copy-start(bf16[1,128,4096]{2,1,0:T(8,128)(2,1)} %param.11) | copy-start | bytes 3145732
  3.1 30.6 %collective-permute-start.8 = (bf16[128,512]{1,0:T(8,128)(2,1)}, bf16[128,512]{1,0:T(8,128)(2,1)S(1)}, u32[]{:S(2)}, u32[]{:S(2)}) collective-permute-start(bf16[128,512]{1,0:T(8,128)(2,1)} %pad_maximum_fusion.1), channel_id=1, source_target_pairs={{0,1},{1,0},{2,3},{3,2},{4,5},{5,4},{6,7},{7,6},{8,9},{9,8},{10,11... | collective-permute-start | bytes 393224 | tf_op jit(solution)/shard_map/ppermute | solution.py:200
  3.6 46.8 %collective-permute-start.7 = (bf16[128,512]{1,0:T(8,128)(2,1)}, bf16[128,512]{1,0:T(8,128)(2,1)S(1)}, u32[]{:S(2)}, u32[]{:S(2)}) collective-permute-start(bf16[128,512]{1,0:T(8,128)(2,1)} %pad_maximum_fusion.1), channel_id=1, source_target_pairs={{0,3},{1,2},{2,5},{3,4},{4,7},{5,6},{8,11},{9,10},{10,13},{11,12},... | collective-permute-start | bytes 393224 | tf_op jit(solution)/shard_map/ppermute | solution.py:200
  11.1 17.9 %all-to-all-start = ((f32[8,10,256]{2,1,0:T(8,128)}), f32[8,10,256]{2,1,0:T(8,128)}, u32[]{:S(2)}, u32[]{:S(2)}) async-start(f32[8,10,256]{2,1,0:T(8,128)} %bitcast.9), calls=%async_computation | async-start | bytes 262144 | tf_op jit(solution)/shard_map/all_to_all | solution.py:231
  15.1 1.4 %copy-start.2 = (bf16[1,128,4096]{2,1,0:T(8,128)(2,1)S(1)}, bf16[1,128,4096]{2,1,0:T(8,128)(2,1)}, u32[]{:S(2)}) copy-start(bf16[1,128,4096]{2,1,0:T(8,128)(2,1)} %param.14) | copy-start | bytes 3145732
  16.0 21.4 %collective-permute-start = (bf16[128,2048]{1,0:T(8,128)(2,1)}, bf16[128,2048]{1,0:T(8,128)(2,1)}, u32[]{:S(2)}, u32[]{:S(2)}) collective-permute-start(bf16[128,2048]{1,0:T(8,128)(2,1)} %slice_select_fusion.1), channel_id=1, source_target_pairs={{0,1},{1,0},{2,3},{3,2},{4,5},{5,4},{6,7},{7,6},{8,9},{9,8},{10,11... | collective-permute-start | bytes 1572872 | tf_op jit(solution)/shard_map/ppermute | solution.py:200
  17.3 21.3 %collective-permute-start.1 = (bf16[128,2048]{1,0:T(8,128)(2,1)}, bf16[128,2048]{1,0:T(8,128)(2,1)}, u32[]{:S(2)}, u32[]{:S(2)}) collective-permute-start(bf16[128,2048]{1,0:T(8,128)(2,1)} %slice_select_fusion), channel_id=1, source_target_pairs={{0,1},{1,0},{2,3},{3,2},{4,5},{5,4},{6,7},{7,6},{8,9},{9,8},{10,11... | collective-permute-start | bytes 1572872 | tf_op jit(solution)/shard_map/ppermute | solution.py:200
  18.6 30.4 %collective-permute-start.6 = (bf16[128,512]{1,0:T(8,128)(2,1)S(1)}, bf16[128,512]{1,0:T(8,128)(2,1)}, u32[]{:S(2)}, u32[]{:S(2)}) collective-permute-start(bf16[128,512]{1,0:T(8,128)(2,1)S(1)} %pad_maximum_fusion.refs_7_.refs_9_), channel_id=1, source_target_pairs={{0,2},{1,3},{2,4},{3,5},{4,6},{5,7},{8,10},{9,11},{10,12},{11,13},... | collective-permute-start | bytes 393224 | tf_op jit(solution)/shard_map/ppermute | solution.py:200
  33.7 22.2 %collective-permute-start.4 = (bf16[128,512]{1,0:T(8,128)(2,1)S(1)}, bf16[128,512]{1,0:T(8,128)(2,1)S(1)}, u32[]{:S(2)}, u32[]{:S(2)}) collective-permute-start(bf16[128,512]{1,0:T(8,128)(2,1)S(1)} %pad_maximum_fusion.refs_7_.refs_9_), channel_id=1, source_target_pairs={{0,4},{1,5},{2,6},{3,7},{8,12},{9,13},{10,14},{11,15},{16,20},{17,... | collective-permute-start | bytes 393224 | tf_op jit(solution)/shard_map/ppermute | solution.py:200
  37.4 18.5 %collective-permute-start.5 = (bf16[128,512]{1,0:T(8,128)(2,1)}, bf16[128,512]{1,0:T(8,128)(2,1)S(1)}, u32[]{:S(2)}, u32[]{:S(2)}) collective-permute-start(bf16[128,512]{1,0:T(8,128)(2,1)} %pad_maximum_fusion.1), channel_id=1, source_target_pairs={{0,5},{1,4},{2,7},{3,6},{8,13},{9,12},{10,15},{11,14},{16,21},{17,... | collective-permute-start | bytes 393224 | tf_op jit(solution)/shard_map/ppermute | solution.py:200
  38.7 22.5 %collective-permute-start.2 = (bf16[128,512]{1,0:T(8,128)(2,1)S(1)}, bf16[128,512]{1,0:T(8,128)(2,1)S(1)}, u32[]{:S(2)}, u32[]{:S(2)}) collective-permute-start(bf16[128,512]{1,0:T(8,128)(2,1)S(1)} %pad_maximum_fusion.refs_7_.refs_9_), channel_id=1, source_target_pairs={{0,6},{1,7},{8,14},{9,15},{16,22},{17,23},{24,30},{25,31}} | collective-permute-start | bytes 393224 | tf_op jit(solution)/shard_map/ppermute | solution.py:200
  40.0 1.2 %copy-start.3 = (bf16[1,128,4096]{2,1,0:T(8,128)(2,1)S(1)}, bf16[1,128,4096]{2,1,0:T(8,128)(2,1)}, u32[]{:S(2)}) copy-start(bf16[1,128,4096]{2,1,0:T(8,128)(2,1)} %param.14) | copy-start | bytes 3145732
  41.2 1.0 %copy-start.5 = (bf16[2048,128]{1,0:T(8,128)(2,1)S(1)}, bf16[2048,128]{1,0:T(8,128)(2,1)}, u32[]{:S(2)}) copy-start(bf16[2048,128]{1,0:T(8,128)(2,1)} %subtract_convert_fusion.6.refs_6_) | copy-start | bytes 1572868
  42.3 0.7 copy-start.8
  43.0 0.7 copy-start.13
  43.6 6.7 %copy-start.9 = (bf16[128,128]{1,0:T(8,128)(2,1)S(1)}, bf16[128,128]{1,0:T(8,128)(2,1)}, u32[]{:S(2)}) copy-start(bf16[128,128]{1,0:T(8,128)(2,1)} %fusion.8.refs_12_) | copy-start | bytes 98308
  43.6 6.9 %copy-start.4 = (bf16[1,128,4096]{2,1,0:T(8,128)(2,1)S(1)}, bf16[1,128,4096]{2,1,0:T(8,128)(2,1)}, u32[]{:S(2)}) copy-start(bf16[1,128,4096]{2,1,0:T(8,128)(2,1)} %param.14) | copy-start | bytes 3145732
  43.6 6.9 %copy-start.6 = (bf16[2048,128]{1,0:T(8,128)(2,1)S(1)}, bf16[2048,128]{1,0:T(8,128)(2,1)}, u32[]{:S(2)}) copy-start(bf16[2048,128]{1,0:T(8,128)(2,1)} %subtract_convert_fusion.6.refs_6_) | copy-start | bytes 1572868
  43.7 6.9 %copy-start.12 = (s32[6]{0:T(128)S(1)}, s32[6]{0:T(128)}, u32[]{:S(2)}) copy-start(s32[6]{0:T(128)} %stack.61.info) | copy-start | bytes 76
  49.0 6.9 %copy-start.11 = (s32[6]{0:T(128)S(1)}, s32[6]{0:T(128)}, u32[]{:S(2)}) copy-start(s32[6]{0:T(128)} %stack.58.info) | copy-start | bytes 76
  49.0 12.2 %collective-permute-start.3 = (bf16[128,512]{1,0:T(8,128)(2,1)}, bf16[128,512]{1,0:T(8,128)(2,1)S(1)}, u32[]{:S(2)}, u32[]{:S(2)}) collective-permute-start(bf16[128,512]{1,0:T(8,128)(2,1)} %pad_maximum_fusion.1), channel_id=1, source_target_pairs={{0,7},{1,6},{8,15},{9,14},{16,23},{17,22},{24,31},{25,30}} | collective-permute-start | bytes 393224 | tf_op jit(solution)/shard_map/ppermute | solution.py:200
  50.4 10.8 %collective-permute-start.9 = (bf16[128,128]{1,0:T(8,128)(2,1)S(1)}, bf16[128,128]{1,0:T(8,128)(2,1)S(1)}, u32[]{:S(2)}, u32[]{:S(2)}) collective-permute-start(bf16[128,128]{1,0:T(8,128)(2,1)S(1)} %copy-done.9), channel_id=1, source_target_pairs={{0,1},{1,0},{2,3},{3,2},{4,5},{5,4},{6,7},{7,6},{8,9},{9,8},{10,11... | collective-permute-start | bytes 98312 | tf_op jit(solution)/shard_map/ppermute | solution.py:200
  55.8 5.4 %copy-start.10 = (s32[6]{0:T(128)S(1)}, s32[6]{0:T(128)}, u32[]{:S(2)}) copy-start(s32[6]{0:T(128)} %stack.55.info) | copy-start | bytes 76
  67.4 11.0 %all-to-all-start.1 = ((f32[32,8,128]{2,1,0:T(8,128)}), f32[32,8,128]{2,1,0:T(8,128)S(1)}, u32[]{:S(2)}, u32[]{:S(2)}) async-start(f32[32,8,128]{2,1,0:T(8,128)} %bitcast.19), calls=%async_computation.1 | async-start | bytes 262144 | tf_op jit(solution)/shard_map/all_to_all | solution.py:282
  78.4 1.6 %copy-start.7 = (bf16[1024,1024]{1,0:T(8,128)(2,1)S(1)}, bf16[1024,1024]{1,0:T(8,128)(2,1)}, u32[]{:S(2)}) copy-start(bf16[1024,1024]{1,0:T(8,128)(2,1)} %stored_ref.1) | copy-start | bytes 6291460

commit v2 on v0

v2 whole, which is shorter than its diff:
```python
import functools

import jax
import jax.numpy as jnp
from jax import lax
from jax.experimental import pallas as pl
from jax.experimental.pallas import tpu as pltpu
from jax.sharding import PartitionSpec as P

HD = 128
K1 = 128
K2 = 64
LANES = 128
FACTOR = HD**-0.5
STAT_TERMS = 3
NO_STEP = 1024
MIB = 1024 * 1024
SMEM = pl.BlockSpec(memory_space=pltpu.SMEM)
VMEM = pl.BlockSpec(memory_space=pltpu.VMEM)
ANY = pl.BlockSpec(memory_space=pl.ANY)


def dot_nt(left, right):
    return lax.dot_general(
        left, right, (((1,), (1,)), ((), ())), preferred_element_type=jnp.float32
    )


def dot_tn(left, right):
    return lax.dot_general(
        left, right, (((0,), (0,)), ((), ())), preferred_element_type=jnp.float32
    )


def split_terms(value, terms):
    parts = []
    for _ in range(terms):
        part = value.astype(jnp.bfloat16)
        parts.append(part)
        value = value - part.astype(jnp.float32)
    return parts


def fetch(pairs, sems):
    copies = [
        pltpu.make_async_copy(source, target, sems.at[index])
        for index, (source, target) in enumerate(pairs)
    ]
    for copy in copies:
        copy.start()
    return copies


def pack_kernel(logs_in, deltas_in, codes_in, packed, logs, deltas, codes, sems):
    for copy in fetch(((logs_in, logs), (deltas_in, deltas), (codes_in, codes)), sems):
        copy.wait()
    heads = logs.shape[0]
    code_rows = codes[...].astype(jnp.float32)
    for target in range(packed.shape[0]):
        own = slice(target * LANES, (target + 1) * LANES)
        sib = slice((target ^ 1) * LANES, ((target ^ 1) + 1) * LANES)
        packed[target, :heads, :] = logs[:, own]
        packed[target, heads : 2 * heads, :] = logs[:, sib]
        packed[target, 2 * heads : 3 * heads, :] = deltas[:, own]
        packed[target, 3 * heads : 4 * heads, :] = deltas[:, sib]
        packed[target, 4 * heads :, :] = code_rows


def prepare_kernel(place, key_in, value_in, mine, other, key, value, sems):
    rows = key.shape[0] // 2
    pieces = [pl.ds(low, rows) for low in (0, rows)]
    for copy in fetch(
        [
            (source.at[piece, :], target.at[piece, :])
            for piece in pieces
            for source, target in ((key_in, key), (value_in, value))
        ],
        sems,
    ):
        copy.wait()
    core = place[0] % 2
    half = key.shape[1] // 2
    for at_core in range(2):

        @pl.when(core == at_core)
        def _(at_core=at_core):
            near = slice(at_core * half, (at_core + 1) * half)
            far = slice((1 - at_core) * half, (2 - at_core) * half)
            mine[:, :half], mine[:, half:] = key[:, near], value[:, near]
            other[:, :half], other[:, half:] = key[:, far], value[:, far]


def join_kernel(upper, lower, _, out, sems):
    rows = upper.shape[0]
    targets = (out.at[pl.ds(0, rows), :], out.at[pl.ds(rows, rows), :])
    for copy in fetch(zip((upper, lower), targets), sems):
        copy.wait()


def hash_kernel(rows_in, codes_in, _, out, rows, codes, sems):
    count, _, width = rows.shape
    pairs = [(codes_in, codes)]
    for part in range(count):
        pairs.append((rows_in.at[:, pl.ds(part * width, width)], rows.at[part]))
    copies = fetch(pairs, sems)
    copies[0].wait()
    level = lax.broadcasted_iota(jnp.int32, (K1, width), 0)
    level = jnp.where(level < K1 // 2, 2 * level, 2 * level - K1 + 1)
    total = jnp.zeros(out.shape, jnp.float32)
    for part in range(count):
        code = codes[:, part * width : (part + 1) * width]
        sign = jnp.where(code >= K1, -1.0, 1.0)
        bucket = jnp.where(code >= K1, code - K1, code)
        table = jnp.where(level == bucket, sign, 0.0).astype(jnp.bfloat16)
        copies[1 + part].wait()
        total += dot_nt(rows[part], table)
    out[...] = total.astype(out.dtype)


def relay_kernel(place, pair, received, _, out, sems, *, relaying):
    chip = place[0] // 2
    passing = functools.reduce(jnp.logical_or, [chip == which for which in relaying])

    @pl.when(passing)
    def _():
        fetch([(received, out)], sems)[0].wait()

    @pl.when(jnp.logical_not(passing))
    def _():
        fetch([(pair, out)], sems)[0].wait()


def attend(place, start, q_at, g_at, tables, pairs, steps, causal, group, kv_groups, total):
    core = place[0] % 2
    rows = total.shape[0]
    half = rows // 2
    count = q_at.shape[0] // rows
    own_base = place[0] * half
    sib_base = jnp.where(core == 0, own_base + half, own_base - half)
    index = lax.broadcasted_iota(jnp.int32, (rows, LANES), 0)
    spread = jnp.where(index < half, own_base + index, sib_base - half + index)
    lane = lax.broadcasted_iota(jnp.int32, (rows, LANES), 1)
    ones = jnp.where(lane < STAT_TERMS * count, 1.0, 0.0).astype(jnp.bfloat16)
    keys, key_sides, value_sides = [], [], []
    for pair, step in zip(pairs, steps):
        at = slice(group * HD, (group + 1) * HD)
        seen = spread - step * rows >= start[0]
        keys.append(jnp.where(seen, pair[:, at], jnp.zeros((), jnp.bfloat16)))
        at = slice((kv_groups + group) * HD, (kv_groups + group + 1) * HD)
        key_sides.append(jnp.concatenate([keys[-1], ones], axis=1))
        value_sides.append(jnp.concatenate([pair[:, at], ones], axis=1))
    if causal:
        shape = (rows, rows)
        row_at = lax.broadcasted_iota(jnp.int32, shape, 0)
        col_at = lax.broadcasted_iota(jnp.int32, shape, 1)
        row_at = jnp.where(row_at < half, own_base + row_at, sib_base - half + row_at)
        col_at = jnp.where(col_at < half, own_base + col_at, sib_base - half + col_at)
        visible = (col_at <= row_at)[None]
    parts = 2 if count % 2 == 0 else 1
    size = count * rows // parts
    hashed = []
    for part in range(parts):
        at = pl.ds(part * size, size)
        grads = None
        for key, key_side, value_side in zip(keys, key_sides, value_sides):
            logits = dot_nt(q_at[at, :], key_side) * FACTOR
            weights = jnp.exp(jnp.minimum(logits, 1.0))
            if causal and key is keys[0]:
                weights = weights.reshape(count // parts, rows, rows)
                weights = jnp.where(visible, weights, 0.0).reshape(size, rows)
            scores = (weights * dot_nt(g_at[at, :], value_side)).astype(jnp.bfloat16)
            product = jnp.dot(scores, key, preferred_element_type=jnp.float32)
            grads = product if grads is None else grads + product
        grads = (grads * FACTOR).astype(jnp.bfloat16)
        hashed += [grads[low : low + rows] for low in range(0, size, rows)]
    hashed = jnp.concatenate(hashed, axis=1)
    total[...] += jnp.dot(hashed, tables[...], preferred_element_type=jnp.float32)


def first_kernel(place, start, q, q_sib, g, g_sib, stats, pair_in, *refs):
    total, q_all, g_all, tables, pair, sems, pair_sem = refs
    pair_copy = fetch([(pair_in, pair)], pair_sem)[0]
    core = place[0] % 2
    rows = total.shape[0]
    half = rows // 2
    kv_groups = pair.shape[1] // (2 * HD)
    heads = q_all.shape[0] // rows
    count = heads // kv_groups
    local_heads = stats.shape[1] // 5
    chips = stats.shape[0] // 2
    for group in range(kv_groups):
        for head in range(group * count, (group + 1) * count):
            column = pl.multiple_of((core * heads + head) * HD, HD)
            for which, (own, sib, out) in enumerate(((q, q_sib, q_all), (g, g_sib, g_all))):
                for source, low in ((own, head * rows), (sib, head * rows + half)):
                    pltpu.make_async_copy(
                        source.at[:, pl.ds(column, HD)],
                        out.at[pl.ds(low, half), pl.ds(0, HD)],
                        sems.at[group, which],
                    ).start()

    def stat_rows(which, group):
        found = []
        for head in range(group * count, (group + 1) * count):
            source, local = divmod(head, local_heads)
            row = which * local_heads + local
            found.append(stats[core * chips + source, row : row + 1, :])
        return jnp.concatenate(found, axis=0)

    total[...] = jnp.zeros_like(total)
    lane = lax.broadcasted_iota(jnp.int32, (half, LANES), 1)
    level = lax.broadcasted_iota(jnp.int32, (LANES, HD), 0)
    level = jnp.where(level < K2, level, level - K2).astype(jnp.float32)
    for group in range(kv_groups):
        for out, base, sign in ((q_all, 0, -1.0 / FACTOR), (g_all, 2, -1.0)):
            for side in range(2):
                terms = split_terms(stat_rows(base + side, group) * sign, STAT_TERMS)
                terms = jnp.concatenate([term.astype(jnp.float32) for term in terms], axis=0)
                fill = jnp.zeros((LANES - terms.shape[0], half), jnp.float32)
                columns = jnp.concatenate([terms, fill], axis=0).T
                for head in range(count):
                    chosen = jnp.where(lane % count == head, columns, 0.0)
                    low = (group * count + head) * rows + side * half
                    out[low : low + half, HD:] = chosen.astype(jnp.bfloat16)
        codes = stat_rows(4, group)
        for head in range(count):
            code = codes[head : head + 1]
            sign = jnp.where(code >= K2, -1.0, 1.0)
            bucket = jnp.where(code >= K2, code - K2, code)
            table = jnp.where(level == bucket, sign, 0.0)
            low = (group * count + head) * HD
            tables[low : low + HD, :] = table.T.astype(jnp.bfloat16)
    pair_copy.wait()
    for group in range(kv_groups):
        at = pl.ds(group * count * rows, count * rows)
        for which, out in enumerate((q_all, g_all)):
            side = out.at[at, pl.ds(0, HD)]
            pltpu.make_async_copy(side, side, sems.at[group, which]).wait()
        attend(
            place, start, q_all.at[at, :], g_all.at[at, :],
            tables.at[pl.ds(group * count * HD, count * HD), :],
            [pair], [0], True, group, kv_groups, total,
        )


def next_kernel(place, start, q_all, g_all, tables, before, pair, total, *, steps):
    rows = total.shape[0]
    kv_groups = pair.shape[1] // (2 * HD)
    size = q_all.shape[0] // kv_groups
    width = tables.shape[0] // kv_groups
    chip = place[0] // 2
    step = jnp.int32(NO_STEP)
    for at_chip, known in steps.items():
        step = jnp.where(chip == at_chip, known, step)
    total[...] = before[...]
    for group in range(kv_groups):
        at = pl.ds(group * size, size)
        attend(
            place, start, q_all.at[at, :], g_all.at[at, :],
            tables.at[pl.ds(group * width, width), :],
            [pair], [step], False, group, kv_groups, total,
        )


def last_kernel(
    place, start, q_all, g_all, tables, before, pair, hi_own, hi_sib, out, total, *, steps, scale
):
    next_kernel(place, start, q_all, g_all, tables, before, pair, total, steps=steps)
    hashed = jnp.concatenate([hi_own[...], hi_sib[...]], axis=0)
    both = sum(dot_tn(hashed, part) for part in split_terms(total[...], 2))
    half = K1 // 2
    lane = lax.broadcasted_iota(jnp.int32, (half, LANES), 1)
    sketch = jnp.where(lane < K2, both[:half], both[half:]) * scale
    parts, chunk = out.shape[1], out.shape[2]
    for part in range(parts):
        for doc in range(out.shape[0]):
            out[doc, part] = sketch[part * chunk : (part + 1) * chunk]


def score_kernel(place, recv_ref, stored_ref, own_ref, partial_ref, sums, flat, *, scale):
    docs, parts, chunk, _ = recv_ref.shape
    for doc in range(docs):
        sums[doc] = jnp.sum(recv_ref[doc], axis=0)
    for row in range(chunk):
        flat[:, row * LANES : (row + 1) * LANES] = sums[:, row, :]
        own_ref[:, row * LANES : (row + 1) * LANES] = sums[place[0], row : row + 1, :]
    pieces = split_terms(flat[...], 3)
    stacked = jnp.concatenate(pieces, axis=0)
    products = dot_nt(stacked, stored_ref[...])
    partial = (products[:docs] + products[docs : 2 * docs] + products[2 * docs :]) * scale
    if len(partial_ref.shape) == 3:
        for part in range(parts):
            partial_ref[part] = partial[:, part * LANES : (part + 1) * LANES]
    else:
        partial_ref[...] = partial


def local(
    queries,
    key_heads,
    value_heads,
    out_grad,
    log_sums,
    row_delta,
    doc_start,
    layer_input,
    hash_in,
    hash_out,
    query_sketch,
):
    ctx_count = lax.axis_size("ctx")
    docs = lax.axis_size("doc")
    chips = ctx_count // 2
    place = lax.axis_index("ctx").astype(jnp.int32).reshape(1)
    doc_place = lax.axis_index("doc").astype(jnp.int32).reshape(1)
    rows = queries.shape[1]
    seq_len = rows * ctx_count
    local_heads = log_sums.shape[1]
    core_heads = local_heads * chips
    kv_width = key_heads.shape[2]
    shape = jax.ShapeDtypeStruct
    params = lambda mib: pltpu.CompilerParams(vmem_limit_bytes=mib * MIB)

    def permute(array, target):
        pairs = [(i, target(i)) for i in range(ctx_count)]
        return lax.ppermute(array, "ctx", [pair for pair in pairs if pair[1] < ctx_count])

    swap = lambda array: permute(array, lambda i: i ^ 1)

    packed_shape = (ctx_count, 5 * local_heads, LANES)
    packed = pl.pallas_call(
        pack_kernel,
        out_shape=shape(packed_shape, jnp.float32),
        in_specs=[ANY] * 3,
        out_specs=VMEM,
        scratch_shapes=[
            pltpu.VMEM((local_heads, seq_len), jnp.float32),
            pltpu.VMEM((local_heads, seq_len), jnp.float32),
            pltpu.VMEM((local_heads, HD), jnp.int32),
            pltpu.SemaphoreType.DMA((3,)),
        ],
        compiler_params=params(60),
    )(log_sums[0], row_delta[0], hash_out.reshape(local_heads, HD))
    stats = lax.all_to_all(packed, "ctx", split_axis=0, concat_axis=0, tiled=True)
    half_shape = shape((rows, kv_width), jnp.bfloat16)
    mine, other = pl.pallas_call(
        prepare_kernel,
        out_shape=(half_shape, half_shape),
        in_specs=[SMEM, ANY, ANY],
        out_specs=(VMEM, VMEM),
        scratch_shapes=[pltpu.VMEM((rows, kv_width), jnp.bfloat16)] * 2
        + [pltpu.SemaphoreType.DMA((4,))],
        compiler_params=params(60),
    )(place, key_heads[0], value_heads[0])
    from_sib = swap(other)

    pair_shape = shape((2 * rows, kv_width), jnp.bfloat16)
    pair = pl.pallas_call(
        join_kernel,
        out_shape=pair_shape,
        in_specs=[ANY] * 3,
        out_specs=VMEM,
        scratch_shapes=[pltpu.SemaphoreType.DMA((2,))],
        compiler_params=params(16),
    )(mine, from_sib, stats)

    if chips == 4:
        plan = [
            [(0, 2, 2), (2, 3, 1)],
            [(1, 3, 2), (0, 1, 1)],
            [(2, 3, 3), (1, 2, 1)],
        ]
    else:
        plan = [
            [(chip, chip + 1, wave + 1) for chip in range(wave, chips - 1)]
            for wave in range(chips - 1)
        ]

    def send(block, wave):
        route = {low: high for low, high, _ in plan[wave]}
        return permute(block, lambda i: 2 * route.get(i // 2, chips) + i % 2)

    received = [send(pair, 0)]
    if chips == 4:
        received.append(send(pair, 1))
    q, g = queries[0], out_grad[0]
    q_sib, g_sib = swap(q), swap(g)


    stacked = shape((core_heads * 2 * rows, 2 * HD), jnp.bfloat16)
    table_shape = shape((core_heads * HD, LANES), jnp.bfloat16)
    total_shape = shape((2 * rows, LANES), jnp.float32)
    total, q_all, g_all, tables = pl.pallas_call(
        first_kernel,
        out_shape=(total_shape, stacked, stacked, table_shape),
        in_specs=[SMEM, SMEM, ANY, ANY, ANY, ANY, VMEM, ANY],
        out_specs=(VMEM, VMEM, VMEM, VMEM),
        scratch_shapes=[
            pltpu.VMEM((2 * rows, kv_width), jnp.bfloat16),
            pltpu.SemaphoreType.DMA((kv_width // (2 * HD), 2)),
            pltpu.SemaphoreType.DMA((1,)),
        ],
        compiler_params=params(24),
    )(place, doc_start, q, q_sib, g, g_sib, stats, pair)

    parts = max(1, layer_input.shape[2] // 1024)
    width = layer_input.shape[2] // parts
    hashed = pl.pallas_call(
        hash_kernel,
        out_shape=shape((rows, K1), jnp.bfloat16),
        in_specs=[ANY, ANY, ANY],
        out_specs=VMEM,
        scratch_shapes=[
            pltpu.VMEM((parts, rows, width), jnp.bfloat16),
            pltpu.VMEM((1, parts * width), jnp.int32),
            pltpu.SemaphoreType.DMA((1 + parts,)),
        ],
        compiler_params=params(16),
    )(layer_input[0], hash_in.reshape(1, -1), total)
    hashed_sib = swap(hashed)

    scale = (seq_len * layer_input.shape[2] // K1) ** -0.5
    chunk = K1 * K2 // LANES // ctx_count
    if chips == 4:
        relayed = pl.pallas_call(
            functools.partial(relay_kernel, relaying=[2]),
            out_shape=pair_shape,
            in_specs=[SMEM] + [ANY] * 3,
            out_specs=VMEM,
            scratch_shapes=[pltpu.SemaphoreType.DMA((1,))],
            compiler_params=params(16),
        )(place, pair, received[0], total)
        received.append(send(relayed, 2))
    for wave in range(len(received), len(plan)):
        received.append(send(received[-1], wave))

    for wave, block in enumerate(received):
        steps = {high: step for _, high, step in plan[wave]}
        last = wave == len(plan) - 1
        args = (place, doc_start, q_all, g_all, tables, total, block)
        if not last:
            total = pl.pallas_call(
                functools.partial(next_kernel, steps=steps),
                out_shape=total_shape,
                in_specs=[SMEM, SMEM] + [VMEM] * 5,
                out_specs=VMEM,
                compiler_params=params(24),
            )(*args)
            continue
        parts = pl.pallas_call(
            functools.partial(last_kernel, steps=steps, scale=scale),
            out_shape=shape((docs, ctx_count, chunk, LANES), jnp.float32),
            in_specs=[SMEM, SMEM] + [VMEM] * 7,
            out_specs=VMEM,
            scratch_shapes=[pltpu.VMEM((2 * rows, LANES), jnp.float32)],
            compiler_params=params(24),
        )(*args, hashed, hashed_sib)

    parts = parts.reshape(-1, chunk, LANES)
    parts = lax.all_to_all(parts, ("doc", "ctx"), split_axis=0, concat_axis=0, tiled=True)
    parts = parts.reshape(docs, ctx_count, chunk, LANES)
    stored = query_sketch.shape[0]
    wide = stored // ctx_count == LANES
    partial_shape = (ctx_count, docs, LANES) if wide else (docs, stored)
    local_sketch, partial = pl.pallas_call(
        functools.partial(score_kernel, scale=(K1 * K2) ** -0.5),
        out_shape=(
            shape((1, chunk * LANES), jnp.float32),
            shape(partial_shape, jnp.float32),
        ),
        in_specs=[SMEM, VMEM, VMEM],
        out_specs=(VMEM, VMEM),
        scratch_shapes=[
            pltpu.VMEM((docs, chunk, LANES), jnp.float32),
            pltpu.VMEM((docs, chunk * LANES), jnp.float32),
        ],
        compiler_params=params(16),
    )(doc_place, parts, query_sketch)
    if not wide:
        partial = partial.reshape(docs, ctx_count, -1).transpose(1, 0, 2)
    partial = lax.all_to_all(partial, "ctx", split_axis=0, concat_axis=0, tiled=True)
    return local_sketch, jnp.sum(partial, axis=0)


def solution(mesh):
    return jax.shard_map(
        local,
        mesh=mesh,
        in_specs=(
            P("doc", "ctx", None),
            P("doc", "ctx", None),
            P("doc", "ctx", None),
            P("doc", "ctx", None),
            P("doc", "ctx", None),
            P("doc", "ctx", None),
            P("doc"),
            P("doc", "ctx", None),
            P(),
            P("ctx"),
            P("doc", "ctx"),
        ),
        out_specs=(P("doc", "ctx"), P(None, ("doc", "ctx"))),
        check_vma=False,
    )
```

time: 224 us -> 63.6 us (0.28)
  waiting for transfers between devices: 86.2 us -> 12.3 us
  blocking collectives: 44.3 us -> 8 us
  matrix products: 32.9 us -> 0 us
  local copies, waits for them, and re-layouts: 26.7 us -> 3.36 us
  Pallas kernels: 0 us -> 18 us
  between operations: 14.7 us -> 1.47 us
  starting transfers between devices: 10.8 us -> 19.3 us
  other arithmetic: 7.84 us -> 0.59 us
    all_gather x2 -> x0, blocking collectives: 44.3 us -> none  [the longest x1 36.2 us: local(): hashed_all = lax.all_gather(hashed_local, 'ctx', axis=0, tiled=True)]
    dot_general x11 -> x0, matrix products: 28.8 us -> none  [the longest x4 15.3 us: local(): jnp.einsum('hqk,khd->qhd', grad_scores, key_rows, preferred_element_type=...]
    reduce_scatter x1 -> x0, waiting for transfers between devices: 28.6 us -> none  [local(): lax.psum_scatter(partial_sketch.astype(jnp.bfloat16), 'ctx', scatter_dime...]
    unnamed x5 -> x0, waiting for transfers between devices: 27.7 us -> none
    all_to_all x2, waiting for transfers between devices: 29.9 us -> 11.1 us  [the longest x1 8.17 us: local(): lax.all_to_all(parts, ('doc', 'ctx'), split_axis=0, concat_axis=0, tiled=...]
    pallas_call x0 -> x10, Pallas kernels: none -> 18 us  [the longest x2 4.49 us: local(): pl.pallas_call(functools.partial(next_kernel, steps=steps), out_shape=tot...]
    slice x11 -> x0, local copies, waits for them, and re-layouts: 8.95 us -> none  [the longest x5 4.54 us: local(): query_rows = query_part[low_row:high_row]]
    all_to_all x0 -> x1, blocking collectives: none -> 8 us  [local(): lax.all_to_all(partial, 'ctx', split_axis=0, concat_axis=0, tiled=True)]
  transfers between devices with their start and end apart: 6 -> 9, of which waited for: 3 -> 3; matrix products, arithmetic and copies ran while one was open for 11% -> 0% of each run, Pallas kernels for 0% -> 22%
where the time goes in v2:
time: 63.6 us; the launch traced here: 63 us
  starting transfers between devices  19.3 us (30%)
  Pallas kernels  18 us (28%)
  waiting for transfers between devices  12.3 us (19%)
  blocking collectives  8 us (13%)
  local copies, waits for them, and re-layouts  3.36 us (5%)
  between operations  1.47 us (2%)
    all_to_all x1, waiting for transfers between devices, local(): lax.all_to_all(parts, ('doc', 'ctx'), split_axis=0, concat_axis=0, tiled=...  8.17 us
    all_to_all x1, blocking collectives, local(): lax.all_to_all(partial, 'ctx', split_axis=0, concat_axis=0, tiled=True)  8 us
    all_to_all x1, starting transfers between devices, local(): lax.all_to_all(parts, ('doc', 'ctx'), split_axis=0, concat_axis=0, tiled=...  7.06 us
    all_to_all x1, starting transfers between devices, local(): lax.all_to_all(packed, 'ctx', split_axis=0, concat_axis=0, tiled=True)  6.31 us
    ppermute x7, starting transfers between devices, permute(): lax.ppermute(array, 'ctx', [pair for pair in pairs if pair[1] < ctx_count])  5.89 us
    pallas_call x2, Pallas kernels, local(): pl.pallas_call(functools.partial(next_kernel, steps=steps), out_shape=tot...  4.49 us
    pallas_call x1, Pallas kernels, local(): pl.pallas_call(first_kernel, out_shape=(total_shape, stacked, stacked, ta...  4.08 us
    unnamed x12, local copies, waits for them, and re-layouts  3.36 us
  transfers between devices with their start and end apart: 9, of which 3 were waited for; matrix products, arithmetic and copies ran while one was open for 0% of the time, Pallas kernels for 22%

profile of v2, /device:TPU:0, one launch (start us, length us, event | category | flops | bytes accessed | tf_op | source)
XLA Modules:
  0.0 63.0 jit_solution(7476943570439477611)
XLA Ops:
  0.6 0.5 collective-permute-start
  1.1 0.1 collective-permute-start.1
  1.2 1.4 %shard_map.122 = f32[8,20,128]{2,1,0:T(8,128)} custom-call(f32[4,1024]{1,0:T(4,128)} %bitcast.22, f32[4,1024]{1,0:T(4,128)} %bitcast.23, s32[4,128]{1,0:T(4,128)} %bitcast.24), custom_call_target="tpu_custom_call" | custom-call | tf_op jit(solution)/shard_map/pallas_call | solution.py:331
  2.6 6.3 %all-to-all-start = ((f32[8,20,128]{2,1,0:T(8,128)}), f32[8,20,128]{2,1,0:T(8,128)S(1)}, u32[]{:S(2)}, u32[]{:S(2)}) async-start(f32[8,20,128]{2,1,0:T(8,128)} %shard_map.122), calls=%async_computation | async-start | bytes 196608 | tf_op jit(solution)/shard_map/all_to_all | solution.py:344
  9.0 1.7 %shard_map.123 = (bf16[128,512]{1,0:T(8,128)(2,1)}, bf16[128,512]{1,0:T(8,128)(2,1)}) custom-call(s32[1]{0:T(128)} %bitcast.1.place, bf16[128,512]{1,0:T(8,128)(2,1)} %bitcast.20, bf16[128,512]{1,0:T(8,128)(2,1)} %bitcast.21), custom_call_target="tpu_custom_call" | custom-call | tf_op jit(solution)/shard_map/pallas_call | solution.py:346
  10.6 0.6 collective-permute-start.2
  11.2 1.2 %collective-permute-done.2.lower = bf16[128,512]{1,0:T(8,128)(2,1)S(1)} collective-permute-done((bf16[128,512]{1,0:T(8,128)(2,1)}, bf16[128,512]{1,0:T(8,128)(2,1)S(1)}, u32[]{:S(2)}, u32[]{:S(2)}) %collective-permute-start.2) | collective-permute-done | bytes 131104 | tf_op jit(solution)/shard_map/ppermute | solution.py:326
  12.4 2.9 %all-to-all-done._.stats = f32[8,20,128]{2,1,0:T(8,128)S(1)} async-done(((f32[8,20,128]{2,1,0:T(8,128)}), f32[8,20,128]{2,1,0:T(8,128)S(1)}, u32[]{:S(2)}, u32[]{:S(2)}) %all-to-all-start) | async-done | bytes 81952 | tf_op jit(solution)/shard_map/all_to_all | solution.py:344
  15.3 0.0 copy-start.4
  15.3 0.9 %copy-done.4 = bf16[128,512]{1,0:T(8,128)(2,1)S(1)} copy-done((bf16[128,512]{1,0:T(8,128)(2,1)S(1)}, bf16[128,512]{1,0:T(8,128)(2,1)}, u32[]{:S(2)}) %copy-start.4) | copy-done | bytes 131096
  16.2 0.3 shard_map.124.pair_in.pair
  16.5 2.4 %collective-permute-start.3 = (bf16[256,512]{1,0:T(8,128)(2,1)S(1)}, bf16[256,512]{1,0:T(8,128)(2,1)S(1)}, u32[]{:S(2)}, u32[]{:S(2)}) collective-permute-start(bf16[256,512]{1,0:T(8,128)(2,1)S(1)} %shard_map.124.pair_in.pair), channel_id=1, source_target_pairs={{0,4},{1,5},{4,6},{5,7},{8,12},{9,13},{12,14},{13,15},{16,20},{17,... | collective-permute-start | bytes 786440 | tf_op jit(solution)/shard_map/ppermute | solution.py:326
  19.5 0.0 copy-start.1
  19.6 1.4 %collective-permute-start.4 = (bf16[256,512]{1,0:T(8,128)(2,1)S(1)}, bf16[256,512]{1,0:T(8,128)(2,1)S(1)}, u32[]{:S(2)}, u32[]{:S(2)}) collective-permute-start(bf16[256,512]{1,0:T(8,128)(2,1)S(1)} %shard_map.124.pair_in.pair), channel_id=1, source_target_pairs={{0,2},{1,3},{2,6},{3,7},{8,10},{9,11},{10,14},{11,15},{16,18},{17,... | collective-permute-start | bytes 786440 | tf_op jit(solution)/shard_map/ppermute | solution.py:326
  21.0 0.0 collective-permute-done.q_sib
  21.0 0.0 collective-permute-done.1.g_sib
  21.0 0.0 copy-start.2
  21.0 1.2 %copy-done.2 = bf16[1,128,4096]{2,1,0:T(8,128)(2,1)S(1)} copy-done((bf16[1,128,4096]{2,1,0:T(8,128)(2,1)S(1)}, bf16[1,128,4096]{2,1,0:T(8,128)(2,1)}, u32[]{:S(2)}) %copy-start.2) | copy-done | bytes 1048600
  22.3 0.0 copy-start.3
  22.3 1.2 %copy-done.3 = bf16[1,128,4096]{2,1,0:T(8,128)(2,1)S(1)} copy-done((bf16[1,128,4096]{2,1,0:T(8,128)(2,1)S(1)}, bf16[1,128,4096]{2,1,0:T(8,128)(2,1)}, u32[]{:S(2)}) %copy-start.3) | copy-done | bytes 1048600
  23.5 0.0 copy-start.5
  23.5 4.1 %shard_map.125 = (f32[256,128]{1,0:T(8,128)S(1)}, bf16[4096,256]{1,0:T(8,128)(2,1)S(1)}, bf16[4096,256]{1,0:T(8,128)(2,1)S(1)}, bf16[2048,128]{1,0:T(8,128)(2,1)S(1)}) custom-call(s32[1]{0:T(128)} %bitcast.1.place, s32[1]{0:T(128)S(6)} %copy.13.start, bf16[128,4096]{1,0:T(8,128)(2,1)S(1)} %bitcast.15, bf16[128,4096]{1,0:T(8,128)(2,1)S(1)} %collective-permute-done.q_sib, ...), custom_call_target="tpu_custom_call" | custom-call | tf_op jit(solution)/shard_map/pallas_call | solution.py:393
  27.6 0.0 collective-permute-done.3.pair.received
  27.6 0.9 %collective-permute-start.5 = (bf16[256,512]{1,0:T(8,128)(2,1)S(1)}, bf16[256,512]{1,0:T(8,128)(2,1)S(1)}, u32[]{:S(2)}, u32[]{:S(2)}) collective-permute-start(bf16[256,512]{1,0:T(8,128)(2,1)S(1)} %shard_map.128), channel_id=1, source_target_pairs={{2,4},{3,5},{4,6},{5,7},{10,12},{11,13},{12,14},{13,15},{18,20},{1... | collective-permute-start | bytes 786440 | tf_op jit(solution)/shard_map/ppermute | solution.py:326
  28.5 0.0 copy-done.1
  28.5 0.0 copy-done.5
  28.5 1.8 %shard_map.129.hi_own = bf16[128,128]{1,0:T(8,128)(2,1)S(1)} custom-call(bf16[128,8192]{1,0:T(8,128)(2,1)S(1)} %bitcast.13, s32[1,8192]{1,0:T(1,128)S(1)} %bitcast.19, f32[256,128]{1,0:T(8,128)S(1)} %get-tuple-element.15.before._), custom_call_target="tpu_custom_call" | custom-call | tf_op jit(solution)/shard_map/pallas_call | solution.py:408
  30.3 0.1 collective-permute-start.6
  30.4 2.2 %shard_map.126.before = f32[256,128]{1,0:T(8,128)S(1)} custom-call(s32[1]{0:T(128)} %bitcast.1.place, s32[1]{0:T(128)S(6)} %copy.13.start, bf16[4096,256]{1,0:T(8,128)(2,1)S(1)} %get-tuple-element.12.q_all, bf16[4096,256]{1,0:T(8,128)(2,1)S(1)} %get-tuple-element.13.g_all, bf16[2048,128]{1,0:T(8,128)(2,1)S(1)} %get-tuple-element.14.tables, ...), custom_call_target="tpu_custom_call" | custom-call | tf_op jit(solution)/shard_map/pallas_call | solution.py:442
  32.7 0.0 collective-permute-done.4.pair
  32.7 2.2 %shard_map.127.before = f32[256,128]{1,0:T(8,128)S(1)} custom-call(s32[1]{0:T(128)} %bitcast.1.place, s32[1]{0:T(128)S(6)} %copy.13.start, bf16[4096,256]{1,0:T(8,128)(2,1)S(1)} %get-tuple-element.12.q_all, bf16[4096,256]{1,0:T(8,128)(2,1)S(1)} %get-tuple-element.13.g_all, bf16[2048,128]{1,0:T(8,128)(2,1)S(1)} %get-tuple-element.14.tables, ...), custom_call_target="tpu_custom_call" | custom-call | tf_op jit(solution)/shard_map/pallas_call | solution.py:442
  34.9 0.0 copy-start
  34.9 0.0 collective-permute-done.6.hi_sib
  34.9 0.0 collective-permute-done.5.pair
  35.0 3.1 %shard_map.130 = f32[4,8,8,128]{3,2,1,0:T(8,128)} custom-call(s32[1]{0:T(128)} %bitcast.1.place, s32[1]{0:T(128)S(6)} %copy.13.start, bf16[4096,256]{1,0:T(8,128)(2,1)S(1)} %get-tuple-element.12.q_all, bf16[4096,256]{1,0:T(8,128)(2,1)S(1)} %get-tuple-element.13.g_all, bf16[2048,128]{1,0:T(8,128)(2,1)S(1)} %get-tuple-element.14.tables, ...), custom_call_target="tpu_custom_call" | custom-call | tf_op jit(solution)/shard_map/pallas_call | solution.py:450
  38.0 7.1 %all-to-all-start.1 = ((f32[32,8,128]{2,1,0:T(8,128)}), f32[32,8,128]{2,1,0:T(8,128)S(1)}, u32[]{:S(2)}, u32[]{:S(2)}) async-start(f32[32,8,128]{2,1,0:T(8,128)} %bitcast.11), calls=%async_computation.1 | async-start | bytes 262144 | tf_op jit(solution)/shard_map/all_to_all | solution.py:460
  45.1 8.2 %all-to-all-done.1 = f32[32,8,128]{2,1,0:T(8,128)S(1)} async-done(((f32[32,8,128]{2,1,0:T(8,128)}), f32[32,8,128]{2,1,0:T(8,128)S(1)}, u32[]{:S(2)}, u32[]{:S(2)}) %all-to-all-start.1) | async-done | bytes 131104 | tf_op jit(solution)/shard_map/all_to_all | solution.py:460
  53.3 0.0 copy-done
  53.3 1.1 %shard_map.131 = (f32[1,1024]{1,0:T(1,128)}, f32[8,4,128]{2,1,0:T(4,128)S(1)}) custom-call(s32[1]{0:T(128)} %bitcast.place, f32[4,8,8,128]{3,2,1,0:T(8,128)S(1)} %bitcast.18, bf16[1024,1024]{1,0:T(8,128)(2,1)S(1)} %copy-done), custom_call_target="tpu_custom_call" | custom-call | tf_op jit(solution)/shard_map/pallas_call | solution.py:465
  54.4 8.0 %all_to_all.15 = f32[8,4,128]{2,1,0:T(4,128)S(1)} all-to-all(f32[8,4,128]{2,1,0:T(4,128)S(1)} %get-tuple-element.17), channel_id=1, replica_groups=mesh['doc'=4,'ctx'=8] {'ctx'}, dimensions={0} | all-to-all | bytes 32768 | tf_op jit(solution)/shard_map/all_to_all | solution.py:481
  62.4 0.6 reduce_sum.9
  (1 shorter events, 0.0 us)
Async XLA Ops:
  0.6 20.4 %collective-permute-start = (bf16[128,4096]{1,0:T(8,128)(2,1)}, bf16[128,4096]{1,0:T(8,128)(2,1)S(1)}, u32[]{:S(2)}, u32[]{:S(2)}) collective-permute-start(bf16[128,4096]{1,0:T(8,128)(2,1)} %bitcast.14), channel_id=1, source_target_pairs={{0,1},{1,0},{2,3},{3,2},{4,5},{5,4},{6,7},{7,6},{8,9},{9,8},{10,11... | collective-permute-start | bytes 3145736 | tf_op jit(solution)/shard_map/ppermute | solution.py:326
  1.1 19.9 %collective-permute-start.1 = (bf16[128,4096]{1,0:T(8,128)(2,1)}, bf16[128,4096]{1,0:T(8,128)(2,1)S(1)}, u32[]{:S(2)}, u32[]{:S(2)}) collective-permute-start(bf16[128,4096]{1,0:T(8,128)(2,1)} %bitcast.16), channel_id=1, source_target_pairs={{0,1},{1,0},{2,3},{3,2},{4,5},{5,4},{6,7},{7,6},{8,9},{9,8},{10,11... | collective-permute-start | bytes 3145736 | tf_op jit(solution)/shard_map/ppermute | solution.py:326
  2.6 12.7 %all-to-all-start = ((f32[8,20,128]{2,1,0:T(8,128)}), f32[8,20,128]{2,1,0:T(8,128)S(1)}, u32[]{:S(2)}, u32[]{:S(2)}) async-start(f32[8,20,128]{2,1,0:T(8,128)} %shard_map.122), calls=%async_computation | async-start | bytes 196608 | tf_op jit(solution)/shard_map/all_to_all | solution.py:344
  10.6 1.8 %collective-permute-start.2 = (bf16[128,512]{1,0:T(8,128)(2,1)}, bf16[128,512]{1,0:T(8,128)(2,1)S(1)}, u32[]{:S(2)}, u32[]{:S(2)}) collective-permute-start(bf16[128,512]{1,0:T(8,128)(2,1)} %get-tuple-element.11), channel_id=1, source_target_pairs={{0,1},{1,0},{2,3},{3,2},{4,5},{5,4},{6,7},{7,6},{8,9},{9,8},{10,11... | collective-permute-start | bytes 393224 | tf_op jit(solution)/shard_map/ppermute | solution.py:326
  15.3 0.9 %copy-start.4 = (bf16[128,512]{1,0:T(8,128)(2,1)S(1)}, bf16[128,512]{1,0:T(8,128)(2,1)}, u32[]{:S(2)}) copy-start(bf16[128,512]{1,0:T(8,128)(2,1)} %get-tuple-element.10.upper) | copy-start | bytes 393220
  16.5 11.0 %collective-permute-start.3 = (bf16[256,512]{1,0:T(8,128)(2,1)S(1)}, bf16[256,512]{1,0:T(8,128)(2,1)S(1)}, u32[]{:S(2)}, u32[]{:S(2)}) collective-permute-start(bf16[256,512]{1,0:T(8,128)(2,1)S(1)} %shard_map.124.pair_in.pair), channel_id=1, source_target_pairs={{0,4},{1,5},{4,6},{5,7},{8,12},{9,13},{12,14},{13,15},{16,20},{17,... | collective-permute-start | bytes 786440 | tf_op jit(solution)/shard_map/ppermute | solution.py:326
  19.5 9.0 %copy-start.1 = (bf16[1,128,8192]{2,1,0:T(8,128)(2,1)S(1)}, bf16[1,128,8192]{2,1,0:T(8,128)(2,1)}, u32[]{:S(2)}) copy-start(bf16[1,128,8192]{2,1,0:T(8,128)(2,1)} %param.18) | copy-start | bytes 6291460
  19.6 13.1 %collective-permute-start.4 = (bf16[256,512]{1,0:T(8,128)(2,1)S(1)}, bf16[256,512]{1,0:T(8,128)(2,1)S(1)}, u32[]{:S(2)}, u32[]{:S(2)}) collective-permute-start(bf16[256,512]{1,0:T(8,128)(2,1)S(1)} %shard_map.124.pair_in.pair), channel_id=1, source_target_pairs={{0,2},{1,3},{2,6},{3,7},{8,10},{9,11},{10,14},{11,15},{16,18},{17,... | collective-permute-start | bytes 786440 | tf_op jit(solution)/shard_map/ppermute | solution.py:326
  21.0 1.2 %copy-start.2 = (bf16[1,128,4096]{2,1,0:T(8,128)(2,1)S(1)}, bf16[1,128,4096]{2,1,0:T(8,128)(2,1)}, u32[]{:S(2)}) copy-start(bf16[1,128,4096]{2,1,0:T(8,128)(2,1)} %param.11) | copy-start | bytes 3145732
  22.3 1.2 %copy-start.3 = (bf16[1,128,4096]{2,1,0:T(8,128)(2,1)S(1)}, bf16[1,128,4096]{2,1,0:T(8,128)(2,1)}, u32[]{:S(2)}) copy-start(bf16[1,128,4096]{2,1,0:T(8,128)(2,1)} %param.14) | copy-start | bytes 3145732
  23.5 5.0 %copy-start.5 = (s32[8192]{0:T(1024)S(1)}, s32[8192]{0:T(1024)}, u32[]{:S(2)}) copy-start(s32[8192]{0:T(1024)} %param.19) | copy-start | bytes 98308
  27.6 7.3 %collective-permute-start.5 = (bf16[256,512]{1,0:T(8,128)(2,1)S(1)}, bf16[256,512]{1,0:T(8,128)(2,1)S(1)}, u32[]{:S(2)}, u32[]{:S(2)}) collective-permute-start(bf16[256,512]{1,0:T(8,128)(2,1)S(1)} %shard_map.128), channel_id=1, source_target_pairs={{2,4},{3,5},{4,6},{5,7},{10,12},{11,13},{12,14},{13,15},{18,20},{1... | collective-permute-start | bytes 786440 | tf_op jit(solution)/shard_map/ppermute | solution.py:326
  30.3 4.6 %collective-permute-start.6 = (bf16[128,128]{1,0:T(8,128)(2,1)S(1)}, bf16[128,128]{1,0:T(8,128)(2,1)S(1)}, u32[]{:S(2)}, u32[]{:S(2)}) collective-permute-start(bf16[128,128]{1,0:T(8,128)(2,1)S(1)} %shard_map.129.hi_own), channel_id=1, source_target_pairs={{0,1},{1,0},{2,3},{3,2},{4,5},{5,4},{6,7},{7,6},{8,9},{9,8},{10,11... | collective-permute-start | bytes 98312 | tf_op jit(solution)/shard_map/ppermute | solution.py:326
  34.9 18.4 %copy-start = (bf16[1024,1024]{1,0:T(8,128)(2,1)S(1)}, bf16[1024,1024]{1,0:T(8,128)(2,1)}, u32[]{:S(2)}) copy-start(bf16[1024,1024]{1,0:T(8,128)(2,1)} %stored_ref.1) | copy-start | bytes 6291460
  38.0 15.2 %all-to-all-start.1 = ((f32[32,8,128]{2,1,0:T(8,128)}), f32[32,8,128]{2,1,0:T(8,128)S(1)}, u32[]{:S(2)}, u32[]{:S(2)}) async-start(f32[32,8,128]{2,1,0:T(8,128)} %bitcast.11), calls=%async_computation.1 | async-start | bytes 262144 | tf_op jit(solution)/shard_map/all_to_all | solution.py:460

commit v3 on v2

--- a/solution.py
+++ b/solution.py
@@ -14,6 +14,7 @@
 FACTOR = HD**-0.5
 STAT_TERMS = 3
 NO_STEP = 1024
+GROUP = 8
 MIB = 1024 * 1024
 SMEM = pl.BlockSpec(memory_space=pltpu.SMEM)
 VMEM = pl.BlockSpec(memory_space=pltpu.VMEM)
@@ -66,7 +67,7 @@
         packed[target, 4 * heads :, :] = code_rows
 
 
-def prepare_kernel(place, key_in, value_in, mine, other, key, value, sems):
+def prepare_kernel(place, key_in, value_in, pair, other, key, value, mine, sems):
     rows = key.shape[0] // 2
     pieces = [pl.ds(low, rows) for low in (0, rows)]
     for copy in fetch(
@@ -89,15 +90,25 @@
             mine[:, :half], mine[:, half:] = key[:, near], value[:, near]
             other[:, :half], other[:, half:] = key[:, far], value[:, far]
 
-
-def join_kernel(upper, lower, _, out, sems):
-    rows = upper.shape[0]
-    targets = (out.at[pl.ds(0, rows), :], out.at[pl.ds(rows, rows), :])
-    for copy in fetch(zip((upper, lower), targets), sems):
+    for copy in fetch([(mine, pair.at[pl.ds(0, mine.shape[0]), :])], sems):
         copy.wait()
 
 
-def hash_kernel(rows_in, codes_in, _, out, rows, codes, sems):
+def join_kernel(_, lower, __, pair, *refs):
+    parts, sems = refs[:-1], refs[-1]
+    rows = lower.shape[0]
+    copies = [(lower, pair.at[pl.ds(rows, rows), :])]
+    for group, part in enumerate(parts):
+        for half in range(2):
+            at = pl.ds((half * len(parts) + group) * HD, HD)
+            to = pl.ds(half * HD, HD)
+            copies.append((pair.at[pl.ds(0, rows), at], part.at[pl.ds(0, rows), to]))
+            copies.append((lower.at[:, at], part.at[pl.ds(rows, rows), to]))
+    for copy in fetch(copies, sems):
+        copy.wait()
+
+
+def hash_kernel(rows_in, codes_in, out, rows, codes, sems):
     count, _, width = rows.shape
     pairs = [(codes_in, codes)]
     for part in range(count):
@@ -117,20 +128,7 @@
     out[...] = total.astype(out.dtype)
 
 
-def relay_kernel(place, pair, received, _, out, sems, *, relaying):
-    chip = place[0] // 2
-    passing = functools.reduce(jnp.logical_or, [chip == which for which in relaying])
-
-    @pl.when(passing)
-    def _():
-        fetch([(received, out)], sems)[0].wait()
-
-    @pl.when(jnp.logical_not(passing))
-    def _():
-        fetch([(pair, out)], sems)[0].wait()
-
-
-def attend(place, start, q_at, g_at, tables, pairs, steps, causal, group, kv_groups, total):
+def attend(place, start, q_at, g_at, tables, blocks, steps, causal, total):
     core = place[0] % 2
     rows = total.shape[0]
     half = rows // 2
@@ -142,13 +140,11 @@
     lane = lax.broadcasted_iota(jnp.int32, (rows, LANES), 1)
     ones = jnp.where(lane < STAT_TERMS * count, 1.0, 0.0).astype(jnp.bfloat16)
     keys, key_sides, value_sides = [], [], []
-    for pair, step in zip(pairs, steps):
-        at = slice(group * HD, (group + 1) * HD)
+    for block, step in zip(blocks, steps):
         seen = spread - step * rows >= start[0]
-        keys.append(jnp.where(seen, pair[:, at], jnp.zeros((), jnp.bfloat16)))
-        at = slice((kv_groups + group) * HD, (kv_groups + group + 1) * HD)
+        keys.append(jnp.where(seen, block[:, :HD], jnp.zeros((), jnp.bfloat16)))
         key_sides.append(jnp.concatenate([keys[-1], ones], axis=1))
-        value_sides.append(jnp.concatenate([pair[:, at], ones], axis=1))
+        value_sides.append(jnp.concatenate([block[:, HD:], ones], axis=1))
     if causal:
         shape = (rows, rows)
         row_at = lax.broadcasted_iota(jnp.int32, shape, 0)
@@ -231,6 +227,11 @@
             low = (group * count + head) * HD
             tables[low : low + HD, :] = table.T.astype(jnp.bfloat16)
     pair_copy.wait()
+
+    def own_block(group):
+        key, value = (pair[:, at * HD : (at + 1) * HD] for at in (group, kv_groups + group))
+        return jnp.concatenate([key, value], axis=1)
+
     for group in range(kv_groups):
         at = pl.ds(group * count * rows, count * rows)
         for which, out in enumerate((q_all, g_all)):
@@ -239,38 +240,55 @@
         attend(
             place, start, q_all.at[at, :], g_all.at[at, :],
             tables.at[pl.ds(group * count * HD, count * HD), :],
-            [pair], [0], True, group, kv_groups, total,
+            [own_block(group)], [0], True, total,
         )
 
 
-def next_kernel(place, start, q_all, g_all, tables, before, pair, total, *, steps):
+def next_kernel(place, start, q_all, g_all, tables, before, *refs, steps, picked):
+    blocks, total = refs[:-1], refs[-1]
     rows = total.shape[0]
-    kv_groups = pair.shape[1] // (2 * HD)
+    kv_groups = tables.shape[0] // HD // GROUP
     size = q_all.shape[0] // kv_groups
     width = tables.shape[0] // kv_groups
     chip = place[0] // 2
+
+    def block_of(group):
+        halves = [block for block in blocks if block.shape[1] == 2 * HD]
+        wholes = [block for block in blocks if block.shape[1] != 2 * HD]
+        found = [halves[picked.index(group)][...]] if halves else []
+        if wholes:
+            key, value = (
+                wholes[0][:, at * HD : (at + 1) * HD] for at in (group, kv_groups + group)
+            )
+            found.append(jnp.concatenate([key, value], axis=1))
+        return found[0] if len(found) == 1 else jnp.where(chip == max(steps), *found)
+
     step = jnp.int32(NO_STEP)
     for at_chip, known in steps.items():
         step = jnp.where(chip == at_chip, known, step)
     total[...] = before[...]
-    for group in range(kv_groups):
-        at = pl.ds(group * size, size)
-        attend(
-            place, start, q_all.at[at, :], g_all.at[at, :],
-            tables.at[pl.ds(group * width, width), :],
-            [pair], [step], False, group, kv_groups, total,
-        )
+
+    @pl.when(step < NO_STEP)
+    def _():
+        for group in picked:
+            at = pl.ds(group * size, size)
+            attend(
+                place, start, q_all.at[at, :], g_all.at[at, :],
+                tables.at[pl.ds(group * width, width), :],
+                [block_of(group)], [step], False, total,
+            )
 
 
 def last_kernel(
-    place, start, q_all, g_all, tables, before, pair, hi_own, hi_sib, out, total, *, steps, scale
+    place, start, q_all, g_all, tables, before, hi_own, hi_sib, *refs, steps, picked, scale
 ):
-    next_kernel(place, start, q_all, g_all, tables, before, pair, total, steps=steps)
+    blocks, out, total = refs[:-2], refs[-2], refs[-1]
+    next_kernel(place, start, q_all, g_all, tables, before, *blocks, total, steps=steps, picked=picked)
     hashed = jnp.concatenate([hi_own[...], hi_sib[...]], axis=0)
     both = sum(dot_tn(hashed, part) for part in split_terms(total[...], 2))
     half = K1 // 2
     lane = lax.broadcasted_iota(jnp.int32, (half, LANES), 1)
-    sketch = jnp.where(lane < K2, both[:half], both[half:]) * scale
+    sketch = (jnp.where(lane < K2, both[:half], both[half:]) * scale).astype(out.dtype)
     parts, chunk = out.shape[1], out.shape[2]
     for part in range(parts):
         for doc in range(out.shape[0]):
@@ -280,7 +298,7 @@
 def score_kernel(place, recv_ref, stored_ref, own_ref, partial_ref, sums, flat, *, scale):
     docs, parts, chunk, _ = recv_ref.shape
     for doc in range(docs):
-        sums[doc] = jnp.sum(recv_ref[doc], axis=0)
+        sums[doc] = jnp.sum(recv_ref[doc].astype(jnp.float32), axis=0)
     for row in range(chunk):
         flat[:, row * LANES : (row + 1) * LANES] = sums[:, row, :]
         own_ref[:, row * LANES : (row + 1) * LANES] = sums[place[0], row : row + 1, :]
@@ -327,10 +345,15 @@
 
     swap = lambda array: permute(array, lambda i: i ^ 1)
 
-    packed_shape = (ctx_count, 5 * local_heads, LANES)
+    def pin(*arrays):
+        return [pltpu.with_memory_space_constraint(array, pltpu.HBM) for array in arrays]
+
+    def after(arrays, *done):
+        return lax.optimization_barrier((tuple(arrays), done))[0]
+
     packed = pl.pallas_call(
         pack_kernel,
-        out_shape=shape(packed_shape, jnp.float32),
+        out_shape=shape((ctx_count, 5 * local_heads, LANES), jnp.float32),
         in_specs=[ANY] * 3,
         out_specs=VMEM,
         scratch_shapes=[
@@ -339,32 +362,40 @@
             pltpu.VMEM((local_heads, HD), jnp.int32),
             pltpu.SemaphoreType.DMA((3,)),
         ],
-        compiler_params=params(60),
-    )(log_sums[0], row_delta[0], hash_out.reshape(local_heads, HD))
+        compiler_params=params(16),
+    )(*pin(log_sums[0], row_delta[0], hash_out.reshape(local_heads, HD)))
     stats = lax.all_to_all(packed, "ctx", split_axis=0, concat_axis=0, tiled=True)
+
+    q, g = queries[0], out_grad[0]
+    q_sib, g_sib = (swap(array) for array in after((q, g), packed))
+
     half_shape = shape((rows, kv_width), jnp.bfloat16)
-    mine, other = pl.pallas_call(
+    pair_shape = shape((2 * rows, kv_width), jnp.bfloat16)
+    pair, other = pl.pallas_call(
         prepare_kernel,
-        out_shape=(half_shape, half_shape),
+        out_shape=(pair_shape, half_shape),
         in_specs=[SMEM, ANY, ANY],
-        out_specs=(VMEM, VMEM),
-        scratch_shapes=[pltpu.VMEM((rows, kv_width), jnp.bfloat16)] * 2
+        out_specs=(ANY, VMEM),
+        scratch_shapes=[pltpu.VMEM((rows, kv_width), jnp.bfloat16)] * 3
         + [pltpu.SemaphoreType.DMA((4,))],
-        compiler_params=params(60),
-    )(place, key_heads[0], value_heads[0])
+        compiler_params=params(16),
+    )(place, *pin(key_heads[0], value_heads[0]))
     from_sib = swap(other)
 
-    pair_shape = shape((2 * rows, kv_width), jnp.bfloat16)
-    pair = pl.pallas_call(
+    groups = kv_width // (2 * HD)
+    part_shape = shape((2 * rows, 2 * HD), jnp.bfloat16)
+    pair, *halves = pl.pallas_call(
         join_kernel,
-        out_shape=pair_shape,
-        in_specs=[ANY] * 3,
-        out_specs=VMEM,
-        scratch_shapes=[pltpu.SemaphoreType.DMA((2,))],
+        out_shape=(pair_shape,) + (part_shape,) * groups,
+        in_specs=[ANY, ANY, SMEM],
+        out_specs=(ANY,) + (VMEM,) * groups,
+        input_output_aliases={0: 0},
+        scratch_shapes=[pltpu.SemaphoreType.DMA((1 + 4 * groups,))],
         compiler_params=params(16),
-    )(mine, from_sib, stats)
-
-    if chips == 4:
+    )(*after((pair, from_sib), stats), doc_start)
+
+    four = chips == 4
+    if four:
         plan = [
             [(0, 2, 2), (2, 3, 1)],
             [(1, 3, 2), (0, 1, 1)],
@@ -376,16 +407,13 @@
             for wave in range(chips - 1)
         ]
 
-    def send(block, wave):
-        route = {low: high for low, high, _ in plan[wave]}
+    def send(block, routes):
+        route = {low: high for low, high, _ in routes}
         return permute(block, lambda i: 2 * route.get(i // 2, chips) + i % 2)
 
-    received = [send(pair, 0)]
-    if chips == 4:
-        received.append(send(pair, 1))
-    q, g = queries[0], out_grad[0]
-    q_sib, g_sib = swap(q), swap(g)
-
+    received = [[send(half, plan[0]) for half in halves] if four else [send(pair, plan[0])]]
+    if four:
+        received.append([send(pair, plan[1])])
 
     stacked = shape((core_heads * 2 * rows, 2 * HD), jnp.bfloat16)
     table_shape = shape((core_heads * HD, LANES), jnp.bfloat16)
@@ -401,14 +429,14 @@
             pltpu.SemaphoreType.DMA((1,)),
         ],
         compiler_params=params(24),
-    )(place, doc_start, q, q_sib, g, g_sib, stats, pair)
+    )(place, doc_start, *pin(q), q_sib, *pin(g), g_sib, stats, pair)
 
     parts = max(1, layer_input.shape[2] // 1024)
     width = layer_input.shape[2] // parts
     hashed = pl.pallas_call(
         hash_kernel,
         out_shape=shape((rows, K1), jnp.bfloat16),
-        in_specs=[ANY, ANY, ANY],
+        in_specs=[ANY, ANY],
         out_specs=VMEM,
         scratch_shapes=[
             pltpu.VMEM((parts, rows, width), jnp.bfloat16),
@@ -416,45 +444,47 @@
             pltpu.SemaphoreType.DMA((1 + parts,)),
         ],
         compiler_params=params(16),
-    )(layer_input[0], hash_in.reshape(1, -1), total)
+    )(*after((layer_input[0], hash_in.reshape(1, -1)), total))
     hashed_sib = swap(hashed)
+
+    if four:
+        passed = after(received[0], total)
+        (own,) = after((pair,), total, received[0][0])
+        received.append([send(half, plan[2][:1]) for half in passed])
+        received[-1].append(send(own, plan[2][1:]))
+    for wave in range(len(received), len(plan)):
+        received.append([send(received[-1][0], plan[wave])])
 
     scale = (seq_len * layer_input.shape[2] // K1) ** -0.5
     chunk = K1 * K2 // LANES // ctx_count
-    if chips == 4:
-        relayed = pl.pallas_call(
-            functools.partial(relay_kernel, relaying=[2]),
-            out_shape=pair_shape,
-            in_specs=[SMEM] + [ANY] * 3,
-            out_specs=VMEM,
-            scratch_shapes=[pltpu.SemaphoreType.DMA((1,))],
-            compiler_params=params(16),
-        )(place, pair, received[0], total)
-        received.append(send(relayed, 2))
-    for wave in range(len(received), len(plan)):
-        received.append(send(received[-1], wave))
-
-    for wave, block in enumerate(received):
+    tiles = [
+        (wave, range(groups), blocks) for wave, blocks in enumerate(received) if len(blocks) < 3
+    ]
+    if four:
+        *halves, own = received[-1]
+        tiles += [(2, [group], [half, own]) for group, half in enumerate(halves)]
+    for wave, picked, blocks in tiles:
+        last = blocks is tiles[-1][2]
         steps = {high: step for _, high, step in plan[wave]}
-        last = wave == len(plan) - 1
-        args = (place, doc_start, q_all, g_all, tables, total, block)
+        given = dict(steps=steps, picked=list(picked))
+        args = (place, doc_start, q_all, g_all, tables, total)
         if not last:
             total = pl.pallas_call(
-                functools.partial(next_kernel, steps=steps),
+                functools.partial(next_kernel, **given),
                 out_shape=total_shape,
-                in_specs=[SMEM, SMEM] + [VMEM] * 5,
+                in_specs=[SMEM, SMEM] + [VMEM] * (4 + len(blocks)),
                 out_specs=VMEM,
                 compiler_params=params(24),
-            )(*args)
+            )(*args, *blocks)
             continue
         parts = pl.pallas_call(
-            functools.partial(last_kernel, steps=steps, scale=scale),
-            out_shape=shape((docs, ctx_count, chunk, LANES), jnp.float32),
-            in_specs=[SMEM, SMEM] + [VMEM] * 7,
+            functools.partial(last_kernel, scale=scale, **given),
+            out_shape=shape((docs, ctx_count, chunk, LANES), jnp.bfloat16),
+            in_specs=[SMEM, SMEM] + [VMEM] * (6 + len(blocks)),
             out_specs=VMEM,
             scratch_shapes=[pltpu.VMEM((2 * rows, LANES), jnp.float32)],
             compiler_params=params(24),
-        )(*args, hashed, hashed_sib)
+        )(*args, hashed, hashed_sib, *blocks)
 
     parts = parts.reshape(-1, chunk, LANES)
     parts = lax.all_to_all(parts, ("doc", "ctx"), split_axis=0, concat_axis=0, tiled=True)

time: 63.6 us -> 61.4 us (0.965)
  starting transfers between devices: 19.3 us -> 27.7 us
  Pallas kernels: 18 us -> 10.6 us
  local copies, waits for them, and re-layouts: 3.36 us -> 0.02 us
    pallas_call x7, Pallas kernels: 11 us -> 3.78 us  [the longest x1 1.42 us: local(): pl.pallas_call(pack_kernel, out_shape=shape((ctx_count, 5 * local_heads,...]
    ppermute x7 -> x10, starting transfers between devices: 5.89 us -> 10.2 us  [permute(): lax.ppermute(array, 'ctx', [pair for pair in pairs if pair[1] < ctx_count])]
    all_to_all x1, starting transfers between devices: 7.06 us -> 11.2 us  [local(): lax.all_to_all(parts, ('doc', 'ctx'), split_axis=0, concat_axis=0, tiled=...]
    unnamed x12 -> x6, local copies, waits for them, and re-layouts: 3.36 us -> 0.02 us
    all_to_all x1, waiting for transfers between devices: 8.17 us -> 7.38 us  [local(): lax.all_to_all(parts, ('doc', 'ctx'), split_axis=0, concat_axis=0, tiled=...]
    all_to_all x1, waiting for transfers between devices: 2.89 us -> 3.63 us  [local(): lax.all_to_all(packed, 'ctx', split_axis=0, concat_axis=0, tiled=True)]
    ppermute x7 -> x10, waiting for transfers between devices: 1.21 us -> 1.42 us  [permute(): lax.ppermute(array, 'ctx', [pair for pair in pairs if pair[1] < ctx_count])]
  transfers between devices with their start and end apart: 9 -> 12, of which waited for: 3 -> 4; matrix products, arithmetic and copies ran while one was open for 0% -> 0% of each run, Pallas kernels for 22% -> 12%
where the time goes in v3:
time: 61.4 us; the launch traced here: 60.8 us
  starting transfers between devices  27.7 us (45%)
  waiting for transfers between devices  12.4 us (20%)
  Pallas kernels  10.6 us (17%)
  blocking collectives  8 us (13%)
  between operations  1.51 us (2%)
    all_to_all x1, starting transfers between devices, local(): lax.all_to_all(parts, ('doc', 'ctx'), split_axis=0, concat_axis=0, tiled=...  11.2 us
    ppermute x10, starting transfers between devices, permute(): lax.ppermute(array, 'ctx', [pair for pair in pairs if pair[1] < ctx_count])  10.2 us
    all_to_all x1, blocking collectives, local(): lax.all_to_all(partial, 'ctx', split_axis=0, concat_axis=0, tiled=True)  8 us
    all_to_all x1, waiting for transfers between devices, local(): lax.all_to_all(parts, ('doc', 'ctx'), split_axis=0, concat_axis=0, tiled=...  7.38 us
    all_to_all x1, starting transfers between devices, local(): lax.all_to_all(packed, 'ctx', split_axis=0, concat_axis=0, tiled=True)  6.3 us
    pallas_call x1, Pallas kernels, local(): pl.pallas_call(first_kernel, out_shape=(total_shape, stacked, stacked, ta...  3.84 us
    all_to_all x1, waiting for transfers between devices, local(): lax.all_to_all(packed, 'ctx', split_axis=0, concat_axis=0, tiled=True)  3.63 us
    pallas_call x1, Pallas kernels, local(): pl.pallas_call(hash_kernel, out_shape=shape((rows, K1), jnp.bfloat16), in...  1.8 us
  transfers between devices with their start and end apart: 12, of which 4 were waited for; matrix products, arithmetic and copies ran while one was open for 0% of the time, Pallas kernels for 12%

profile of v3, /device:TPU:0, one launch (start us, length us, event | category | flops | bytes accessed | tf_op | source)
XLA Modules:
  0.0 60.8 jit_solution(6027211737573102333)
XLA Ops:
  0.6 1.4 %shard_map.122 = f32[8,20,128]{2,1,0:T(8,128)} custom-call(f32[4,1024]{1,0:T(4,128)} %bitcast.22, f32[4,1024]{1,0:T(4,128)} %bitcast.23, s32[4,128]{1,0:T(4,128)} %bitcast.24), custom_call_target="tpu_custom_call" | custom-call | tf_op jit(solution)/shard_map/pallas_call | solution.py:354
  2.1 0.5 collective-permute-start
  2.6 0.1 collective-permute-start.1
  2.7 6.3 %all-to-all-start = ((f32[8,20,128]{2,1,0:T(8,128)}), f32[8,20,128]{2,1,0:T(8,128)S(1)}, u32[]{:S(2)}, u32[]{:S(2)}) async-start(f32[8,20,128]{2,1,0:T(8,128)} %shard_map.122), calls=%async_computation | async-start | bytes 196608 | tf_op jit(solution)/shard_map/all_to_all | solution.py:367
  9.0 1.2 %shard_map.123 = (bf16[256,512]{1,0:T(8,128)(2,1)S(1)}, bf16[128,512]{1,0:T(8,128)(2,1)S(1)}) custom-call(s32[1]{0:T(128)} %bitcast.1.place, bf16[128,512]{1,0:T(8,128)(2,1)} %bitcast.20, bf16[128,512]{1,0:T(8,128)(2,1)} %bitcast.21), custom_call_target="tpu_custom_call" | custom-call | tf_op jit(solution)/shard_map/pallas_call | solution.py:374
  10.1 0.6 collective-permute-start.2
  11.3 0.3 collective-permute-done.2.lower
  11.7 3.6 %all-to-all-done.stats = f32[8,20,128]{2,1,0:T(8,128)S(1)} async-done(((f32[8,20,128]{2,1,0:T(8,128)}), f32[8,20,128]{2,1,0:T(8,128)S(1)}, u32[]{:S(2)}, u32[]{:S(2)}) %all-to-all-start) | async-done | bytes 81952 | tf_op jit(solution)/shard_map/all_to_all | solution.py:367
  15.3 0.3 shard_map.124
  15.6 2.3 %collective-permute-start.3 = (bf16[256,256]{1,0:T(8,128)(2,1)S(1)}, bf16[256,256]{1,0:T(8,128)(2,1)S(1)}, u32[]{:S(2)}, u32[]{:S(2)}) collective-permute-start(bf16[256,256]{1,0:T(8,128)(2,1)S(1)} %get-tuple-element.33), channel_id=1, source_target_pairs={{0,4},{1,5},{4,6},{5,7},{8,12},{9,13},{12,14},{13,15},{16,20},{17,... | collective-permute-start | bytes 393224 | tf_op jit(solution)/shard_map/ppermute | solution.py:344
  17.9 3.2 %collective-permute-start.4 = (bf16[256,256]{1,0:T(8,128)(2,1)S(1)}, bf16[256,256]{1,0:T(8,128)(2,1)S(1)}, u32[]{:S(2)}, u32[]{:S(2)}) collective-permute-start(bf16[256,256]{1,0:T(8,128)(2,1)S(1)} %get-tuple-element.34), channel_id=1, source_target_pairs={{0,4},{1,5},{4,6},{5,7},{8,12},{9,13},{12,14},{13,15},{16,20},{17,... | collective-permute-start | bytes 393224 | tf_op jit(solution)/shard_map/ppermute | solution.py:344
  21.1 0.0 copy-start.1
  21.2 0.0 copy-start.2
  21.2 1.4 %collective-permute-start.5 = (bf16[256,512]{1,0:T(8,128)(2,1)S(1)}, bf16[256,512]{1,0:T(8,128)(2,1)S(1)}, u32[]{:S(2)}, u32[]{:S(2)}) collective-permute-start(bf16[256,512]{1,0:T(8,128)(2,1)S(1)} %get-tuple-element.36.pair_in), channel_id=1, source_target_pairs={{0,2},{1,3},{2,6},{3,7},{8,10},{9,11},{10,14},{11,15},{16,18},{17,... | collective-permute-start | bytes 786440 | tf_op jit(solution)/shard_map/ppermute | solution.py:344
  22.6 0.0 collective-permute-done.q_sib
  22.6 0.0 collective-permute-done.1.g_sib
  22.6 3.8 %shard_map.125 = (f32[256,128]{1,0:T(8,128)S(1)}, bf16[4096,256]{1,0:T(8,128)(2,1)S(1)}, bf16[4096,256]{1,0:T(8,128)(2,1)S(1)}, bf16[2048,128]{1,0:T(8,128)(2,1)S(1)}) custom-call(s32[1]{0:T(128)} %bitcast.1.place, s32[1]{0:T(128)S(6)} %copy.15.__.start, bf16[128,4096]{1,0:T(8,128)(2,1)} %bitcast.17, bf16[128,4096]{1,0:T(8,128)(2,1)S(1)} %collective-permute-done.q_sib, ...), custom_call_target="tpu_custom_call" | custom-call | tf_op jit(solution)/shard_map/pallas_call | solution.py:421
  26.5 0.0 collective-permute-done.3.refs_0_
  26.5 0.7 %collective-permute-start.7 = (bf16[256,512]{1,0:T(8,128)(2,1)S(1)}, bf16[256,512]{1,0:T(8,128)(2,1)S(1)}, u32[]{:S(2)}, u32[]{:S(2)}) collective-permute-start(bf16[256,512]{1,0:T(8,128)(2,1)S(1)} %get-tuple-element.36.pair_in), channel_id=1, source_target_pairs={{2,4},{3,5},{10,12},{11,13},{18,20},{19,21},{26,28},{27,29}} | collective-permute-start | bytes 786440 | tf_op jit(solution)/shard_map/ppermute | solution.py:344
  27.2 0.0 collective-permute-done.4.refs_1_
  27.2 0.7 %collective-permute-start.6 = (bf16[256,256]{1,0:T(8,128)(2,1)S(1)}, bf16[256,256]{1,0:T(8,128)(2,1)S(1)}, u32[]{:S(2)}, u32[]{:S(2)}) collective-permute-start(bf16[256,256]{1,0:T(8,128)(2,1)S(1)} %collective-permute-done.3.refs_0_), channel_id=1, source_target_pairs={{4,6},{5,7},{12,14},{13,15},{20,22},{21,23},{28,30},{29,31}} | collective-permute-start | bytes 393224 | tf_op jit(solution)/shard_map/ppermute | solution.py:344
  27.9 0.7 %collective-permute-start.9 = (bf16[256,256]{1,0:T(8,128)(2,1)S(1)}, bf16[256,256]{1,0:T(8,128)(2,1)S(1)}, u32[]{:S(2)}, u32[]{:S(2)}) collective-permute-start(bf16[256,256]{1,0:T(8,128)(2,1)S(1)} %collective-permute-done.4.refs_1_), channel_id=1, source_target_pairs={{4,6},{5,7},{12,14},{13,15},{20,22},{21,23},{28,30},{29,31}} | collective-permute-start | bytes 393224 | tf_op jit(solution)/shard_map/ppermute | solution.py:344
  28.5 0.0 copy-done.1
  28.6 0.0 copy-done.2
  28.6 1.8 %shard_map.129.hi_own = bf16[128,128]{1,0:T(8,128)(2,1)S(1)} custom-call(bf16[128,8192]{1,0:T(8,128)(2,1)S(1)} %bitcast.13, s32[1,8192]{1,0:T(1,128)S(1)} %bitcast.15), custom_call_target="tpu_custom_call" | custom-call | tf_op jit(solution)/shard_map/pallas_call | solution.py:436
  30.4 0.1 collective-permute-start.8
  30.5 0.0 collective-permute-done.5.refs_0_
  30.5 0.0 collective-permute-done.6.refs_0_
  30.5 0.0 collective-permute-done.7.refs_1_
  30.6 0.0 copy-start
  30.6 1.1 %collective-permute-done.8.hi_sib = bf16[128,128]{1,0:T(8,128)(2,1)S(1)} collective-permute-done((bf16[128,128]{1,0:T(8,128)(2,1)S(1)}, bf16[128,128]{1,0:T(8,128)(2,1)S(1)}, u32[]{:S(2)}, u32[]{:S(2)}) %collective-permute-start.8) | collective-permute-done | bytes 32800 | tf_op jit(solution)/shard_map/ppermute | solution.py:344
  31.6 0.0 collective-permute-done.9.refs_0_
  31.6 0.9 %shard_map.130 = bf16[4,8,8,128]{3,2,1,0:T(8,128)(2,1)} custom-call(s32[1]{0:T(128)} %bitcast.1.place, s32[1]{0:T(128)S(6)} %copy.15.__.start, bf16[4096,256]{1,0:T(8,128)(2,1)S(1)} %get-tuple-element.29.q_all, bf16[4096,256]{1,0:T(8,128)(2,1)S(1)} %get-tuple-element.30.g_all, bf16[2048,128]{1,0:T(8,128)(2,1)S(1)} %get-tuple-element.31.tables, ...), custom_call_target="tpu_custom_call" | custom-call | tf_op jit(solution)/shard_map/pallas_call | solution.py:480
  32.5 11.2 %all-to-all-start.1 = ((bf16[32,8,128]{2,1,0:T(8,128)(2,1)}), bf16[32,8,128]{2,1,0:T(8,128)(2,1)S(1)}, u32[]{:S(2)}, u32[]{:S(2)}) async-start(bf16[32,8,128]{2,1,0:T(8,128)(2,1)} %bitcast.11), calls=%async_computation.1 | async-start | bytes 131072 | tf_op jit(solution)/shard_map/all_to_all | solution.py:490
  43.7 7.4 %all-to-all-done.1 = bf16[32,8,128]{2,1,0:T(8,128)(2,1)S(1)} async-done(((bf16[32,8,128]{2,1,0:T(8,128)(2,1)}), bf16[32,8,128]{2,1,0:T(8,128)(2,1)S(1)}, u32[]{:S(2)}, u32[]{:S(2)}) %all-to-all-start.1) | async-done | bytes 65568 | tf_op jit(solution)/shard_map/all_to_all | solution.py:490
  51.1 0.0 copy-done
  51.1 1.1 %shard_map.131 = (f32[1,1024]{1,0:T(1,128)}, f32[8,4,128]{2,1,0:T(4,128)S(1)}) custom-call(s32[1]{0:T(128)} %bitcast.place, bf16[4,8,8,128]{3,2,1,0:T(8,128)(2,1)S(1)} %bitcast.14, bf16[1024,1024]{1,0:T(8,128)(2,1)S(1)} %copy-done), custom_call_target="tpu_custom_call" | custom-call | tf_op jit(solution)/shard_map/pallas_call | solution.py:495
  52.2 8.0 %all_to_all.15 = f32[8,4,128]{2,1,0:T(4,128)S(1)} all-to-all(f32[8,4,128]{2,1,0:T(4,128)S(1)} %get-tuple-element.41), channel_id=1, replica_groups=mesh['doc'=4,'ctx'=8] {'ctx'}, dimensions={0} | all-to-all | bytes 32768 | tf_op jit(solution)/shard_map/all_to_all | solution.py:511
  60.2 0.6 reduce_sum.9
  (3 shorter events, 0.1 us)
Async XLA Ops:
  2.1 20.6 %collective-permute-start = (bf16[128,4096]{1,0:T(8,128)(2,1)}, bf16[128,4096]{1,0:T(8,128)(2,1)S(1)}, u32[]{:S(2)}, u32[]{:S(2)}) collective-permute-start(bf16[128,4096]{1,0:T(8,128)(2,1)} %bitcast.16), channel_id=1, source_target_pairs={{0,1},{1,0},{2,3},{3,2},{4,5},{5,4},{6,7},{7,6},{8,9},{9,8},{10,11... | collective-permute-start | bytes 3145736 | tf_op jit(solution)/shard_map/ppermute | solution.py:344
  2.6 20.0 %collective-permute-start.1 = (bf16[128,4096]{1,0:T(8,128)(2,1)}, bf16[128,4096]{1,0:T(8,128)(2,1)S(1)}, u32[]{:S(2)}, u32[]{:S(2)}) collective-permute-start(bf16[128,4096]{1,0:T(8,128)(2,1)} %bitcast.18), channel_id=1, source_target_pairs={{0,1},{1,0},{2,3},{3,2},{4,5},{5,4},{6,7},{7,6},{8,9},{9,8},{10,11... | collective-permute-start | bytes 3145736 | tf_op jit(solution)/shard_map/ppermute | solution.py:344
  2.7 12.6 %all-to-all-start = ((f32[8,20,128]{2,1,0:T(8,128)}), f32[8,20,128]{2,1,0:T(8,128)S(1)}, u32[]{:S(2)}, u32[]{:S(2)}) async-start(f32[8,20,128]{2,1,0:T(8,128)} %shard_map.122), calls=%async_computation | async-start | bytes 196608 | tf_op jit(solution)/shard_map/all_to_all | solution.py:367
  10.1 1.6 %collective-permute-start.2 = (bf16[128,512]{1,0:T(8,128)(2,1)S(1)}, bf16[128,512]{1,0:T(8,128)(2,1)S(1)}, u32[]{:S(2)}, u32[]{:S(2)}) collective-permute-start(bf16[128,512]{1,0:T(8,128)(2,1)S(1)} %get-tuple-element.25), channel_id=1, source_target_pairs={{0,1},{1,0},{2,3},{3,2},{4,5},{5,4},{6,7},{7,6},{8,9},{9,8},{10,11... | collective-permute-start | bytes 393224 | tf_op jit(solution)/shard_map/ppermute | solution.py:344
  15.6 10.9 %collective-permute-start.3 = (bf16[256,256]{1,0:T(8,128)(2,1)S(1)}, bf16[256,256]{1,0:T(8,128)(2,1)S(1)}, u32[]{:S(2)}, u32[]{:S(2)}) collective-permute-start(bf16[256,256]{1,0:T(8,128)(2,1)S(1)} %get-tuple-element.33), channel_id=1, source_target_pairs={{0,4},{1,5},{4,6},{5,7},{8,12},{9,13},{12,14},{13,15},{16,20},{17,... | collective-permute-start | bytes 393224 | tf_op jit(solution)/shard_map/ppermute | solution.py:344
  17.9 9.2 %collective-permute-start.4 = (bf16[256,256]{1,0:T(8,128)(2,1)S(1)}, bf16[256,256]{1,0:T(8,128)(2,1)S(1)}, u32[]{:S(2)}, u32[]{:S(2)}) collective-permute-start(bf16[256,256]{1,0:T(8,128)(2,1)S(1)} %get-tuple-element.34), channel_id=1, source_target_pairs={{0,4},{1,5},{4,6},{5,7},{8,12},{9,13},{12,14},{13,15},{16,20},{17,... | collective-permute-start | bytes 393224 | tf_op jit(solution)/shard_map/ppermute | solution.py:344
  21.1 7.4 %copy-start.1 = (bf16[1,128,8192]{2,1,0:T(8,128)(2,1)S(1)}, bf16[1,128,8192]{2,1,0:T(8,128)(2,1)}, u32[]{:S(2)}) copy-start(bf16[1,128,8192]{2,1,0:T(8,128)(2,1)} %param.18) | copy-start | bytes 6291460
  21.2 7.4 %copy-start.2 = (s32[8192]{0:T(1024)S(1)}, s32[8192]{0:T(1024)}, u32[]{:S(2)}) copy-start(s32[8192]{0:T(1024)} %param.19) | copy-start | bytes 98308
  21.2 9.3 %collective-permute-start.5 = (bf16[256,512]{1,0:T(8,128)(2,1)S(1)}, bf16[256,512]{1,0:T(8,128)(2,1)S(1)}, u32[]{:S(2)}, u32[]{:S(2)}) collective-permute-start(bf16[256,512]{1,0:T(8,128)(2,1)S(1)} %get-tuple-element.36.pair_in), channel_id=1, source_target_pairs={{0,2},{1,3},{2,6},{3,7},{8,10},{9,11},{10,14},{11,15},{16,18},{17,... | collective-permute-start | bytes 786440 | tf_op jit(solution)/shard_map/ppermute | solution.py:344
  26.5 4.0 %collective-permute-start.7 = (bf16[256,512]{1,0:T(8,128)(2,1)S(1)}, bf16[256,512]{1,0:T(8,128)(2,1)S(1)}, u32[]{:S(2)}, u32[]{:S(2)}) collective-permute-start(bf16[256,512]{1,0:T(8,128)(2,1)S(1)} %get-tuple-element.36.pair_in), channel_id=1, source_target_pairs={{2,4},{3,5},{10,12},{11,13},{18,20},{19,21},{26,28},{27,29}} | collective-permute-start | bytes 786440 | tf_op jit(solution)/shard_map/ppermute | solution.py:344
  27.2 3.3 %collective-permute-start.6 = (bf16[256,256]{1,0:T(8,128)(2,1)S(1)}, bf16[256,256]{1,0:T(8,128)(2,1)S(1)}, u32[]{:S(2)}, u32[]{:S(2)}) collective-permute-start(bf16[256,256]{1,0:T(8,128)(2,1)S(1)} %collective-permute-done.3.refs_0_), channel_id=1, source_target_pairs={{4,6},{5,7},{12,14},{13,15},{20,22},{21,23},{28,30},{29,31}} | collective-permute-start | bytes 393224 | tf_op jit(solution)/shard_map/ppermute | solution.py:344
  27.9 3.8 %collective-permute-start.9 = (bf16[256,256]{1,0:T(8,128)(2,1)S(1)}, bf16[256,256]{1,0:T(8,128)(2,1)S(1)}, u32[]{:S(2)}, u32[]{:S(2)}) collective-permute-start(bf16[256,256]{1,0:T(8,128)(2,1)S(1)} %collective-permute-done.4.refs_1_), channel_id=1, source_target_pairs={{4,6},{5,7},{12,14},{13,15},{20,22},{21,23},{28,30},{29,31}} | collective-permute-start | bytes 393224 | tf_op jit(solution)/shard_map/ppermute | solution.py:344
  30.4 1.3 %collective-permute-start.8 = (bf16[128,128]{1,0:T(8,128)(2,1)S(1)}, bf16[128,128]{1,0:T(8,128)(2,1)S(1)}, u32[]{:S(2)}, u32[]{:S(2)}) collective-permute-start(bf16[128,128]{1,0:T(8,128)(2,1)S(1)} %shard_map.129.hi_own), channel_id=1, source_target_pairs={{0,1},{1,0},{2,3},{3,2},{4,5},{5,4},{6,7},{7,6},{8,9},{9,8},{10,11... | collective-permute-start | bytes 98312 | tf_op jit(solution)/shard_map/ppermute | solution.py:344
  30.6 20.5 %copy-start = (bf16[1024,1024]{1,0:T(8,128)(2,1)S(1)}, bf16[1024,1024]{1,0:T(8,128)(2,1)}, u32[]{:S(2)}) copy-start(bf16[1024,1024]{1,0:T(8,128)(2,1)} %stored_ref.1) | copy-start | bytes 6291460
  32.5 18.6 %all-to-all-start.1 = ((bf16[32,8,128]{2,1,0:T(8,128)(2,1)}), bf16[32,8,128]{2,1,0:T(8,128)(2,1)S(1)}, u32[]{:S(2)}, u32[]{:S(2)}) async-start(bf16[32,8,128]{2,1,0:T(8,128)(2,1)} %bitcast.11), calls=%async_computation.1 | async-start | bytes 131072 | tf_op jit(solution)/shard_map/all_to_all | solution.py:490

commit v4 on v3

--- a/solution.py
+++ b/solution.py
@@ -106,6 +106,18 @@
             copies.append((lower.at[:, at], part.at[pl.ds(rows, rows), to]))
     for copy in fetch(copies, sems):
         copy.wait()
+
+
+def relay_kernel(place, own, received, out, sems, *, relaying):
+    passing = place[0] // 2 == relaying
+
+    @pl.when(passing)
+    def _():
+        fetch([(received, out)], sems)[0].wait()
+
+    @pl.when(jnp.logical_not(passing))
+    def _():
+        fetch([(own, out)], sems)[0].wait()
 
 
 def hash_kernel(rows_in, codes_in, out, rows, codes, sems):
@@ -253,15 +265,11 @@
     chip = place[0] // 2
 
     def block_of(group):
-        halves = [block for block in blocks if block.shape[1] == 2 * HD]
-        wholes = [block for block in blocks if block.shape[1] != 2 * HD]
-        found = [halves[picked.index(group)][...]] if halves else []
-        if wholes:
-            key, value = (
-                wholes[0][:, at * HD : (at + 1) * HD] for at in (group, kv_groups + group)
-            )
-            found.append(jnp.concatenate([key, value], axis=1))
-        return found[0] if len(found) == 1 else jnp.where(chip == max(steps), *found)
+        block = blocks[picked.index(group) % len(blocks)]
+        if block.shape[1] == 2 * HD:
+            return block[...]
+        key, value = (block[:, at * HD : (at + 1) * HD] for at in (group, kv_groups + group))
+        return jnp.concatenate([key, value], axis=1)
 
     step = jnp.int32(NO_STEP)
     for at_chip, known in steps.items():
@@ -448,21 +456,29 @@
     hashed_sib = swap(hashed)
 
     if four:
-        passed = after(received[0], total)
-        (own,) = after((pair,), total, received[0][0])
-        received.append([send(half, plan[2][:1]) for half in passed])
-        received[-1].append(send(own, plan[2][1:]))
+        relayed = []
+        passed = list(after(received[0][:1], total))
+        passed += after(received[0][1:], hashed)
+        for own, block in zip(halves, passed):
+            relayed.append(
+                pl.pallas_call(
+                    functools.partial(relay_kernel, relaying=2),
+                    out_shape=part_shape,
+                    in_specs=[SMEM, ANY, ANY],
+                    out_specs=VMEM,
+                    scratch_shapes=[pltpu.SemaphoreType.DMA((1,))],
+                    compiler_params=params(16),
+                )(place, own, block)
+            )
+        received.append([send(half, plan[2]) for half in relayed])
     for wave in range(len(received), len(plan)):
         received.append([send(received[-1][0], plan[wave])])
 
     scale = (seq_len * layer_input.shape[2] // K1) ** -0.5
     chunk = K1 * K2 // LANES // ctx_count
-    tiles = [
-        (wave, range(groups), blocks) for wave, blocks in enumerate(received) if len(blocks) < 3
-    ]
+    tiles = [(wave, range(groups), blocks) for wave, blocks in enumerate(received)]
     if four:
-        *halves, own = received[-1]
-        tiles += [(2, [group], [half, own]) for group, half in enumerate(halves)]
+        tiles[-1:] = [(2, [group], [half]) for group, half in enumerate(received[-1])]
     for wave, picked, blocks in tiles:
         last = blocks is tiles[-1][2]
         steps = {high: step for _, high, step in plan[wave]}

time: 61.4 us -> 60.9 us (level)
  starting transfers between devices: 27.7 us -> 26.8 us
    ppermute x10 -> x9, starting transfers between devices: 10.2 us -> 9.54 us  [permute(): lax.ppermute(array, 'ctx', [pair for pair in pairs if pair[1] < ctx_count])]
    ppermute x10 -> x9, waiting for transfers between devices: 1.42 us -> 1.43 us  [permute(): lax.ppermute(array, 'ctx', [pair for pair in pairs if pair[1] < ctx_count])]
  transfers between devices with their start and end apart: 12 -> 11, of which waited for: 4 -> 4; matrix products, arithmetic and copies ran while one was open for 0% -> 0% of each run, Pallas kernels for 12% -> 12%
where the time goes in v4:
time: 60.9 us; the launch traced here: 60.4 us
  starting transfers between devices  26.8 us (44%)
  waiting for transfers between devices  12.4 us (20%)
  Pallas kernels  11 us (18%)
  blocking collectives  8 us (13%)
  between operations  1.51 us (2%)
    all_to_all x1, starting transfers between devices, local(): lax.all_to_all(parts, ('doc', 'ctx'), split_axis=0, concat_axis=0, tiled=...  11 us
    ppermute x9, starting transfers between devices, permute(): lax.ppermute(array, 'ctx', [pair for pair in pairs if pair[1] < ctx_count])  9.54 us
    all_to_all x1, blocking collectives, local(): lax.all_to_all(partial, 'ctx', split_axis=0, concat_axis=0, tiled=True)  8 us
    all_to_all x1, waiting for transfers between devices, local(): lax.all_to_all(parts, ('doc', 'ctx'), split_axis=0, concat_axis=0, tiled=...  7.38 us
    all_to_all x1, starting transfers between devices, local(): lax.all_to_all(packed, 'ctx', split_axis=0, concat_axis=0, tiled=True)  6.3 us
    pallas_call x1, Pallas kernels, local(): pl.pallas_call(first_kernel, out_shape=(total_shape, stacked, stacked, ta...  3.84 us
    all_to_all x1, waiting for transfers between devices, local(): lax.all_to_all(packed, 'ctx', split_axis=0, concat_axis=0, tiled=True)  3.63 us
    pallas_call x1, Pallas kernels, local(): pl.pallas_call(hash_kernel, out_shape=shape((rows, K1), jnp.bfloat16), in...  1.8 us
  transfers between devices with their start and end apart: 11, of which 4 were waited for; matrix products, arithmetic and copies ran while one was open for 0% of the time, Pallas kernels for 12%

profile of v4, /device:TPU:0, one launch (start us, length us, event | category | flops | bytes accessed | tf_op | source)
XLA Modules:
  0.0 60.4 jit_solution(14861139417160587435)
XLA Ops:
  0.6 1.4 %shard_map.122 = f32[8,20,128]{2,1,0:T(8,128)} custom-call(f32[4,1024]{1,0:T(4,128)} %bitcast.22, f32[4,1024]{1,0:T(4,128)} %bitcast.23, s32[4,128]{1,0:T(4,128)} %bitcast.24), custom_call_target="tpu_custom_call" | custom-call | tf_op jit(solution)/shard_map/pallas_call | solution.py:362
  2.1 0.5 collective-permute-start
  2.6 0.1 collective-permute-start.1
  2.7 6.3 %all-to-all-start = ((f32[8,20,128]{2,1,0:T(8,128)}), f32[8,20,128]{2,1,0:T(8,128)S(1)}, u32[]{:S(2)}, u32[]{:S(2)}) async-start(f32[8,20,128]{2,1,0:T(8,128)} %shard_map.122), calls=%async_computation | async-start | bytes 196608 | tf_op jit(solution)/shard_map/all_to_all | solution.py:375
  9.0 1.2 %shard_map.123 = (bf16[256,512]{1,0:T(8,128)(2,1)S(1)}, bf16[128,512]{1,0:T(8,128)(2,1)S(1)}) custom-call(s32[1]{0:T(128)} %bitcast.1.place, bf16[128,512]{1,0:T(8,128)(2,1)} %bitcast.20, bf16[128,512]{1,0:T(8,128)(2,1)} %bitcast.21), custom_call_target="tpu_custom_call" | custom-call | tf_op jit(solution)/shard_map/pallas_call | solution.py:382
  10.1 0.6 collective-permute-start.2
  11.3 0.3 collective-permute-done.2.lower
  11.7 3.6 %all-to-all-done.stats = f32[8,20,128]{2,1,0:T(8,128)S(1)} async-done(((f32[8,20,128]{2,1,0:T(8,128)}), f32[8,20,128]{2,1,0:T(8,128)S(1)}, u32[]{:S(2)}, u32[]{:S(2)}) %all-to-all-start) | async-done | bytes 81952 | tf_op jit(solution)/shard_map/all_to_all | solution.py:375
  15.3 0.3 shard_map.124
  15.6 2.3 %collective-permute-start.4 = (bf16[256,256]{1,0:T(8,128)(2,1)S(1)}, bf16[256,256]{1,0:T(8,128)(2,1)S(1)}, u32[]{:S(2)}, u32[]{:S(2)}) collective-permute-start(bf16[256,256]{1,0:T(8,128)(2,1)S(1)} %get-tuple-element.33.own), channel_id=1, source_target_pairs={{0,4},{1,5},{4,6},{5,7},{8,12},{9,13},{12,14},{13,15},{16,20},{17,... | collective-permute-start | bytes 393224 | tf_op jit(solution)/shard_map/ppermute | solution.py:352
  17.9 3.2 %collective-permute-start.3 = (bf16[256,256]{1,0:T(8,128)(2,1)S(1)}, bf16[256,256]{1,0:T(8,128)(2,1)S(1)}, u32[]{:S(2)}, u32[]{:S(2)}) collective-permute-start(bf16[256,256]{1,0:T(8,128)(2,1)S(1)} %get-tuple-element.32.own), channel_id=1, source_target_pairs={{0,4},{1,5},{4,6},{5,7},{8,12},{9,13},{12,14},{13,15},{16,20},{17,... | collective-permute-start | bytes 393224 | tf_op jit(solution)/shard_map/ppermute | solution.py:352
  21.1 0.0 copy-start.1
  21.2 0.0 copy-start.2
  21.2 1.4 %collective-permute-start.5 = (bf16[256,512]{1,0:T(8,128)(2,1)S(1)}, bf16[256,512]{1,0:T(8,128)(2,1)S(1)}, u32[]{:S(2)}, u32[]{:S(2)}) collective-permute-start(bf16[256,512]{1,0:T(8,128)(2,1)S(1)} %get-tuple-element.27.pair_in), channel_id=1, source_target_pairs={{0,2},{1,3},{2,6},{3,7},{8,10},{9,11},{10,14},{11,15},{16,18},{17,... | collective-permute-start | bytes 786440 | tf_op jit(solution)/shard_map/ppermute | solution.py:352
  22.6 0.0 collective-permute-done.q_sib
  22.6 0.0 collective-permute-done.1.g_sib
  22.6 3.8 %shard_map.125 = (f32[256,128]{1,0:T(8,128)S(1)}, bf16[4096,256]{1,0:T(8,128)(2,1)S(1)}, bf16[4096,256]{1,0:T(8,128)(2,1)S(1)}, bf16[2048,128]{1,0:T(8,128)(2,1)S(1)}) custom-call(s32[1]{0:T(128)} %bitcast.1.place, s32[1]{0:T(128)S(6)} %copy.15.__.start, bf16[128,4096]{1,0:T(8,128)(2,1)} %bitcast.17, bf16[128,4096]{1,0:T(8,128)(2,1)S(1)} %collective-permute-done.q_sib, ...), custom_call_target="tpu_custom_call" | custom-call | tf_op jit(solution)/shard_map/pallas_call | solution.py:429
  26.5 0.0 copy-done.1
  26.5 0.0 copy-done.2
  26.5 1.8 %shard_map.130.hi_own = bf16[128,128]{1,0:T(8,128)(2,1)S(1)} custom-call(bf16[128,8192]{1,0:T(8,128)(2,1)S(1)} %bitcast.13, s32[1,8192]{1,0:T(1,128)S(1)} %bitcast.15), custom_call_target="tpu_custom_call" | custom-call | tf_op jit(solution)/shard_map/pallas_call | solution.py:444
  28.3 0.0 collective-permute-done.4.refs_1_.received
  28.3 0.0 collective-permute-done.3.refs_0_.received
  28.3 0.2 shard_map.128
  28.5 0.7 %collective-permute-start.6 = (bf16[256,256]{1,0:T(8,128)(2,1)S(1)}, bf16[256,256]{1,0:T(8,128)(2,1)S(1)}, u32[]{:S(2)}, u32[]{:S(2)}) collective-permute-start(bf16[256,256]{1,0:T(8,128)(2,1)S(1)} %shard_map.128), channel_id=1, source_target_pairs={{2,4},{3,5},{4,6},{5,7},{10,12},{11,13},{12,14},{13,15},{18,20},{1... | collective-permute-start | bytes 393224 | tf_op jit(solution)/shard_map/ppermute | solution.py:352
  29.2 0.2 shard_map.131
  29.4 0.7 %collective-permute-start.8 = (bf16[256,256]{1,0:T(8,128)(2,1)S(1)}, bf16[256,256]{1,0:T(8,128)(2,1)S(1)}, u32[]{:S(2)}, u32[]{:S(2)}) collective-permute-start(bf16[256,256]{1,0:T(8,128)(2,1)S(1)} %shard_map.131), channel_id=1, source_target_pairs={{2,4},{3,5},{4,6},{5,7},{10,12},{11,13},{12,14},{13,15},{18,20},{1... | collective-permute-start | bytes 393224 | tf_op jit(solution)/shard_map/ppermute | solution.py:352
  30.1 0.1 collective-permute-start.7
  30.2 0.0 collective-permute-done.5.refs_0_
  30.2 0.0 collective-permute-done.6.refs_0_
  30.3 0.0 copy-start
  30.3 1.1 %collective-permute-done.7.hi_sib = bf16[128,128]{1,0:T(8,128)(2,1)S(1)} collective-permute-done((bf16[128,128]{1,0:T(8,128)(2,1)S(1)}, bf16[128,128]{1,0:T(8,128)(2,1)S(1)}, u32[]{:S(2)}, u32[]{:S(2)}) %collective-permute-start.7) | collective-permute-done | bytes 32800 | tf_op jit(solution)/shard_map/ppermute | solution.py:352
  31.4 0.0 collective-permute-done.8.refs_0_
  31.4 0.9 %shard_map.132 = bf16[4,8,8,128]{3,2,1,0:T(8,128)(2,1)} custom-call(s32[1]{0:T(128)} %bitcast.1.place, s32[1]{0:T(128)S(6)} %copy.15.__.start, bf16[4096,256]{1,0:T(8,128)(2,1)S(1)} %get-tuple-element.28.q_all, bf16[4096,256]{1,0:T(8,128)(2,1)S(1)} %get-tuple-element.29.g_all, bf16[2048,128]{1,0:T(8,128)(2,1)S(1)} %get-tuple-element.30.tables, ...), custom_call_target="tpu_custom_call" | custom-call | tf_op jit(solution)/shard_map/pallas_call | solution.py:496
  32.2 11.0 %all-to-all-start.1 = ((bf16[32,8,128]{2,1,0:T(8,128)(2,1)}), bf16[32,8,128]{2,1,0:T(8,128)(2,1)S(1)}, u32[]{:S(2)}, u32[]{:S(2)}) async-start(bf16[32,8,128]{2,1,0:T(8,128)(2,1)} %bitcast.11), calls=%async_computation.1 | async-start | bytes 131072 | tf_op jit(solution)/shard_map/all_to_all | solution.py:506
  43.2 7.4 %all-to-all-done.1 = bf16[32,8,128]{2,1,0:T(8,128)(2,1)S(1)} async-done(((bf16[32,8,128]{2,1,0:T(8,128)(2,1)}), bf16[32,8,128]{2,1,0:T(8,128)(2,1)S(1)}, u32[]{:S(2)}, u32[]{:S(2)}) %all-to-all-start.1) | async-done | bytes 65568 | tf_op jit(solution)/shard_map/all_to_all | solution.py:506
  50.6 0.0 copy-done
  50.6 1.1 %shard_map.133 = (f32[1,1024]{1,0:T(1,128)}, f32[8,4,128]{2,1,0:T(4,128)S(1)}) custom-call(s32[1]{0:T(128)} %bitcast.place, bf16[4,8,8,128]{3,2,1,0:T(8,128)(2,1)S(1)} %bitcast.14, bf16[1024,1024]{1,0:T(8,128)(2,1)S(1)} %copy-done), custom_call_target="tpu_custom_call" | custom-call | tf_op jit(solution)/shard_map/pallas_call | solution.py:511
  51.8 8.0 %all_to_all.15 = f32[8,4,128]{2,1,0:T(4,128)S(1)} all-to-all(f32[8,4,128]{2,1,0:T(4,128)S(1)} %get-tuple-element.39), channel_id=1, replica_groups=mesh['doc'=4,'ctx'=8] {'ctx'}, dimensions={0} | all-to-all | bytes 32768 | tf_op jit(solution)/shard_map/all_to_all | solution.py:527
  59.8 0.6 reduce_sum.9
  (3 shorter events, 0.1 us)
Async XLA Ops:
  2.1 20.6 %collective-permute-start = (bf16[128,4096]{1,0:T(8,128)(2,1)}, bf16[128,4096]{1,0:T(8,128)(2,1)S(1)}, u32[]{:S(2)}, u32[]{:S(2)}) collective-permute-start(bf16[128,4096]{1,0:T(8,128)(2,1)} %bitcast.16), channel_id=1, source_target_pairs={{0,1},{1,0},{2,3},{3,2},{4,5},{5,4},{6,7},{7,6},{8,9},{9,8},{10,11... | collective-permute-start | bytes 3145736 | tf_op jit(solution)/shard_map/ppermute | solution.py:352
  2.6 20.0 %collective-permute-start.1 = (bf16[128,4096]{1,0:T(8,128)(2,1)}, bf16[128,4096]{1,0:T(8,128)(2,1)S(1)}, u32[]{:S(2)}, u32[]{:S(2)}) collective-permute-start(bf16[128,4096]{1,0:T(8,128)(2,1)} %bitcast.18), channel_id=1, source_target_pairs={{0,1},{1,0},{2,3},{3,2},{4,5},{5,4},{6,7},{7,6},{8,9},{9,8},{10,11... | collective-permute-start | bytes 3145736 | tf_op jit(solution)/shard_map/ppermute | solution.py:352
  2.7 12.6 %all-to-all-start = ((f32[8,20,128]{2,1,0:T(8,128)}), f32[8,20,128]{2,1,0:T(8,128)S(1)}, u32[]{:S(2)}, u32[]{:S(2)}) async-start(f32[8,20,128]{2,1,0:T(8,128)} %shard_map.122), calls=%async_computation | async-start | bytes 196608 | tf_op jit(solution)/shard_map/all_to_all | solution.py:375
  10.1 1.6 %collective-permute-start.2 = (bf16[128,512]{1,0:T(8,128)(2,1)S(1)}, bf16[128,512]{1,0:T(8,128)(2,1)S(1)}, u32[]{:S(2)}, u32[]{:S(2)}) collective-permute-start(bf16[128,512]{1,0:T(8,128)(2,1)S(1)} %get-tuple-element.24), channel_id=1, source_target_pairs={{0,1},{1,0},{2,3},{3,2},{4,5},{5,4},{6,7},{7,6},{8,9},{9,8},{10,11... | collective-permute-start | bytes 393224 | tf_op jit(solution)/shard_map/ppermute | solution.py:352
  15.6 12.7 %collective-permute-start.4 = (bf16[256,256]{1,0:T(8,128)(2,1)S(1)}, bf16[256,256]{1,0:T(8,128)(2,1)S(1)}, u32[]{:S(2)}, u32[]{:S(2)}) collective-permute-start(bf16[256,256]{1,0:T(8,128)(2,1)S(1)} %get-tuple-element.33.own), channel_id=1, source_target_pairs={{0,4},{1,5},{4,6},{5,7},{8,12},{9,13},{12,14},{13,15},{16,20},{17,... | collective-permute-start | bytes 393224 | tf_op jit(solution)/shard_map/ppermute | solution.py:352
  17.9 10.4 %collective-permute-start.3 = (bf16[256,256]{1,0:T(8,128)(2,1)S(1)}, bf16[256,256]{1,0:T(8,128)(2,1)S(1)}, u32[]{:S(2)}, u32[]{:S(2)}) collective-permute-start(bf16[256,256]{1,0:T(8,128)(2,1)S(1)} %get-tuple-element.32.own), channel_id=1, source_target_pairs={{0,4},{1,5},{4,6},{5,7},{8,12},{9,13},{12,14},{13,15},{16,20},{17,... | collective-permute-start | bytes 393224 | tf_op jit(solution)/shard_map/ppermute | solution.py:352
  21.1 5.3 %copy-start.1 = (bf16[1,128,8192]{2,1,0:T(8,128)(2,1)S(1)}, bf16[1,128,8192]{2,1,0:T(8,128)(2,1)}, u32[]{:S(2)}) copy-start(bf16[1,128,8192]{2,1,0:T(8,128)(2,1)} %param.18) | copy-start | bytes 6291460
  21.2 5.3 %copy-start.2 = (s32[8192]{0:T(1024)S(1)}, s32[8192]{0:T(1024)}, u32[]{:S(2)}) copy-start(s32[8192]{0:T(1024)} %param.19) | copy-start | bytes 98308
  21.2 9.0 %collective-permute-start.5 = (bf16[256,512]{1,0:T(8,128)(2,1)S(1)}, bf16[256,512]{1,0:T(8,128)(2,1)S(1)}, u32[]{:S(2)}, u32[]{:S(2)}) collective-permute-start(bf16[256,512]{1,0:T(8,128)(2,1)S(1)} %get-tuple-element.27.pair_in), channel_id=1, source_target_pairs={{0,2},{1,3},{2,6},{3,7},{8,10},{9,11},{10,14},{11,15},{16,18},{17,... | collective-permute-start | bytes 786440 | tf_op jit(solution)/shard_map/ppermute | solution.py:352
  28.5 1.7 %collective-permute-start.6 = (bf16[256,256]{1,0:T(8,128)(2,1)S(1)}, bf16[256,256]{1,0:T(8,128)(2,1)S(1)}, u32[]{:S(2)}, u32[]{:S(2)}) collective-permute-start(bf16[256,256]{1,0:T(8,128)(2,1)S(1)} %shard_map.128), channel_id=1, source_target_pairs={{2,4},{3,5},{4,6},{5,7},{10,12},{11,13},{12,14},{13,15},{18,20},{1... | collective-permute-start | bytes 393224 | tf_op jit(solution)/shard_map/ppermute | solution.py:352
  29.4 2.0 %collective-permute-start.8 = (bf16[256,256]{1,0:T(8,128)(2,1)S(1)}, bf16[256,256]{1,0:T(8,128)(2,1)S(1)}, u32[]{:S(2)}, u32[]{:S(2)}) collective-permute-start(bf16[256,256]{1,0:T(8,128)(2,1)S(1)} %shard_map.131), channel_id=1, source_target_pairs={{2,4},{3,5},{4,6},{5,7},{10,12},{11,13},{12,14},{13,15},{18,20},{1... | collective-permute-start | bytes 393224 | tf_op jit(solution)/shard_map/ppermute | solution.py:352
  30.1 1.3 %collective-permute-start.7 = (bf16[128,128]{1,0:T(8,128)(2,1)S(1)}, bf16[128,128]{1,0:T(8,128)(2,1)S(1)}, u32[]{:S(2)}, u32[]{:S(2)}) collective-permute-start(bf16[128,128]{1,0:T(8,128)(2,1)S(1)} %shard_map.130.hi_own), channel_id=1, source_target_pairs={{0,1},{1,0},{2,3},{3,2},{4,5},{5,4},{6,7},{7,6},{8,9},{9,8},{10,11... | collective-permute-start | bytes 98312 | tf_op jit(solution)/shard_map/ppermute | solution.py:352
  30.3 20.3 %copy-start = (bf16[1024,1024]{1,0:T(8,128)(2,1)S(1)}, bf16[1024,1024]{1,0:T(8,128)(2,1)}, u32[]{:S(2)}) copy-start(bf16[1024,1024]{1,0:T(8,128)(2,1)} %stored_ref.1) | copy-start | bytes 6291460
  32.2 18.4 %all-to-all-start.1 = ((bf16[32,8,128]{2,1,0:T(8,128)(2,1)}), bf16[32,8,128]{2,1,0:T(8,128)(2,1)S(1)}, u32[]{:S(2)}, u32[]{:S(2)}) async-start(bf16[32,8,128]{2,1,0:T(8,128)(2,1)} %bitcast.11), calls=%async_computation.1 | async-start | bytes 131072 | tf_op jit(solution)/shard_map/all_to_all | solution.py:506

commit v5 on v4

--- a/solution.py
+++ b/solution.py
@@ -94,30 +94,32 @@
         copy.wait()
 
 
-def join_kernel(_, lower, __, pair, *refs):
+def join_kernel(_, lower, __, pair, sems):
+    rows = lower.shape[0]
+    for copy in fetch([(lower, pair.at[pl.ds(rows, rows), :])], sems):
+        copy.wait()
+
+
+def relay_kernel(place, own, received, *refs, relaying):
     parts, sems = refs[:-1], refs[-1]
-    rows = lower.shape[0]
-    copies = [(lower, pair.at[pl.ds(rows, rows), :])]
-    for group, part in enumerate(parts):
-        for half in range(2):
-            at = pl.ds((half * len(parts) + group) * HD, HD)
-            to = pl.ds(half * HD, HD)
-            copies.append((pair.at[pl.ds(0, rows), at], part.at[pl.ds(0, rows), to]))
-            copies.append((lower.at[:, at], part.at[pl.ds(rows, rows), to]))
-    for copy in fetch(copies, sems):
-        copy.wait()
-
-
-def relay_kernel(place, own, received, out, sems, *, relaying):
     passing = place[0] // 2 == relaying
+
+    def cut(block):
+        copies = []
+        for group, part in enumerate(parts):
+            for half in range(2):
+                at = pl.ds((half * len(parts) + group) * HD, HD)
+                copies.append((block.at[:, at], part.at[:, pl.ds(half * HD, HD)]))
+        for copy in fetch(copies, sems):
+            copy.wait()
 
     @pl.when(passing)
     def _():
-        fetch([(received, out)], sems)[0].wait()
+        cut(received)
 
     @pl.when(jnp.logical_not(passing))
     def _():
-        fetch([(own, out)], sems)[0].wait()
+        cut(own)
 
 
 def hash_kernel(rows_in, codes_in, out, rows, codes, sems):
@@ -392,13 +394,13 @@
 
     groups = kv_width // (2 * HD)
     part_shape = shape((2 * rows, 2 * HD), jnp.bfloat16)
-    pair, *halves = pl.pallas_call(
+    pair = pl.pallas_call(
         join_kernel,
-        out_shape=(pair_shape,) + (part_shape,) * groups,
+        out_shape=pair_shape,
         in_specs=[ANY, ANY, SMEM],
-        out_specs=(ANY,) + (VMEM,) * groups,
+        out_specs=ANY,
         input_output_aliases={0: 0},
-        scratch_shapes=[pltpu.SemaphoreType.DMA((1 + 4 * groups,))],
+        scratch_shapes=[pltpu.SemaphoreType.DMA((1,))],
         compiler_params=params(16),
     )(*after((pair, from_sib), stats), doc_start)
 
@@ -419,9 +421,7 @@
         route = {low: high for low, high, _ in routes}
         return permute(block, lambda i: 2 * route.get(i // 2, chips) + i % 2)
 
-    received = [[send(half, plan[0]) for half in halves] if four else [send(pair, plan[0])]]
-    if four:
-        received.append([send(pair, plan[1])])
+    received = [[send(pair, plan[0])]]
 
     stacked = shape((core_heads * 2 * rows, 2 * HD), jnp.bfloat16)
     table_shape = shape((core_heads * HD, LANES), jnp.bfloat16)
@@ -456,21 +456,18 @@
     hashed_sib = swap(hashed)
 
     if four:
+        (own,) = after((pair,), total)
+        received.append([send(own, plan[1])])
         relayed = []
-        passed = list(after(received[0][:1], total))
-        passed += after(received[0][1:], hashed)
-        for own, block in zip(halves, passed):
-            relayed.append(
-                pl.pallas_call(
-                    functools.partial(relay_kernel, relaying=2),
-                    out_shape=part_shape,
-                    in_specs=[SMEM, ANY, ANY],
-                    out_specs=VMEM,
-                    scratch_shapes=[pltpu.SemaphoreType.DMA((1,))],
-                    compiler_params=params(16),
-                )(place, own, block)
-            )
-        received.append([send(half, plan[2]) for half in relayed])
+        halves = pl.pallas_call(
+            functools.partial(relay_kernel, relaying=2),
+            out_shape=(part_shape,) * groups,
+            in_specs=[SMEM, ANY, ANY],
+            out_specs=(VMEM,) * groups,
+            scratch_shapes=[pltpu.SemaphoreType.DMA((2 * groups,))],
+            compiler_params=params(16),
+        )(place, *after((pair, received[0][0]), total, hashed))
+        received.append([send(half, plan[2]) for half in halves])
     for wave in range(len(received), len(plan)):
         received.append([send(received[-1][0], plan[wave])])
 

time: 60.9 us -> 60.9 us (level)
  waiting for transfers between devices: 12.4 us -> 13.7 us
  starting transfers between devices: 26.8 us -> 26 us
    ppermute x9 -> x8, starting transfers between devices: 9.54 us -> 6.36 us  [permute(): lax.ppermute(array, 'ctx', [pair for pair in pairs if pair[1] < ctx_count])]
    all_to_all x1, starting transfers between devices: 11 us -> 13.3 us  [local(): lax.all_to_all(parts, ('doc', 'ctx'), split_axis=0, concat_axis=0, tiled=...]
    ppermute x9 -> x8, waiting for transfers between devices: 1.43 us -> 2.73 us  [permute(): lax.ppermute(array, 'ctx', [pair for pair in pairs if pair[1] < ctx_count])]
  transfers between devices with their start and end apart: 11 -> 10, of which waited for: 4 -> 4; matrix products, arithmetic and copies ran while one was open for 0% -> 0% of each run, Pallas kernels for 12% -> 12%
where the time goes in v5:
time: 60.9 us; the launch traced here: 60.4 us
  starting transfers between devices  26 us (43%)
  waiting for transfers between devices  13.7 us (22%)
  Pallas kernels  10.5 us (17%)
  blocking collectives  8 us (13%)
  between operations  1.5 us (2%)
    all_to_all x1, starting transfers between devices, local(): lax.all_to_all(parts, ('doc', 'ctx'), split_axis=0, concat_axis=0, tiled=...  13.3 us
    all_to_all x1, blocking collectives, local(): lax.all_to_all(partial, 'ctx', split_axis=0, concat_axis=0, tiled=True)  8 us
    all_to_all x1, waiting for transfers between devices, local(): lax.all_to_all(parts, ('doc', 'ctx'), split_axis=0, concat_axis=0, tiled=...  7.38 us
    ppermute x8, starting transfers between devices, permute(): lax.ppermute(array, 'ctx', [pair for pair in pairs if pair[1] < ctx_count])  6.36 us
    all_to_all x1, starting transfers between devices, local(): lax.all_to_all(packed, 'ctx', split_axis=0, concat_axis=0, tiled=True)  6.3 us
    pallas_call x1, Pallas kernels, local(): pl.pallas_call(first_kernel, out_shape=(total_shape, stacked, stacked, ta...  3.84 us
    all_to_all x1, waiting for transfers between devices, local(): lax.all_to_all(packed, 'ctx', split_axis=0, concat_axis=0, tiled=True)  3.63 us
    ppermute x8, waiting for transfers between devices, permute(): lax.ppermute(array, 'ctx', [pair for pair in pairs if pair[1] < ctx_count])  2.73 us
  transfers between devices with their start and end apart: 10, of which 4 were waited for; matrix products, arithmetic and copies ran while one was open for 0% of the time, Pallas kernels for 12%

profile of v5, /device:TPU:0, one launch (start us, length us, event | category | flops | bytes accessed | tf_op | source)
XLA Modules:
  0.0 60.4 jit_solution(6725519084509871664)
XLA Ops:
  0.6 1.4 %shard_map.122 = f32[8,20,128]{2,1,0:T(8,128)} custom-call(f32[4,1024]{1,0:T(4,128)} %bitcast.22, f32[4,1024]{1,0:T(4,128)} %bitcast.23, s32[4,128]{1,0:T(4,128)} %bitcast.24), custom_call_target="tpu_custom_call" | custom-call | tf_op jit(solution)/shard_map/pallas_call | solution.py:364
  2.1 0.5 collective-permute-start
  2.6 0.1 collective-permute-start.1
  2.7 6.3 %all-to-all-start = ((f32[8,20,128]{2,1,0:T(8,128)}), f32[8,20,128]{2,1,0:T(8,128)S(1)}, u32[]{:S(2)}, u32[]{:S(2)}) async-start(f32[8,20,128]{2,1,0:T(8,128)} %shard_map.122), calls=%async_computation | async-start | bytes 196608 | tf_op jit(solution)/shard_map/all_to_all | solution.py:377
  9.0 1.2 %shard_map.123 = (bf16[256,512]{1,0:T(8,128)(2,1)S(1)}, bf16[128,512]{1,0:T(8,128)(2,1)S(1)}) custom-call(s32[1]{0:T(128)} %bitcast.1.place, bf16[128,512]{1,0:T(8,128)(2,1)} %bitcast.20, bf16[128,512]{1,0:T(8,128)(2,1)} %bitcast.21), custom_call_target="tpu_custom_call" | custom-call | tf_op jit(solution)/shard_map/pallas_call | solution.py:384
  10.1 0.6 collective-permute-start.2
  11.3 0.3 collective-permute-done.2.lower
  11.7 3.6 %all-to-all-done.stats = f32[8,20,128]{2,1,0:T(8,128)S(1)} async-done(((f32[8,20,128]{2,1,0:T(8,128)}), f32[8,20,128]{2,1,0:T(8,128)S(1)}, u32[]{:S(2)}, u32[]{:S(2)}) %all-to-all-start) | async-done | bytes 81952 | tf_op jit(solution)/shard_map/all_to_all | solution.py:377
  15.3 0.1 shard_map.124.pair_in.own
  15.5 0.0 copy-start.1
  15.5 0.0 copy-start.2
  15.5 2.5 %collective-permute-start.3 = (bf16[256,512]{1,0:T(8,128)(2,1)S(1)}, bf16[256,512]{1,0:T(8,128)(2,1)S(1)}, u32[]{:S(2)}, u32[]{:S(2)}) collective-permute-start(bf16[256,512]{1,0:T(8,128)(2,1)S(1)} %shard_map.124.pair_in.own), channel_id=1, source_target_pairs={{0,4},{1,5},{4,6},{5,7},{8,12},{9,13},{12,14},{13,15},{16,20},{17,... | collective-permute-start | bytes 786440 | tf_op jit(solution)/shard_map/ppermute | solution.py:354
  18.0 0.0 collective-permute-done.q_sib
  18.0 0.0 collective-permute-done.1.g_sib
  18.0 3.8 %shard_map.125 = (f32[256,128]{1,0:T(8,128)S(1)}, bf16[4096,256]{1,0:T(8,128)(2,1)S(1)}, bf16[4096,256]{1,0:T(8,128)(2,1)S(1)}, bf16[2048,128]{1,0:T(8,128)(2,1)S(1)}) custom-call(s32[1]{0:T(128)} %bitcast.1.place, s32[1]{0:T(128)S(6)} %copy.15.__.start, bf16[128,4096]{1,0:T(8,128)(2,1)} %bitcast.17, bf16[128,4096]{1,0:T(8,128)(2,1)S(1)} %collective-permute-done.q_sib, ...), custom_call_target="tpu_custom_call" | custom-call | tf_op jit(solution)/shard_map/pallas_call | solution.py:429
  21.8 1.3 %collective-permute-start.4 = (bf16[256,512]{1,0:T(8,128)(2,1)S(1)}, bf16[256,512]{1,0:T(8,128)(2,1)S(1)}, u32[]{:S(2)}, u32[]{:S(2)}) collective-permute-start(bf16[256,512]{1,0:T(8,128)(2,1)S(1)} %shard_map.124.pair_in.own), channel_id=1, source_target_pairs={{0,2},{1,3},{2,6},{3,7},{8,10},{9,11},{10,14},{11,15},{16,18},{17,... | collective-permute-start | bytes 786440 | tf_op jit(solution)/shard_map/ppermute | solution.py:354
  23.2 0.0 copy-done.1
  23.2 0.0 copy-done.2
  23.2 1.8 %shard_map.128.hi_own = bf16[128,128]{1,0:T(8,128)(2,1)S(1)} custom-call(bf16[128,8192]{1,0:T(8,128)(2,1)S(1)} %bitcast.13, s32[1,8192]{1,0:T(1,128)S(1)} %bitcast.15), custom_call_target="tpu_custom_call" | custom-call | tf_op jit(solution)/shard_map/pallas_call | solution.py:444
  25.0 0.0 collective-permute-done.3.refs_0_.received
  25.0 0.1 shard_map.129
  25.1 0.7 %collective-permute-start.5 = (bf16[256,256]{1,0:T(8,128)(2,1)S(1)}, bf16[256,256]{1,0:T(8,128)(2,1)S(1)}, u32[]{:S(2)}, u32[]{:S(2)}) collective-permute-start(bf16[256,256]{1,0:T(8,128)(2,1)S(1)} %get-tuple-element.36), channel_id=1, source_target_pairs={{2,4},{3,5},{4,6},{5,7},{10,12},{11,13},{12,14},{13,15},{18,20},{1... | collective-permute-start | bytes 393224 | tf_op jit(solution)/shard_map/ppermute | solution.py:354
  25.8 0.7 %collective-permute-start.7 = (bf16[256,256]{1,0:T(8,128)(2,1)S(1)}, bf16[256,256]{1,0:T(8,128)(2,1)S(1)}, u32[]{:S(2)}, u32[]{:S(2)}) collective-permute-start(bf16[256,256]{1,0:T(8,128)(2,1)S(1)} %get-tuple-element.37), channel_id=1, source_target_pairs={{2,4},{3,5},{4,6},{5,7},{10,12},{11,13},{12,14},{13,15},{18,20},{1... | collective-permute-start | bytes 393224 | tf_op jit(solution)/shard_map/ppermute | solution.py:354
  26.5 0.1 collective-permute-start.6
  26.6 2.4 %collective-permute-done.4.refs_0_ = bf16[256,512]{1,0:T(8,128)(2,1)S(1)} collective-permute-done((bf16[256,512]{1,0:T(8,128)(2,1)S(1)}, bf16[256,512]{1,0:T(8,128)(2,1)S(1)}, u32[]{:S(2)}, u32[]{:S(2)}) %collective-permute-start.4) | collective-permute-done | bytes 262176 | tf_op jit(solution)/shard_map/ppermute | solution.py:354
  29.0 0.0 collective-permute-done.5.refs_0_
  29.0 0.0 copy-start
  29.0 0.0 collective-permute-done.6.hi_sib
  29.0 0.0 collective-permute-done.7.refs_0_
  29.0 0.9 %shard_map.131 = bf16[4,8,8,128]{3,2,1,0:T(8,128)(2,1)} custom-call(s32[1]{0:T(128)} %bitcast.1.place, s32[1]{0:T(128)S(6)} %copy.15.__.start, bf16[4096,256]{1,0:T(8,128)(2,1)S(1)} %get-tuple-element.27.q_all, bf16[4096,256]{1,0:T(8,128)(2,1)S(1)} %get-tuple-element.28.g_all, bf16[2048,128]{1,0:T(8,128)(2,1)S(1)} %get-tuple-element.29.tables, ...), custom_call_target="tpu_custom_call" | custom-call | tf_op jit(solution)/shard_map/pallas_call | solution.py:493
  29.9 13.3 %all-to-all-start.1 = ((bf16[32,8,128]{2,1,0:T(8,128)(2,1)}), bf16[32,8,128]{2,1,0:T(8,128)(2,1)S(1)}, u32[]{:S(2)}, u32[]{:S(2)}) async-start(bf16[32,8,128]{2,1,0:T(8,128)(2,1)} %bitcast.11), calls=%async_computation.1 | async-start | bytes 131072 | tf_op jit(solution)/shard_map/all_to_all | solution.py:503
  43.2 7.4 %all-to-all-done.1 = bf16[32,8,128]{2,1,0:T(8,128)(2,1)S(1)} async-done(((bf16[32,8,128]{2,1,0:T(8,128)(2,1)}), bf16[32,8,128]{2,1,0:T(8,128)(2,1)S(1)}, u32[]{:S(2)}, u32[]{:S(2)}) %all-to-all-start.1) | async-done | bytes 65568 | tf_op jit(solution)/shard_map/all_to_all | solution.py:503
  50.6 0.0 copy-done
  50.6 1.1 %shard_map.132 = (f32[1,1024]{1,0:T(1,128)}, f32[8,4,128]{2,1,0:T(4,128)S(1)}) custom-call(s32[1]{0:T(128)} %bitcast.place, bf16[4,8,8,128]{3,2,1,0:T(8,128)(2,1)S(1)} %bitcast.14, bf16[1024,1024]{1,0:T(8,128)(2,1)S(1)} %copy-done), custom_call_target="tpu_custom_call" | custom-call | tf_op jit(solution)/shard_map/pallas_call | solution.py:508
  51.8 8.0 %all_to_all.15 = f32[8,4,128]{2,1,0:T(4,128)S(1)} all-to-all(f32[8,4,128]{2,1,0:T(4,128)S(1)} %get-tuple-element.39), channel_id=1, replica_groups=mesh['doc'=4,'ctx'=8] {'ctx'}, dimensions={0} | all-to-all | bytes 32768 | tf_op jit(solution)/shard_map/all_to_all | solution.py:524
  59.8 0.6 reduce_sum.9
  (3 shorter events, 0.1 us)
Async XLA Ops:
  2.1 15.9 %collective-permute-start = (bf16[128,4096]{1,0:T(8,128)(2,1)}, bf16[128,4096]{1,0:T(8,128)(2,1)S(1)}, u32[]{:S(2)}, u32[]{:S(2)}) collective-permute-start(bf16[128,4096]{1,0:T(8,128)(2,1)} %bitcast.16), channel_id=1, source_target_pairs={{0,1},{1,0},{2,3},{3,2},{4,5},{5,4},{6,7},{7,6},{8,9},{9,8},{10,11... | collective-permute-start | bytes 3145736 | tf_op jit(solution)/shard_map/ppermute | solution.py:354
  2.6 15.4 %collective-permute-start.1 = (bf16[128,4096]{1,0:T(8,128)(2,1)}, bf16[128,4096]{1,0:T(8,128)(2,1)S(1)}, u32[]{:S(2)}, u32[]{:S(2)}) collective-permute-start(bf16[128,4096]{1,0:T(8,128)(2,1)} %bitcast.18), channel_id=1, source_target_pairs={{0,1},{1,0},{2,3},{3,2},{4,5},{5,4},{6,7},{7,6},{8,9},{9,8},{10,11... | collective-permute-start | bytes 3145736 | tf_op jit(solution)/shard_map/ppermute | solution.py:354
  2.7 12.6 %all-to-all-start = ((f32[8,20,128]{2,1,0:T(8,128)}), f32[8,20,128]{2,1,0:T(8,128)S(1)}, u32[]{:S(2)}, u32[]{:S(2)}) async-start(f32[8,20,128]{2,1,0:T(8,128)} %shard_map.122), calls=%async_computation | async-start | bytes 196608 | tf_op jit(solution)/shard_map/all_to_all | solution.py:377
  10.1 1.6 %collective-permute-start.2 = (bf16[128,512]{1,0:T(8,128)(2,1)S(1)}, bf16[128,512]{1,0:T(8,128)(2,1)S(1)}, u32[]{:S(2)}, u32[]{:S(2)}) collective-permute-start(bf16[128,512]{1,0:T(8,128)(2,1)S(1)} %get-tuple-element.24), channel_id=1, source_target_pairs={{0,1},{1,0},{2,3},{3,2},{4,5},{5,4},{6,7},{7,6},{8,9},{9,8},{10,11... | collective-permute-start | bytes 393224 | tf_op jit(solution)/shard_map/ppermute | solution.py:354
  15.5 7.7 %copy-start.1 = (bf16[1,128,8192]{2,1,0:T(8,128)(2,1)S(1)}, bf16[1,128,8192]{2,1,0:T(8,128)(2,1)}, u32[]{:S(2)}) copy-start(bf16[1,128,8192]{2,1,0:T(8,128)(2,1)} %param.18) | copy-start | bytes 6291460
  15.5 7.7 %copy-start.2 = (s32[8192]{0:T(1024)S(1)}, s32[8192]{0:T(1024)}, u32[]{:S(2)}) copy-start(s32[8192]{0:T(1024)} %param.19) | copy-start | bytes 98308
  15.5 9.5 %collective-permute-start.3 = (bf16[256,512]{1,0:T(8,128)(2,1)S(1)}, bf16[256,512]{1,0:T(8,128)(2,1)S(1)}, u32[]{:S(2)}, u32[]{:S(2)}) collective-permute-start(bf16[256,512]{1,0:T(8,128)(2,1)S(1)} %shard_map.124.pair_in.own), channel_id=1, source_target_pairs={{0,4},{1,5},{4,6},{5,7},{8,12},{9,13},{12,14},{13,15},{16,20},{17,... | collective-permute-start | bytes 786440 | tf_op jit(solution)/shard_map/ppermute | solution.py:354
  21.8 7.1 %collective-permute-start.4 = (bf16[256,512]{1,0:T(8,128)(2,1)S(1)}, bf16[256,512]{1,0:T(8,128)(2,1)S(1)}, u32[]{:S(2)}, u32[]{:S(2)}) collective-permute-start(bf16[256,512]{1,0:T(8,128)(2,1)S(1)} %shard_map.124.pair_in.own), channel_id=1, source_target_pairs={{0,2},{1,3},{2,6},{3,7},{8,10},{9,11},{10,14},{11,15},{16,18},{17,... | collective-permute-start | bytes 786440 | tf_op jit(solution)/shard_map/ppermute | solution.py:354
  25.1 3.9 %collective-permute-start.5 = (bf16[256,256]{1,0:T(8,128)(2,1)S(1)}, bf16[256,256]{1,0:T(8,128)(2,1)S(1)}, u32[]{:S(2)}, u32[]{:S(2)}) collective-permute-start(bf16[256,256]{1,0:T(8,128)(2,1)S(1)} %get-tuple-element.36), channel_id=1, source_target_pairs={{2,4},{3,5},{4,6},{5,7},{10,12},{11,13},{12,14},{13,15},{18,20},{1... | collective-permute-start | bytes 393224 | tf_op jit(solution)/shard_map/ppermute | solution.py:354
  25.8 3.2 %collective-permute-start.7 = (bf16[256,256]{1,0:T(8,128)(2,1)S(1)}, bf16[256,256]{1,0:T(8,128)(2,1)S(1)}, u32[]{:S(2)}, u32[]{:S(2)}) collective-permute-start(bf16[256,256]{1,0:T(8,128)(2,1)S(1)} %get-tuple-element.37), channel_id=1, source_target_pairs={{2,4},{3,5},{4,6},{5,7},{10,12},{11,13},{12,14},{13,15},{18,20},{1... | collective-permute-start | bytes 393224 | tf_op jit(solution)/shard_map/ppermute | solution.py:354
  26.5 2.6 %collective-permute-start.6 = (bf16[128,128]{1,0:T(8,128)(2,1)S(1)}, bf16[128,128]{1,0:T(8,128)(2,1)S(1)}, u32[]{:S(2)}, u32[]{:S(2)}) collective-permute-start(bf16[128,128]{1,0:T(8,128)(2,1)S(1)} %shard_map.128.hi_own), channel_id=1, source_target_pairs={{0,1},{1,0},{2,3},{3,2},{4,5},{5,4},{6,7},{7,6},{8,9},{9,8},{10,11... | collective-permute-start | bytes 98312 | tf_op jit(solution)/shard_map/ppermute | solution.py:354
  29.0 21.6 %copy-start = (bf16[1024,1024]{1,0:T(8,128)(2,1)S(1)}, bf16[1024,1024]{1,0:T(8,128)(2,1)}, u32[]{:S(2)}) copy-start(bf16[1024,1024]{1,0:T(8,128)(2,1)} %stored_ref.1) | copy-start | bytes 6291460
  29.9 20.7 %all-to-all-start.1 = ((bf16[32,8,128]{2,1,0:T(8,128)(2,1)}), bf16[32,8,128]{2,1,0:T(8,128)(2,1)S(1)}, u32[]{:S(2)}, u32[]{:S(2)}) async-start(bf16[32,8,128]{2,1,0:T(8,128)(2,1)} %bitcast.11), calls=%async_computation.1 | async-start | bytes 131072 | tf_op jit(solution)/shard_map/all_to_all | solution.py:503

commit v6 on v5

--- a/solution.py
+++ b/solution.py
@@ -402,7 +402,7 @@
         input_output_aliases={0: 0},
         scratch_shapes=[pltpu.SemaphoreType.DMA((1,))],
         compiler_params=params(16),
-    )(*after((pair, from_sib), stats), doc_start)
+    )(*after((pair, from_sib), packed), doc_start)
 
     four = chips == 4
     if four:
@@ -456,7 +456,7 @@
     hashed_sib = swap(hashed)
 
     if four:
-        (own,) = after((pair,), total)
+        (own,) = after((pair,), stats)
         received.append([send(own, plan[1])])
         relayed = []
         halves = pl.pallas_call(

time: 60.9 us -> 59.7 us (0.980)
  waiting for transfers between devices: 13.7 us -> 7.56 us
  starting transfers between devices: 26 us -> 29.9 us
  Pallas kernels: 10.5 us -> 11.5 us
    ppermute x8, starting transfers between devices: 6.36 us -> 10.7 us  [permute(): lax.ppermute(array, 'ctx', [pair for pair in pairs if pair[1] < ctx_count])]
    all_to_all x1, waiting for transfers between devices: 3.63 us -> 0.01 us  [local(): lax.all_to_all(packed, 'ctx', split_axis=0, concat_axis=0, tiled=True)]
    ppermute x8, waiting for transfers between devices: 2.73 us -> 0.17 us  [permute(): lax.ppermute(array, 'ctx', [pair for pair in pairs if pair[1] < ctx_count])]
    pallas_call x3, Pallas kernels: 0.05 us -> 1 us  [local(): pl.pallas_call(functools.partial(next_kernel, **given), out_shape=total_s...]
  transfers between devices with their start and end apart: 10 -> 10, of which waited for: 4 -> 2; matrix products, arithmetic and copies ran while one was open for 0% -> 0% of each run, Pallas kernels for 12% -> 14%
where the time goes in v6:
time: 59.7 us; the launch traced here: 59.1 us
  starting transfers between devices  29.9 us (50%)
  Pallas kernels  11.5 us (19%)
  blocking collectives  8 us (13%)
  waiting for transfers between devices  7.56 us (13%)
  between operations  1.48 us (2%)
    all_to_all x1, starting transfers between devices, local(): lax.all_to_all(parts, ('doc', 'ctx'), split_axis=0, concat_axis=0, tiled=...  13.2 us
    ppermute x8, starting transfers between devices, permute(): lax.ppermute(array, 'ctx', [pair for pair in pairs if pair[1] < ctx_count])  10.7 us
    all_to_all x1, blocking collectives, local(): lax.all_to_all(partial, 'ctx', split_axis=0, concat_axis=0, tiled=True)  8 us
    all_to_all x1, waiting for transfers between devices, local(): lax.all_to_all(parts, ('doc', 'ctx'), split_axis=0, concat_axis=0, tiled=...  7.38 us
    all_to_all x1, starting transfers between devices, local(): lax.all_to_all(packed, 'ctx', split_axis=0, concat_axis=0, tiled=True)  6.01 us
    pallas_call x1, Pallas kernels, local(): pl.pallas_call(first_kernel, out_shape=(total_shape, stacked, stacked, ta...  3.84 us
    pallas_call x1, Pallas kernels, local(): pl.pallas_call(hash_kernel, out_shape=shape((rows, K1), jnp.bfloat16), in...  1.8 us
    pallas_call x1, Pallas kernels, local(): pl.pallas_call(pack_kernel, out_shape=shape((ctx_count, 5 * local_heads,...  1.42 us
  transfers between devices with their start and end apart: 10, of which 2 were waited for; matrix products, arithmetic and copies ran while one was open for 0% of the time, Pallas kernels for 14%

profile of v6, /device:TPU:0, one launch (start us, length us, event | category | flops | bytes accessed | tf_op | source)
XLA Modules:
  0.0 59.1 jit_solution(18131416427202900843)
XLA Ops:
  0.6 1.4 %shard_map.122 = f32[8,20,128]{2,1,0:T(8,128)} custom-call(f32[4,1024]{1,0:T(4,128)} %bitcast.22, f32[4,1024]{1,0:T(4,128)} %bitcast.23, s32[4,128]{1,0:T(4,128)} %bitcast.24), custom_call_target="tpu_custom_call" | custom-call | tf_op jit(solution)/shard_map/pallas_call | solution.py:364
  2.1 0.5 collective-permute-start
  2.6 0.1 collective-permute-start.1
  2.7 1.2 %shard_map.123 = (bf16[256,512]{1,0:T(8,128)(2,1)S(1)}, bf16[128,512]{1,0:T(8,128)(2,1)S(1)}) custom-call(s32[1]{0:T(128)} %bitcast.1.place, bf16[128,512]{1,0:T(8,128)(2,1)} %bitcast.20, bf16[128,512]{1,0:T(8,128)(2,1)} %bitcast.21), custom_call_target="tpu_custom_call" | custom-call | tf_op jit(solution)/shard_map/pallas_call | solution.py:384
  3.8 0.5 collective-permute-start.2
  4.3 6.0 %all-to-all-start = ((f32[8,20,128]{2,1,0:T(8,128)}), f32[8,20,128]{2,1,0:T(8,128)S(1)}, u32[]{:S(2)}, u32[]{:S(2)}) async-start(f32[8,20,128]{2,1,0:T(8,128)} %shard_map.122), calls=%async_computation | async-start | bytes 196608 | tf_op jit(solution)/shard_map/all_to_all | solution.py:377
  11.0 0.0 collective-permute-done.2.lower
  11.0 0.2 shard_map.124.pair_in.own
  11.2 0.0 copy-start.1
  11.2 0.0 copy-start.2
  11.2 5.7 %collective-permute-start.3 = (bf16[256,512]{1,0:T(8,128)(2,1)S(1)}, bf16[256,512]{1,0:T(8,128)(2,1)}, u32[]{:S(2)}, u32[]{:S(2)}) collective-permute-start(bf16[256,512]{1,0:T(8,128)(2,1)S(1)} %shard_map.124.pair_in.own), channel_id=1, source_target_pairs={{0,4},{1,5},{4,6},{5,7},{8,12},{9,13},{12,14},{13,15},{16,20},{17,... | collective-permute-start | bytes 786440 | tf_op jit(solution)/shard_map/ppermute | solution.py:354
  16.9 0.0 all-to-all-done.stats
  16.9 2.5 %collective-permute-start.4 = (bf16[256,512]{1,0:T(8,128)(2,1)S(1)}, bf16[256,512]{1,0:T(8,128)(2,1)S(1)}, u32[]{:S(2)}, u32[]{:S(2)}) collective-permute-start(bf16[256,512]{1,0:T(8,128)(2,1)S(1)} %shard_map.124.pair_in.own), channel_id=1, source_target_pairs={{0,2},{1,3},{2,6},{3,7},{8,10},{9,11},{10,14},{11,15},{16,18},{17,... | collective-permute-start | bytes 786440 | tf_op jit(solution)/shard_map/ppermute | solution.py:354
  19.4 0.0 collective-permute-done.q_sib
  19.4 0.0 collective-permute-done.1.g_sib
  19.4 3.8 %shard_map.125 = (f32[256,128]{1,0:T(8,128)S(1)}, bf16[4096,256]{1,0:T(8,128)(2,1)S(1)}, bf16[4096,256]{1,0:T(8,128)(2,1)S(1)}, bf16[2048,128]{1,0:T(8,128)(2,1)S(1)}) custom-call(s32[1]{0:T(128)} %bitcast.1.place, s32[1]{0:T(128)S(6)} %copy.15.__.start, bf16[128,4096]{1,0:T(8,128)(2,1)} %bitcast.17, bf16[128,4096]{1,0:T(8,128)(2,1)S(1)} %collective-permute-done.q_sib, ...), custom_call_target="tpu_custom_call" | custom-call | tf_op jit(solution)/shard_map/pallas_call | solution.py:429
  23.3 0.0 copy-done.1
  23.3 0.0 copy-done.2
  23.3 1.8 %shard_map.128.hi_own = bf16[128,128]{1,0:T(8,128)(2,1)S(1)} custom-call(bf16[128,8192]{1,0:T(8,128)(2,1)S(1)} %bitcast.13, s32[1,8192]{1,0:T(1,128)S(1)} %bitcast.15), custom_call_target="tpu_custom_call" | custom-call | tf_op jit(solution)/shard_map/pallas_call | solution.py:444
  25.1 0.0 collective-permute-done.3.refs_0_.received
  25.1 0.1 shard_map.129
  25.2 0.7 %collective-permute-start.5 = (bf16[256,256]{1,0:T(8,128)(2,1)S(1)}, bf16[256,256]{1,0:T(8,128)(2,1)S(1)}, u32[]{:S(2)}, u32[]{:S(2)}) collective-permute-start(bf16[256,256]{1,0:T(8,128)(2,1)S(1)} %get-tuple-element.36), channel_id=1, source_target_pairs={{2,4},{3,5},{4,6},{5,7},{10,12},{11,13},{12,14},{13,15},{18,20},{1... | collective-permute-start | bytes 393224 | tf_op jit(solution)/shard_map/ppermute | solution.py:354
  25.9 0.7 %collective-permute-start.7 = (bf16[256,256]{1,0:T(8,128)(2,1)S(1)}, bf16[256,256]{1,0:T(8,128)(2,1)S(1)}, u32[]{:S(2)}, u32[]{:S(2)}) collective-permute-start(bf16[256,256]{1,0:T(8,128)(2,1)S(1)} %get-tuple-element.37), channel_id=1, source_target_pairs={{2,4},{3,5},{4,6},{5,7},{10,12},{11,13},{12,14},{13,15},{18,20},{1... | collective-permute-start | bytes 393224 | tf_op jit(solution)/shard_map/ppermute | solution.py:354
  26.6 0.1 collective-permute-start.6
  26.7 1.0 %shard_map.126.before = f32[256,128]{1,0:T(8,128)S(1)} custom-call(s32[1]{0:T(128)} %bitcast.1.place, s32[1]{0:T(128)S(6)} %copy.15.__.start, bf16[4096,256]{1,0:T(8,128)(2,1)S(1)} %get-tuple-element.27.q_all, bf16[4096,256]{1,0:T(8,128)(2,1)S(1)} %get-tuple-element.28.g_all, bf16[2048,128]{1,0:T(8,128)(2,1)S(1)} %get-tuple-element.29.tables, ...), custom_call_target="tpu_custom_call" | custom-call | tf_op jit(solution)/shard_map/pallas_call | solution.py:485
  27.6 0.1 collective-permute-done.4.refs_0_
  27.7 0.0 collective-permute-done.5.refs_0_
  27.7 0.0 copy-start
  27.7 0.1 collective-permute-done.6.hi_sib
  27.9 0.0 collective-permute-done.7.refs_0_
  27.9 0.9 %shard_map.131 = bf16[4,8,8,128]{3,2,1,0:T(8,128)(2,1)} custom-call(s32[1]{0:T(128)} %bitcast.1.place, s32[1]{0:T(128)S(6)} %copy.15.__.start, bf16[4096,256]{1,0:T(8,128)(2,1)S(1)} %get-tuple-element.27.q_all, bf16[4096,256]{1,0:T(8,128)(2,1)S(1)} %get-tuple-element.28.g_all, bf16[2048,128]{1,0:T(8,128)(2,1)S(1)} %get-tuple-element.29.tables, ...), custom_call_target="tpu_custom_call" | custom-call | tf_op jit(solution)/shard_map/pallas_call | solution.py:493
  28.7 13.2 %all-to-all-start.1 = ((bf16[32,8,128]{2,1,0:T(8,128)(2,1)}), bf16[32,8,128]{2,1,0:T(8,128)(2,1)S(1)}, u32[]{:S(2)}, u32[]{:S(2)}) async-start(bf16[32,8,128]{2,1,0:T(8,128)(2,1)} %bitcast.11), calls=%async_computation.1 | async-start | bytes 131072 | tf_op jit(solution)/shard_map/all_to_all | solution.py:503
  41.9 7.4 %all-to-all-done.1 = bf16[32,8,128]{2,1,0:T(8,128)(2,1)S(1)} async-done(((bf16[32,8,128]{2,1,0:T(8,128)(2,1)}), bf16[32,8,128]{2,1,0:T(8,128)(2,1)S(1)}, u32[]{:S(2)}, u32[]{:S(2)}) %all-to-all-start.1) | async-done | bytes 65568 | tf_op jit(solution)/shard_map/all_to_all | solution.py:503
  49.3 0.0 copy-done
  49.3 1.1 %shard_map.132 = (f32[1,1024]{1,0:T(1,128)}, f32[8,4,128]{2,1,0:T(4,128)S(1)}) custom-call(s32[1]{0:T(128)} %bitcast.place, bf16[4,8,8,128]{3,2,1,0:T(8,128)(2,1)S(1)} %bitcast.14, bf16[1024,1024]{1,0:T(8,128)(2,1)S(1)} %copy-done), custom_call_target="tpu_custom_call" | custom-call | tf_op jit(solution)/shard_map/pallas_call | solution.py:508
  50.5 8.0 %all_to_all.15 = f32[8,4,128]{2,1,0:T(4,128)S(1)} all-to-all(f32[8,4,128]{2,1,0:T(4,128)S(1)} %get-tuple-element.39), channel_id=1, replica_groups=mesh['doc'=4,'ctx'=8] {'ctx'}, dimensions={0} | all-to-all | bytes 32768 | tf_op jit(solution)/shard_map/all_to_all | solution.py:524
  58.5 0.6 %reduce_sum.9 = f32[4,128]{1,0:T(4,128)} reduce(f32[8,4,128]{2,1,0:T(4,128)S(1)} %all_to_all.15, f32[]{:T(128)} %constant.9.clone.1), dimensions={0}, to_apply=%region_0.0 | reduce | flops 3584 | bytes 18436 | tf_op jit(solution)/shard_map/reduce_sum | solution.py:525
  (2 shorter events, 0.0 us)
Async XLA Ops:
  2.1 17.3 %collective-permute-start = (bf16[128,4096]{1,0:T(8,128)(2,1)}, bf16[128,4096]{1,0:T(8,128)(2,1)S(1)}, u32[]{:S(2)}, u32[]{:S(2)}) collective-permute-start(bf16[128,4096]{1,0:T(8,128)(2,1)} %bitcast.16), channel_id=1, source_target_pairs={{0,1},{1,0},{2,3},{3,2},{4,5},{5,4},{6,7},{7,6},{8,9},{9,8},{10,11... | collective-permute-start | bytes 3145736 | tf_op jit(solution)/shard_map/ppermute | solution.py:354
  2.6 16.8 %collective-permute-start.1 = (bf16[128,4096]{1,0:T(8,128)(2,1)}, bf16[128,4096]{1,0:T(8,128)(2,1)}, u32[]{:S(2)}, u32[]{:S(2)}) collective-permute-start(bf16[128,4096]{1,0:T(8,128)(2,1)} %bitcast.18), channel_id=1, source_target_pairs={{0,1},{1,0},{2,3},{3,2},{4,5},{5,4},{6,7},{7,6},{8,9},{9,8},{10,11... | collective-permute-start | bytes 3145736 | tf_op jit(solution)/shard_map/ppermute | solution.py:354
  3.8 7.2 %collective-permute-start.2 = (bf16[128,512]{1,0:T(8,128)(2,1)S(1)}, bf16[128,512]{1,0:T(8,128)(2,1)S(1)}, u32[]{:S(2)}, u32[]{:S(2)}) collective-permute-start(bf16[128,512]{1,0:T(8,128)(2,1)S(1)} %get-tuple-element.24), channel_id=1, source_target_pairs={{0,1},{1,0},{2,3},{3,2},{4,5},{5,4},{6,7},{7,6},{8,9},{9,8},{10,11... | collective-permute-start | bytes 393224 | tf_op jit(solution)/shard_map/ppermute | solution.py:354
  4.3 12.6 %all-to-all-start = ((f32[8,20,128]{2,1,0:T(8,128)}), f32[8,20,128]{2,1,0:T(8,128)S(1)}, u32[]{:S(2)}, u32[]{:S(2)}) async-start(f32[8,20,128]{2,1,0:T(8,128)} %shard_map.122), calls=%async_computation | async-start | bytes 196608 | tf_op jit(solution)/shard_map/all_to_all | solution.py:377
  11.2 12.1 %copy-start.1 = (bf16[1,128,8192]{2,1,0:T(8,128)(2,1)S(1)}, bf16[1,128,8192]{2,1,0:T(8,128)(2,1)}, u32[]{:S(2)}) copy-start(bf16[1,128,8192]{2,1,0:T(8,128)(2,1)} %param.18) | copy-start | bytes 6291460
  11.2 12.1 %copy-start.2 = (s32[8192]{0:T(1024)S(1)}, s32[8192]{0:T(1024)}, u32[]{:S(2)}) copy-start(s32[8192]{0:T(1024)} %param.19) | copy-start | bytes 98308
  11.2 13.9 %collective-permute-start.3 = (bf16[256,512]{1,0:T(8,128)(2,1)S(1)}, bf16[256,512]{1,0:T(8,128)(2,1)}, u32[]{:S(2)}, u32[]{:S(2)}) collective-permute-start(bf16[256,512]{1,0:T(8,128)(2,1)S(1)} %shard_map.124.pair_in.own), channel_id=1, source_target_pairs={{0,4},{1,5},{4,6},{5,7},{8,12},{9,13},{12,14},{13,15},{16,20},{17,... | collective-permute-start | bytes 786440 | tf_op jit(solution)/shard_map/ppermute | solution.py:354
  16.9 10.8 %collective-permute-start.4 = (bf16[256,512]{1,0:T(8,128)(2,1)S(1)}, bf16[256,512]{1,0:T(8,128)(2,1)S(1)}, u32[]{:S(2)}, u32[]{:S(2)}) collective-permute-start(bf16[256,512]{1,0:T(8,128)(2,1)S(1)} %shard_map.124.pair_in.own), channel_id=1, source_target_pairs={{0,2},{1,3},{2,6},{3,7},{8,10},{9,11},{10,14},{11,15},{16,18},{17,... | collective-permute-start | bytes 786440 | tf_op jit(solution)/shard_map/ppermute | solution.py:354
  25.2 2.5 %collective-permute-start.5 = (bf16[256,256]{1,0:T(8,128)(2,1)S(1)}, bf16[256,256]{1,0:T(8,128)(2,1)S(1)}, u32[]{:S(2)}, u32[]{:S(2)}) collective-permute-start(bf16[256,256]{1,0:T(8,128)(2,1)S(1)} %get-tuple-element.36), channel_id=1, source_target_pairs={{2,4},{3,5},{4,6},{5,7},{10,12},{11,13},{12,14},{13,15},{18,20},{1... | collective-permute-start | bytes 393224 | tf_op jit(solution)/shard_map/ppermute | solution.py:354
  25.9 2.0 %collective-permute-start.7 = (bf16[256,256]{1,0:T(8,128)(2,1)S(1)}, bf16[256,256]{1,0:T(8,128)(2,1)S(1)}, u32[]{:S(2)}, u32[]{:S(2)}) collective-permute-start(bf16[256,256]{1,0:T(8,128)(2,1)S(1)} %get-tuple-element.37), channel_id=1, source_target_pairs={{2,4},{3,5},{4,6},{5,7},{10,12},{11,13},{12,14},{13,15},{18,20},{1... | collective-permute-start | bytes 393224 | tf_op jit(solution)/shard_map/ppermute | solution.py:354
  26.6 1.3 %collective-permute-start.6 = (bf16[128,128]{1,0:T(8,128)(2,1)S(1)}, bf16[128,128]{1,0:T(8,128)(2,1)S(1)}, u32[]{:S(2)}, u32[]{:S(2)}) collective-permute-start(bf16[128,128]{1,0:T(8,128)(2,1)S(1)} %shard_map.128.hi_own), channel_id=1, source_target_pairs={{0,1},{1,0},{2,3},{3,2},{4,5},{5,4},{6,7},{7,6},{8,9},{9,8},{10,11... | collective-permute-start | bytes 98312 | tf_op jit(solution)/shard_map/ppermute | solution.py:354
  27.7 21.6 %copy-start = (bf16[1024,1024]{1,0:T(8,128)(2,1)S(1)}, bf16[1024,1024]{1,0:T(8,128)(2,1)}, u32[]{:S(2)}) copy-start(bf16[1024,1024]{1,0:T(8,128)(2,1)} %stored_ref.1) | copy-start | bytes 6291460
  28.7 20.6 %all-to-all-start.1 = ((bf16[32,8,128]{2,1,0:T(8,128)(2,1)}), bf16[32,8,128]{2,1,0:T(8,128)(2,1)S(1)}, u32[]{:S(2)}, u32[]{:S(2)}) async-start(bf16[32,8,128]{2,1,0:T(8,128)(2,1)} %bitcast.11), calls=%async_computation.1 | async-start | bytes 131072 | tf_op jit(solution)/shard_map/all_to_all | solution.py:503

commit v7 on v6

--- a/solution.py
+++ b/solution.py
@@ -50,6 +50,12 @@
     for copy in copies:
         copy.start()
     return copies
+
+
+def first_step_kernel(place, logs_in, deltas_in, codes_in, key_in, value_in, packed, pair, other, logs, deltas, codes, key, value, mine, sems, more_sems):
+    copies = fetch(((key_in, key), (value_in, value)), more_sems)
+    pack_kernel(logs_in, deltas_in, codes_in, packed, logs, deltas, codes, sems)
+    prepare_kernel(place, copies, pair, other, key, value, mine, sems)
 
 
 def pack_kernel(logs_in, deltas_in, codes_in, packed, logs, deltas, codes, sems):
@@ -67,17 +73,8 @@
         packed[target, 4 * heads :, :] = code_rows
 
 
-def prepare_kernel(place, key_in, value_in, pair, other, key, value, mine, sems):
-    rows = key.shape[0] // 2
-    pieces = [pl.ds(low, rows) for low in (0, rows)]
-    for copy in fetch(
-        [
-            (source.at[piece, :], target.at[piece, :])
-            for piece in pieces
-            for source, target in ((key_in, key), (value_in, value))
-        ],
-        sems,
-    ):
+def prepare_kernel(place, copies, pair, other, key, value, mine, sems):
+    for copy in copies:
         copy.wait()
     core = place[0] % 2
     half = key.shape[1] // 2
@@ -361,35 +358,35 @@
     def after(arrays, *done):
         return lax.optimization_barrier((tuple(arrays), done))[0]
 
-    packed = pl.pallas_call(
-        pack_kernel,
-        out_shape=shape((ctx_count, 5 * local_heads, LANES), jnp.float32),
-        in_specs=[ANY] * 3,
-        out_specs=VMEM,
+    half_shape = shape((rows, kv_width), jnp.bfloat16)
+    pair_shape = shape((2 * rows, kv_width), jnp.bfloat16)
+    packed, pair, other = pl.pallas_call(
+        first_step_kernel,
+        out_shape=(
+            shape((ctx_count, 5 * local_heads, LANES), jnp.float32), pair_shape, half_shape,
+        ),
+        in_specs=[SMEM] + [ANY] * 5,
+        out_specs=(VMEM, ANY, VMEM),
         scratch_shapes=[
             pltpu.VMEM((local_heads, seq_len), jnp.float32),
             pltpu.VMEM((local_heads, seq_len), jnp.float32),
             pltpu.VMEM((local_heads, HD), jnp.int32),
-            pltpu.SemaphoreType.DMA((3,)),
-        ],
+        ]
+        + [pltpu.VMEM((rows, kv_width), jnp.bfloat16)] * 3
+        + [pltpu.SemaphoreType.DMA((3,)), pltpu.SemaphoreType.DMA((2,))],
         compiler_params=params(16),
-    )(*pin(log_sums[0], row_delta[0], hash_out.reshape(local_heads, HD)))
+    )(
+        place,
+        *pin(
+            log_sums[0], row_delta[0], hash_out.reshape(local_heads, HD),
+            key_heads[0], value_heads[0],
+        ),
+    )
     stats = lax.all_to_all(packed, "ctx", split_axis=0, concat_axis=0, tiled=True)
 
     q, g = queries[0], out_grad[0]
     q_sib, g_sib = (swap(array) for array in after((q, g), packed))
 
-    half_shape = shape((rows, kv_width), jnp.bfloat16)
-    pair_shape = shape((2 * rows, kv_width), jnp.bfloat16)
-    pair, other = pl.pallas_call(
-        prepare_kernel,
-        out_shape=(pair_shape, half_shape),
-        in_specs=[SMEM, ANY, ANY],
-        out_specs=(ANY, VMEM),
-        scratch_shapes=[pltpu.VMEM((rows, kv_width), jnp.bfloat16)] * 3
-        + [pltpu.SemaphoreType.DMA((4,))],
-        compiler_params=params(16),
-    )(place, *pin(key_heads[0], value_heads[0]))
     from_sib = swap(other)
 
     groups = kv_width // (2 * HD)

time: 59.7 us -> 58.8 us (0.985)
  Pallas kernels: 11.5 us -> 10.8 us
    pallas_call x2 -> x1, Pallas kernels: 2.57 us -> 1.88 us  [local(): pl.pallas_call(first_step_kernel, out_shape=(shape((ctx_count, 5 * local_...]
  transfers between devices with their start and end apart: 10 -> 10, of which waited for: 2 -> 2; matrix products, arithmetic and copies ran while one was open for 0% -> 0% of each run, Pallas kernels for 14% -> 12%
where the time goes in v7:
time: 58.8 us; the launch traced here: 58.3 us
  starting transfers between devices  29.9 us (51%)
  Pallas kernels  10.8 us (18%)
  blocking collectives  8 us (14%)
  waiting for transfers between devices  7.56 us (13%)
  between operations  1.48 us (3%)
  other arithmetic  0.59 us (1%)
    all_to_all x1, starting transfers between devices, local(): lax.all_to_all(parts, ('doc', 'ctx'), split_axis=0, concat_axis=0, tiled=...  13.2 us
    ppermute x8, starting transfers between devices, permute(): lax.ppermute(array, 'ctx', [pair for pair in pairs if pair[1] < ctx_count])  10.6 us
    all_to_all x1, blocking collectives, local(): lax.all_to_all(partial, 'ctx', split_axis=0, concat_axis=0, tiled=True)  8 us
    all_to_all x1, waiting for transfers between devices, local(): lax.all_to_all(parts, ('doc', 'ctx'), split_axis=0, concat_axis=0, tiled=...  7.38 us
    all_to_all x1, starting transfers between devices, local(): lax.all_to_all(packed, 'ctx', split_axis=0, concat_axis=0, tiled=True)  6.01 us
    pallas_call x1, Pallas kernels, local(): pl.pallas_call(first_kernel, out_shape=(total_shape, stacked, stacked, ta...  3.84 us
    pallas_call x1, Pallas kernels, local(): pl.pallas_call(first_step_kernel, out_shape=(shape((ctx_count, 5 * local_...  1.88 us
    pallas_call x1, Pallas kernels, local(): pl.pallas_call(hash_kernel, out_shape=shape((rows, K1), jnp.bfloat16), in...  1.8 us
  transfers between devices with their start and end apart: 10, of which 2 were waited for; matrix products, arithmetic and copies ran while one was open for 0% of the time, Pallas kernels for 12%

profile of v7, /device:TPU:0, one launch (start us, length us, event | category | flops | bytes accessed | tf_op | source)
XLA Modules:
  0.0 58.3 jit_solution(4849764848200252604)
XLA Ops:
  0.6 1.9 %shard_map.122 = (f32[8,20,128]{2,1,0:T(8,128)}, bf16[256,512]{1,0:T(8,128)(2,1)S(1)}, bf16[128,512]{1,0:T(8,128)(2,1)S(1)}) custom-call(s32[1]{0:T(128)} %bitcast.1.place, f32[4,1024]{1,0:T(4,128)} %bitcast.22, f32[4,1024]{1,0:T(4,128)} %bitcast.23, s32[4,128]{1,0:T(4,128)} %bitcast.24, bf16[128,512]{1,0:T(8,128)(2,1)} %bitcast.20, bf16[128,512]{1,0:T(8,128)(2,1)} %bitcast.21), custom_call_target="tpu_custom_call" | custom-call | tf_op jit(solution)/shard_map/pallas_call | solution.py:363
  2.5 0.5 collective-permute-start
  3.0 0.1 collective-permute-start.1
  3.1 0.4 collective-permute-start.2
  3.5 6.0 %all-to-all-start = ((f32[8,20,128]{2,1,0:T(8,128)}), f32[8,20,128]{2,1,0:T(8,128)S(1)}, u32[]{:S(2)}, u32[]{:S(2)}) async-start(f32[8,20,128]{2,1,0:T(8,128)} %get-tuple-element.22), calls=%async_computation | async-start | bytes 196608 | tf_op jit(solution)/shard_map/all_to_all | solution.py:385
  10.2 0.0 collective-permute-done.2.lower
  10.2 0.2 shard_map.123.pair_in.own
  10.4 0.0 copy-start.1
  10.4 0.0 copy-start.2
  10.4 5.7 %collective-permute-start.3 = (bf16[256,512]{1,0:T(8,128)(2,1)S(1)}, bf16[256,512]{1,0:T(8,128)(2,1)}, u32[]{:S(2)}, u32[]{:S(2)}) collective-permute-start(bf16[256,512]{1,0:T(8,128)(2,1)S(1)} %shard_map.123.pair_in.own), channel_id=1, source_target_pairs={{0,4},{1,5},{4,6},{5,7},{8,12},{9,13},{12,14},{13,15},{16,20},{17,... | collective-permute-start | bytes 786440 | tf_op jit(solution)/shard_map/ppermute | solution.py:351
  16.1 0.0 all-to-all-done.stats
  16.1 2.5 %collective-permute-start.4 = (bf16[256,512]{1,0:T(8,128)(2,1)S(1)}, bf16[256,512]{1,0:T(8,128)(2,1)S(1)}, u32[]{:S(2)}, u32[]{:S(2)}) collective-permute-start(bf16[256,512]{1,0:T(8,128)(2,1)S(1)} %shard_map.123.pair_in.own), channel_id=1, source_target_pairs={{0,2},{1,3},{2,6},{3,7},{8,10},{9,11},{10,14},{11,15},{16,18},{17,... | collective-permute-start | bytes 786440 | tf_op jit(solution)/shard_map/ppermute | solution.py:351
  18.6 0.0 collective-permute-done.q_sib
  18.6 0.0 collective-permute-done.1.g_sib
  18.7 3.8 %shard_map.124 = (f32[256,128]{1,0:T(8,128)S(1)}, bf16[4096,256]{1,0:T(8,128)(2,1)S(1)}, bf16[4096,256]{1,0:T(8,128)(2,1)S(1)}, bf16[2048,128]{1,0:T(8,128)(2,1)S(1)}) custom-call(s32[1]{0:T(128)} %bitcast.1.place, s32[1]{0:T(128)S(6)} %copy.15.__.start, bf16[128,4096]{1,0:T(8,128)(2,1)} %bitcast.17, bf16[128,4096]{1,0:T(8,128)(2,1)S(1)} %collective-permute-done.q_sib, ...), custom_call_target="tpu_custom_call" | custom-call | tf_op jit(solution)/shard_map/pallas_call | solution.py:426
  22.5 0.0 copy-done.1
  22.5 0.0 copy-done.2
  22.5 1.8 %shard_map.127.hi_own = bf16[128,128]{1,0:T(8,128)(2,1)S(1)} custom-call(bf16[128,8192]{1,0:T(8,128)(2,1)S(1)} %bitcast.13, s32[1,8192]{1,0:T(1,128)S(1)} %bitcast.15), custom_call_target="tpu_custom_call" | custom-call | tf_op jit(solution)/shard_map/pallas_call | solution.py:441
  24.3 0.0 collective-permute-done.3.refs_0_.received
  24.3 0.1 shard_map.128
  24.5 0.7 %collective-permute-start.5 = (bf16[256,256]{1,0:T(8,128)(2,1)S(1)}, bf16[256,256]{1,0:T(8,128)(2,1)S(1)}, u32[]{:S(2)}, u32[]{:S(2)}) collective-permute-start(bf16[256,256]{1,0:T(8,128)(2,1)S(1)} %get-tuple-element.38), channel_id=1, source_target_pairs={{2,4},{3,5},{4,6},{5,7},{10,12},{11,13},{12,14},{13,15},{18,20},{1... | collective-permute-start | bytes 393224 | tf_op jit(solution)/shard_map/ppermute | solution.py:351
  25.1 0.7 %collective-permute-start.7 = (bf16[256,256]{1,0:T(8,128)(2,1)S(1)}, bf16[256,256]{1,0:T(8,128)(2,1)S(1)}, u32[]{:S(2)}, u32[]{:S(2)}) collective-permute-start(bf16[256,256]{1,0:T(8,128)(2,1)S(1)} %get-tuple-element.39), channel_id=1, source_target_pairs={{2,4},{3,5},{4,6},{5,7},{10,12},{11,13},{12,14},{13,15},{18,20},{1... | collective-permute-start | bytes 393224 | tf_op jit(solution)/shard_map/ppermute | solution.py:351
  25.8 0.1 collective-permute-start.6
  25.9 1.0 %shard_map.125.before = f32[256,128]{1,0:T(8,128)S(1)} custom-call(s32[1]{0:T(128)} %bitcast.1.place, s32[1]{0:T(128)S(6)} %copy.15.__.start, bf16[4096,256]{1,0:T(8,128)(2,1)S(1)} %get-tuple-element.29.q_all, bf16[4096,256]{1,0:T(8,128)(2,1)S(1)} %get-tuple-element.30.g_all, bf16[2048,128]{1,0:T(8,128)(2,1)S(1)} %get-tuple-element.31.tables, ...), custom_call_target="tpu_custom_call" | custom-call | tf_op jit(solution)/shard_map/pallas_call | solution.py:482
  26.9 0.1 collective-permute-done.4.refs_0_
  26.9 0.0 collective-permute-done.5.refs_0_
  27.0 0.0 copy-start
  27.0 0.1 collective-permute-done.6.hi_sib
  27.1 0.0 collective-permute-done.7.refs_0_
  27.1 0.9 %shard_map.130 = bf16[4,8,8,128]{3,2,1,0:T(8,128)(2,1)} custom-call(s32[1]{0:T(128)} %bitcast.1.place, s32[1]{0:T(128)S(6)} %copy.15.__.start, bf16[4096,256]{1,0:T(8,128)(2,1)S(1)} %get-tuple-element.29.q_all, bf16[4096,256]{1,0:T(8,128)(2,1)S(1)} %get-tuple-element.30.g_all, bf16[2048,128]{1,0:T(8,128)(2,1)S(1)} %get-tuple-element.31.tables, ...), custom_call_target="tpu_custom_call" | custom-call | tf_op jit(solution)/shard_map/pallas_call | solution.py:490
  27.9 13.2 %all-to-all-start.1 = ((bf16[32,8,128]{2,1,0:T(8,128)(2,1)}), bf16[32,8,128]{2,1,0:T(8,128)(2,1)S(1)}, u32[]{:S(2)}, u32[]{:S(2)}) async-start(bf16[32,8,128]{2,1,0:T(8,128)(2,1)} %bitcast.11), calls=%async_computation.1 | async-start | bytes 131072 | tf_op jit(solution)/shard_map/all_to_all | solution.py:500
  41.2 7.4 %all-to-all-done.1 = bf16[32,8,128]{2,1,0:T(8,128)(2,1)S(1)} async-done(((bf16[32,8,128]{2,1,0:T(8,128)(2,1)}), bf16[32,8,128]{2,1,0:T(8,128)(2,1)S(1)}, u32[]{:S(2)}, u32[]{:S(2)}) %all-to-all-start.1) | async-done | bytes 65568 | tf_op jit(solution)/shard_map/all_to_all | solution.py:500
  48.6 0.0 copy-done
  48.6 1.1 %shard_map.131 = (f32[1,1024]{1,0:T(1,128)}, f32[8,4,128]{2,1,0:T(4,128)S(1)}) custom-call(s32[1]{0:T(128)} %bitcast.place, bf16[4,8,8,128]{3,2,1,0:T(8,128)(2,1)S(1)} %bitcast.14, bf16[1024,1024]{1,0:T(8,128)(2,1)S(1)} %copy-done), custom_call_target="tpu_custom_call" | custom-call | tf_op jit(solution)/shard_map/pallas_call | solution.py:505
  49.7 8.0 %all_to_all.15 = f32[8,4,128]{2,1,0:T(4,128)S(1)} all-to-all(f32[8,4,128]{2,1,0:T(4,128)S(1)} %get-tuple-element.41), channel_id=1, replica_groups=mesh['doc'=4,'ctx'=8] {'ctx'}, dimensions={0} | all-to-all | bytes 32768 | tf_op jit(solution)/shard_map/all_to_all | solution.py:521
  57.7 0.6 %reduce_sum.9 = f32[4,128]{1,0:T(4,128)} reduce(f32[8,4,128]{2,1,0:T(4,128)S(1)} %all_to_all.15, f32[]{:T(128)} %constant.9.clone.1), dimensions={0}, to_apply=%region_0.0 | reduce | flops 3584 | bytes 18436 | tf_op jit(solution)/shard_map/reduce_sum | solution.py:522
  (2 shorter events, 0.0 us)
Async XLA Ops:
  2.5 16.1 %collective-permute-start = (bf16[128,4096]{1,0:T(8,128)(2,1)}, bf16[128,4096]{1,0:T(8,128)(2,1)S(1)}, u32[]{:S(2)}, u32[]{:S(2)}) collective-permute-start(bf16[128,4096]{1,0:T(8,128)(2,1)} %bitcast.16), channel_id=1, source_target_pairs={{0,1},{1,0},{2,3},{3,2},{4,5},{5,4},{6,7},{7,6},{8,9},{9,8},{10,11... | collective-permute-start | bytes 3145736 | tf_op jit(solution)/shard_map/ppermute | solution.py:351
  3.0 15.6 %collective-permute-start.1 = (bf16[128,4096]{1,0:T(8,128)(2,1)}, bf16[128,4096]{1,0:T(8,128)(2,1)}, u32[]{:S(2)}, u32[]{:S(2)}) collective-permute-start(bf16[128,4096]{1,0:T(8,128)(2,1)} %bitcast.18), channel_id=1, source_target_pairs={{0,1},{1,0},{2,3},{3,2},{4,5},{5,4},{6,7},{7,6},{8,9},{9,8},{10,11... | collective-permute-start | bytes 3145736 | tf_op jit(solution)/shard_map/ppermute | solution.py:351
  3.1 7.1 %collective-permute-start.2 = (bf16[128,512]{1,0:T(8,128)(2,1)S(1)}, bf16[128,512]{1,0:T(8,128)(2,1)S(1)}, u32[]{:S(2)}, u32[]{:S(2)}) collective-permute-start(bf16[128,512]{1,0:T(8,128)(2,1)S(1)} %get-tuple-element.26), channel_id=1, source_target_pairs={{0,1},{1,0},{2,3},{3,2},{4,5},{5,4},{6,7},{7,6},{8,9},{9,8},{10,11... | collective-permute-start | bytes 393224 | tf_op jit(solution)/shard_map/ppermute | solution.py:351
  3.5 12.6 %all-to-all-start = ((f32[8,20,128]{2,1,0:T(8,128)}), f32[8,20,128]{2,1,0:T(8,128)S(1)}, u32[]{:S(2)}, u32[]{:S(2)}) async-start(f32[8,20,128]{2,1,0:T(8,128)} %get-tuple-element.22), calls=%async_computation | async-start | bytes 196608 | tf_op jit(solution)/shard_map/all_to_all | solution.py:385
  10.4 12.1 %copy-start.1 = (bf16[1,128,8192]{2,1,0:T(8,128)(2,1)S(1)}, bf16[1,128,8192]{2,1,0:T(8,128)(2,1)}, u32[]{:S(2)}) copy-start(bf16[1,128,8192]{2,1,0:T(8,128)(2,1)} %param.18) | copy-start | bytes 6291460
  10.4 12.1 %copy-start.2 = (s32[8192]{0:T(1024)S(1)}, s32[8192]{0:T(1024)}, u32[]{:S(2)}) copy-start(s32[8192]{0:T(1024)} %param.19) | copy-start | bytes 98308
  10.4 13.9 %collective-permute-start.3 = (bf16[256,512]{1,0:T(8,128)(2,1)S(1)}, bf16[256,512]{1,0:T(8,128)(2,1)}, u32[]{:S(2)}, u32[]{:S(2)}) collective-permute-start(bf16[256,512]{1,0:T(8,128)(2,1)S(1)} %shard_map.123.pair_in.own), channel_id=1, source_target_pairs={{0,4},{1,5},{4,6},{5,7},{8,12},{9,13},{12,14},{13,15},{16,20},{17,... | collective-permute-start | bytes 786440 | tf_op jit(solution)/shard_map/ppermute | solution.py:351
  16.1 10.8 %collective-permute-start.4 = (bf16[256,512]{1,0:T(8,128)(2,1)S(1)}, bf16[256,512]{1,0:T(8,128)(2,1)S(1)}, u32[]{:S(2)}, u32[]{:S(2)}) collective-permute-start(bf16[256,512]{1,0:T(8,128)(2,1)S(1)} %shard_map.123.pair_in.own), channel_id=1, source_target_pairs={{0,2},{1,3},{2,6},{3,7},{8,10},{9,11},{10,14},{11,15},{16,18},{17,... | collective-permute-start | bytes 786440 | tf_op jit(solution)/shard_map/ppermute | solution.py:351
  24.5 2.5 %collective-permute-start.5 = (bf16[256,256]{1,0:T(8,128)(2,1)S(1)}, bf16[256,256]{1,0:T(8,128)(2,1)S(1)}, u32[]{:S(2)}, u32[]{:S(2)}) collective-permute-start(bf16[256,256]{1,0:T(8,128)(2,1)S(1)} %get-tuple-element.38), channel_id=1, source_target_pairs={{2,4},{3,5},{4,6},{5,7},{10,12},{11,13},{12,14},{13,15},{18,20},{1... | collective-permute-start | bytes 393224 | tf_op jit(solution)/shard_map/ppermute | solution.py:351
  25.1 2.0 %collective-permute-start.7 = (bf16[256,256]{1,0:T(8,128)(2,1)S(1)}, bf16[256,256]{1,0:T(8,128)(2,1)S(1)}, u32[]{:S(2)}, u32[]{:S(2)}) collective-permute-start(bf16[256,256]{1,0:T(8,128)(2,1)S(1)} %get-tuple-element.39), channel_id=1, source_target_pairs={{2,4},{3,5},{4,6},{5,7},{10,12},{11,13},{12,14},{13,15},{18,20},{1... | collective-permute-start | bytes 393224 | tf_op jit(solution)/shard_map/ppermute | solution.py:351
  25.8 1.3 %collective-permute-start.6 = (bf16[128,128]{1,0:T(8,128)(2,1)S(1)}, bf16[128,128]{1,0:T(8,128)(2,1)S(1)}, u32[]{:S(2)}, u32[]{:S(2)}) collective-permute-start(bf16[128,128]{1,0:T(8,128)(2,1)S(1)} %shard_map.127.hi_own), channel_id=1, source_target_pairs={{0,1},{1,0},{2,3},{3,2},{4,5},{5,4},{6,7},{7,6},{8,9},{9,8},{10,11... | collective-permute-start | bytes 98312 | tf_op jit(solution)/shard_map/ppermute | solution.py:351
  27.0 21.6 %copy-start = (bf16[1024,1024]{1,0:T(8,128)(2,1)S(1)}, bf16[1024,1024]{1,0:T(8,128)(2,1)}, u32[]{:S(2)}) copy-start(bf16[1024,1024]{1,0:T(8,128)(2,1)} %stored_ref.1) | copy-start | bytes 6291460
  27.9 20.6 %all-to-all-start.1 = ((bf16[32,8,128]{2,1,0:T(8,128)(2,1)}), bf16[32,8,128]{2,1,0:T(8,128)(2,1)S(1)}, u32[]{:S(2)}, u32[]{:S(2)}) async-start(bf16[32,8,128]{2,1,0:T(8,128)(2,1)} %bitcast.11), calls=%async_computation.1 | async-start | bytes 131072 | tf_op jit(solution)/shard_map/all_to_all | solution.py:500
